TPU v7x, 32 devices: a whole 2x2x4 slice. The times are simulated.
32 devices in a mesh: level: 4 (over x, core), band: 8 (over z, y).
Axes of the slice: x: 2, y: 2, z: 4, core: 2. Of those that a mesh axis runs over, the one named last changes fastest.
Arguments:
- features: bfloat16 [16384, 128], P('band'), may hold values from -6 to 6
- block_perm: int32 [4, 8, 8], P('level', 'band'), may hold values from 0 to 7, each once within a row
- tile_rows: int32 [4, 288], P('level', 'band'), may hold values from 0 to 63, as said below
- tile_cols: int32 [4, 288], P('level', 'band'), may hold values from 0 to 63, as said below
- tile_vals: bfloat16 [4, 288, 256, 256], P('level', 'band'), may hold values from -0.1875 to 0.1875
Outputs:
- forward: bfloat16 [8, 2048, 128], P('band', 'level')
- backward: bfloat16 [8, 2048, 128], P('band', 'level')
Inputs may be any that keep to these rules, and one draw needn't show every extreme that they name: `block_perm`: each band device's 8 entries of a level are a permutation of 0 to 7. `tile_rows`: the 36 tiles stored at band index b of a level each have either block row in b's blocks [b * 8, (b + 1) * 8) and block column in the blocks of band indices b - 1, b, b + 1 or below 2, or block row below 2 and block column in b's blocks; positions may repeat. `tile_cols`: as for tile_rows, paired entry by entry.
All inputs are finite; a program needn't handle non-finite values.
Results may differ from a plain program's by a relative error of at most 0.001.
Values may be sent and summed in bfloat16 or wider, within the bound.
No kernel may reach another device: no remote copies, remote signals or barrier semaphores. Data moves between devices by JAX's collectives and lax.ppermute only.
A program may use at most 128 MiB of HBM per device.

v0:
```python
import jax
import jax.numpy as jnp
from jax import lax
from jax.sharding import PartitionSpec as P

HEADB = 2


def with_halo(block, sides, width):
    for axis, dim in sides:
        count = lax.axis_size(axis)
        forward = [(i, i + 1) for i in range(count - 1)]
        backward = [(target, source) for source, target in forward]
        low = lax.ppermute(
            lax.slice_in_dim(block, block.shape[dim] - width, None, axis=dim), axis, forward
        )
        high = lax.ppermute(lax.slice_in_dim(block, 0, width, axis=dim), axis, backward)
        block = jnp.concatenate([low, block, high], axis=dim)
    return block


def from_root(block, axis, owner):
    block = jnp.where(lax.axis_index(axis) == owner, block, jnp.zeros_like(block))
    return lax.psum(block, axis)


def passed_along(array, axis, by):
    devices = lax.axis_size(axis)
    pairs = [(i, i + by) for i in range(devices) if 0 <= i + by < devices]
    return lax.ppermute(array, axis, pairs)


def on_device(features, block_perm, tile_rows, tile_cols, tile_vals):
    rdev, width = features.shape
    blocks = block_perm.shape[2]
    tile = tile_vals.shape[2]
    count = tile_vals.shape[1]
    heads = HEADB
    window_len = 3 * blocks + heads
    band_id = lax.axis_index("band")
    perm_local = block_perm[0, 0]
    block_ids = jnp.arange(blocks, dtype=jnp.int32)
    perm_hot = perm_local[:, None] == block_ids[None, :]
    inverse = jnp.sum(jnp.where(perm_hot, block_ids[:, None], 0), axis=0)
    x_blocks = features.reshape(blocks, tile, width)
    level_x = jnp.take(x_blocks, perm_local, axis=0)
    rimmed = with_halo(level_x, (("band", 0),), blocks)
    head_x = from_root(level_x[:heads], "band", 0)
    window = jnp.concatenate([rimmed, head_x], axis=0).reshape(window_len, tile * width)
    rows = tile_rows[0]
    cols = tile_cols[0]
    low = (band_id - 1) * blocks
    near = (cols >= low) & (cols < low + 3 * blocks)
    col_slot = jnp.where(near, cols - low, 3 * blocks + cols)
    own = (rows >= band_id * blocks) & (rows < (band_id + 1) * blocks)
    row_slot = jnp.where(own, rows - low, 3 * blocks + rows)
    by_col = jnp.take(window, col_slot, axis=0).reshape(count, tile, width)
    by_row = jnp.take(window, row_slot, axis=0).reshape(count, tile, width)
    vals = tile_vals[0]
    prod_fwd = jnp.einsum("kij,kjf->kif", vals, by_col, preferred_element_type=jnp.float32)
    prod_bwd = jnp.einsum("kij,kif->kjf", vals, by_row, preferred_element_type=jnp.float32)
    fwd_slot = jnp.where(own, rows - band_id * blocks, blocks + rows)
    fwd_sums = jax.ops.segment_sum(prod_fwd, fwd_slot, num_segments=blocks + heads)
    fwd_local = fwd_sums[:blocks]
    fwd_head = fwd_sums[blocks:]
    bwd_window = jax.ops.segment_sum(prod_bwd, col_slot, num_segments=window_len)
    from_left = passed_along(bwd_window[2 * blocks : 3 * blocks], "band", 1)
    from_right = passed_along(bwd_window[0:blocks], "band", -1)
    bwd_local = bwd_window[blocks : 2 * blocks] + from_left + from_right
    head_fwd, head_bwd = lax.psum((fwd_head, bwd_window[3 * blocks :]), "band")
    is_root = (band_id == 0).astype(jnp.float32)
    pad_rows = jnp.zeros((blocks - heads, tile, width), jnp.float32)
    fwd_local = fwd_local + is_root * jnp.concatenate([head_fwd, pad_rows], axis=0)
    bwd_local = bwd_local + is_root * jnp.concatenate([head_bwd, pad_rows], axis=0)
    fwd_global = jnp.take(fwd_local, inverse, axis=0).reshape(rdev, width)
    bwd_global = jnp.take(bwd_local, inverse, axis=0).reshape(rdev, width)
    share = rdev // lax.axis_size("level")
    fwd_all, bwd_all = lax.psum((fwd_global, bwd_global), "level")
    start = lax.axis_index("level") * share
    fwd_mine = lax.dynamic_slice_in_dim(fwd_all, start, share, 0)
    bwd_mine = lax.dynamic_slice_in_dim(bwd_all, start, share, 0)
    forward = fwd_mine.reshape(1, share, width).astype(jnp.bfloat16)
    backward = bwd_mine.reshape(1, share, width).astype(jnp.bfloat16)
    return (forward, backward)


def solution(mesh):
    return jax.shard_map(
        on_device,
        mesh=mesh,
        in_specs=(
            P("band", None),
            P("level", "band", None),
            P("level", "band"),
            P("level", "band"),
            P("level", "band", None, None),
        ),
        out_specs=(P("band", "level", None), P("band", "level", None)),
        check_vma=False,
    )
```

profile of v0, /device:TPU:0, one launch (start us, length us, event | category | flops | bytes accessed | tf_op | source)
XLA Modules:
  0.0 301.9 jit_solution(3957798239568365826)
XLA Ops:
  7.2 0.0 copy-start
  7.2 0.0 all-reduce.8.cloned.1.call-start
  7.2 0.7 compare_and_fusion.3
  7.9 0.7 fusion.20
  8.6 0.0 copy-done
  8.6 0.6 gather_fusion
  9.3 0.1 broadcast_select_fusion.4
  9.4 1.3 collective-permute-start.1
  10.7 5.5 %collective-permute-start = (bf16[8,256,128]{2,1,0:T(8,128)(2,1)S(1)}, bf16[8,256,128]{2,1,0:T(8,128)(2,1)S(1)}, u32[]{:S(2)}, u32[]{:S(2)}) collective-permute-start(bf16[8,256,128]{2,1,0:T(8,128)(2,1)S(1)} %broadcast_select_fusion.4), channel_id=1, source_target_pairs={{0,1},{1,2},{2,3},{3,4},{4,5},{5,6},{6,7},{8,9},{9,10},{10,11},{11... | collective-permute-start | bytes 1572872 | tf_op jit(solution)/shard_map/ppermute | solution.py:14
  16.2 0.7 slice_select_fusion
  16.9 0.0 all-reduce.8.cloned.1.call-update
  16.9 0.0 all-reduce.10.cloned.1.call-start
  17.0 0.7 compare_and_fusion.2
  17.7 0.7 select_bitcast_fusion
  18.3 0.7 compare_and_fusion
  19.0 0.7 select_reduce_fusion
  19.7 72.9 %all-reduce.8.cloned.1.call-done = bf16[2,256,128]{2,1,0:T(8,128)(2,1)} async-done(((bf16[2,256,128]{2,1,0:T(8,128)(2,1)}), bf16[2,256,128]{2,1,0:T(8,128)(2,1)}) %all-reduce.8.cloned.1.call-update) | async-done | bytes 131088 | tf_op jit(solution)/shard_map/psum | solution.py:24
  92.6 0.0 collective-permute-done.1
  92.7 0.0 collective-permute-done
  92.7 1.1 pad_maximum_fusion
  93.8 0.2 pad.11
  94.0 1.4 copy.17
  95.4 3.6 %gather_fusion.3 = bf16[36,32768]{1,0:T(8,128)(2,1)} fusion(bf16[26,32768]{1,0:T(8,128)(2,1)S(1)} %bitcast.44, s32[1024]{0:T(1024)S(1)} %pad_clamp_fusion), kind=kCustom, calls=%fused_computation.2.clone | custom fusion | bytes 4718736 | tf_op jit(solution)/shard_map/jit(_take)/gather | solution.py:58
  99.0 2.0 broadcast_select_fusion
  101.1 2.1 copy.19
  103.2 3.6 %gather_fusion.1 = bf16[36,32768]{1,0:T(8,128)(2,1)} fusion(bf16[26,32768]{1,0:T(8,128)(2,1)S(1)} %bitcast.45, s32[1024]{0:T(1024)S(1)} %pad_clamp_fusion.2), kind=kCustom, calls=%fused_computation.clone | custom fusion | bytes 4718736 | tf_op jit(solution)/shard_map/jit(_take)/gather | solution.py:57
  106.8 2.0 broadcast_select_fusion.1
  108.9 0.0 copy-start.1
  108.9 0.6 copy.18
  109.5 1.1 copy-done.1
  110.6 5.5 %fusion.11 = f32[36,256,128]{1,2,0:T(8,128)} fusion(bf16[1,36,256,256]{3,2,1,0:T(8,128)(2,1)} %param.13, bf16[40,256,128]{2,1,0:T(8,128)(2,1)S(1)} %bitcast.49), kind=kOutput, calls=%fused_computation.16 | convolution fusion | flops 603979776 | bytes 11796480 | tf_op jit(solution)/shard_map/kij,kif->kjf/dot_general | solution.py:61
  116.1 6.0 %copy.14 = f32[36,256,128]{2,1,0:T(8,128)} copy(f32[36,256,128]{1,2,0:T(8,128)} %fusion.11) | data formatting | bytes 9437184 | tf_op jit(solution)/shard_map/kij,kif->kjf/dot_general | solution.py:61
  122.2 2.1 broadcast_in_dim.60
  124.3 14.1 %scatter_fusion.1 = f32[26,256,128]{2,1,0:T(8,128)} fusion(f32[26,256,128]{2,1,0:T(8,128)} %broadcast_in_dim.60, s32[36]{0:T(128)S(1)} %get-tuple-element.11, f32[36,256,128]{2,1,0:T(8,128)} %copy.14), kind=kCustom, calls=%fused_computation.6 | custom fusion | flops 1179648 | bytes 14155920 | tf_op jit(solution)/shard_map/scatter-add | solution.py:66
  138.4 3.0 %fusion.23 = (f32[8,256,128]{2,1,0:T(8,128)}, f32[8,256,128]{2,1,0:T(8,128)}) fusion(f32[26,256,128]{2,1,0:T(8,128)} %scatter_fusion.1), kind=kLoop, calls=%fused_computation.50 | loop fusion | bytes 4194304 | tf_op jit(solution)/shard_map/slice | solution.py:67
  141.4 3.9 %collective-permute-start.2 = (f32[8,256,128]{2,1,0:T(8,128)}, f32[8,256,128]{2,1,0:T(8,128)}, u32[]{:S(2)}, u32[]{:S(2)}) collective-permute-start(f32[8,256,128]{2,1,0:T(8,128)} %get-tuple-element.12), channel_id=1, source_target_pairs={{0,1},{1,2},{2,3},{3,4},{4,5},{5,6},{6,7},{8,9},{9,10},{10,11},{11... | collective-permute-start | bytes 3145736 | tf_op jit(solution)/shard_map/ppermute | solution.py:30
  145.3 1.5 collective-permute-start.3
  146.7 6.1 %fusion.6 = f32[36,256,128]{1,2,0:T(8,128)} fusion(bf16[1,36,256,256]{3,2,1,0:T(8,128)(2,1)} %param.13, bf16[40,256,128]{2,1,0:T(8,128)(2,1)S(1)} %bitcast.48), kind=kOutput, calls=%fused_computation.15 | convolution fusion | flops 603979776 | bytes 11796480 | tf_op jit(solution)/shard_map/kij,kjf->kif/dot_general | solution.py:60
  152.9 1.7 slice.44
  154.6 6.1 %copy.12 = f32[36,256,128]{2,1,0:T(8,128)} copy(f32[36,256,128]{1,2,0:T(8,128)} %fusion.6) | data formatting | bytes 9437184 | tf_op jit(solution)/shard_map/kij,kjf->kif/dot_general | solution.py:60
  160.7 0.1 broadcast_in_dim.54
  160.8 8.8 %scatter_fusion = f32[10,256,128]{2,1,0:T(8,128)S(1)} fusion(f32[10,256,128]{2,1,0:T(8,128)S(1)} %broadcast_in_dim.54, s32[36]{0:T(128)S(1)} %select_bitcast_fusion, f32[36,256,128]{2,1,0:T(8,128)} %copy.12), kind=kCustom, calls=%fused_computation.5 | custom fusion | flops 1179648 | bytes 14155920 | tf_op jit(solution)/shard_map/scatter-add | solution.py:63
  169.6 0.7 slice.40
  170.3 0.0 all-reduce.10.cloned.1.call-update
  170.4 75.4 %all-reduce.10.cloned.1.call-done = (f32[2,256,128]{2,1,0:T(8,128)}, f32[2,256,128]{2,1,0:T(8,128)}) async-done(((f32[2,256,128]{2,1,0:T(8,128)}, f32[2,256,128]{2,1,0:T(8,128)}), (f32[2,256,128]{2,1,0:T(8,128)}, f32[2,256,128]{2,1,0:T(8,128)})) %all-reduce.10.cloned.1.call-update) | async-done | bytes 524304 | tf_op jit(solution)/shard_map/psum | solution.py:70
  245.8 0.0 copy-start.2
  245.8 1.1 slice_add_fusion.1
  246.9 0.6 gather_fusion.2
  247.5 0.0 collective-permute-done.2
  247.5 0.0 collective-permute-done.3
  247.5 0.0 copy-done.2
  247.5 2.0 fusion.17
  249.5 1.6 gather_fusion.4
  251.1 2.5 broadcast_select_fusion.2
  253.6 40.7 %all-reduce.11 = (bf16[2048,128]{1,0:T(8,128)(2,1)S(1)}, bf16[2048,128]{1,0:T(8,128)(2,1)S(1)}) all-reduce(f32[2048,128]{1,0:T(8,128)} %bitcast.52, f32[2048,128]{1,0:T(8,128)S(1)} %bitcast.51), channel_id=1, replica_groups=mesh['level'=4,'band'=8] {'level'}, use_global_device_ids=true, to_apply=%region_4.7 | all-reduce | flops 524288 | bytes 3145728 | tf_op jit(solution)/shard_map/psum | solution.py:78
  294.3 0.7 fusion.18
  (7 shorter events, 0.0 us)
Async XLA Ops:
  7.2 1.4 copy-start
  7.2 85.5 %all-reduce.8.cloned.1.call-start = ((), (), s32[]{:S(2)}) async-start(), calls=%async_computation | async-start | bytes 262144 | tf_op jit(solution)/shard_map/psum | solution.py:24
  9.4 83.3 %collective-permute-start.1 = (bf16[8,256,128]{2,1,0:T(8,128)(2,1)S(1)}, bf16[8,256,128]{2,1,0:T(8,128)(2,1)S(1)}, u32[]{:S(2)}, u32[]{:S(2)}) collective-permute-start(bf16[8,256,128]{2,1,0:T(8,128)(2,1)S(1)} %broadcast_select_fusion.4), channel_id=1, source_target_pairs={{1,0},{2,1},{3,2},{4,3},{5,4},{6,5},{7,6},{9,8},{10,9},{11,10},{12... | collective-permute-start | bytes 1572872 | tf_op jit(solution)/shard_map/ppermute | solution.py:17
  10.7 82.0 %collective-permute-start = (bf16[8,256,128]{2,1,0:T(8,128)(2,1)S(1)}, bf16[8,256,128]{2,1,0:T(8,128)(2,1)S(1)}, u32[]{:S(2)}, u32[]{:S(2)}) collective-permute-start(bf16[8,256,128]{2,1,0:T(8,128)(2,1)S(1)} %broadcast_select_fusion.4), channel_id=1, source_target_pairs={{0,1},{1,2},{2,3},{3,4},{4,5},{5,6},{6,7},{8,9},{9,10},{10,11},{11... | collective-permute-start | bytes 1572872 | tf_op jit(solution)/shard_map/ppermute | solution.py:14
  16.9 228.9 %all-reduce.10.cloned.1.call-start = ((), (), s32[]{:S(2)}) async-start(), calls=%async_computation.1 | async-start | bytes 1048576 | tf_op jit(solution)/shard_map/psum | solution.py:70
  108.9 1.7 copy-start.1
  141.4 106.1 %collective-permute-start.2 = (f32[8,256,128]{2,1,0:T(8,128)}, f32[8,256,128]{2,1,0:T(8,128)}, u32[]{:S(2)}, u32[]{:S(2)}) collective-permute-start(f32[8,256,128]{2,1,0:T(8,128)} %get-tuple-element.12), channel_id=1, source_target_pairs={{0,1},{1,2},{2,3},{3,4},{4,5},{5,6},{6,7},{8,9},{9,10},{10,11},{11... | collective-permute-start | bytes 3145736 | tf_op jit(solution)/shard_map/ppermute | solution.py:30
  145.3 102.2 %collective-permute-start.3 = (f32[8,256,128]{2,1,0:T(8,128)}, f32[8,256,128]{2,1,0:T(8,128)}, u32[]{:S(2)}, u32[]{:S(2)}) collective-permute-start(f32[8,256,128]{2,1,0:T(8,128)} %get-tuple-element.13), channel_id=1, source_target_pairs={{1,0},{2,1},{3,2},{4,3},{5,4},{6,5},{7,6},{9,8},{10,9},{11,10},{12... | collective-permute-start | bytes 3145736 | tf_op jit(solution)/shard_map/ppermute | solution.py:30
  245.8 1.7 copy-start.2
Sparse Core Ops, SparseCore 0:
  17.0 75.5 all-reduce.7
  170.5 75.2 all-reduce.9
where the time goes:
time: 303 us; the launch traced here: 302 us
  waiting for transfers between devices  148 us (49%)
  blocking collectives  40.7 us (13%)
  other arithmetic  38.6 us (13%)
  local copies, waits for them, and re-layouts  36.1 us (12%)
  between operations  14.3 us (5%)
  starting transfers between devices  12.2 us (4%)
  matrix products  11.6 us (4%)
    psum x1, waiting for transfers between devices, on_device(): head_fwd, head_bwd = lax.psum((fwd_head, bwd_window[3 * blocks:]), 'band')  75.4 us
    psum x1, waiting for transfers between devices, from_root(): return lax.psum(block, axis)  72.9 us
    psum x1, blocking collectives, on_device(): fwd_all, bwd_all = lax.psum((fwd_global, bwd_global), 'level')  40.7 us
    scatter-add x1, other arithmetic, on_device(): jax.ops.segment_sum(prod_bwd, col_slot, num_segments=window_len)  14.1 us
    scatter-add x1, other arithmetic, on_device(): jax.ops.segment_sum(prod_fwd, fwd_slot, num_segments=blocks + heads)  8.84 us
    dot_general x1, matrix products, on_device(): jnp.einsum('kij,kjf->kif', vals, by_col, preferred_element_type=jnp.float32)  6.14 us
    dot_general x1, local copies, waits for them, and re-layouts, on_device(): jnp.einsum('kij,kjf->kif', vals, by_col, preferred_element_type=jnp.float32)  6.13 us
  transfers between devices with their start and end apart: 6, of which 2 were waited for; matrix products, arithmetic and copies ran while one was open for 10% of the time, Pallas kernels for 0%

commit v1 on v0

v1 whole, which is shorter than its diff:
```python
import functools

import jax
import jax.numpy as jnp
from jax import lax
from jax.experimental import pallas as pl
from jax.experimental.pallas import tpu as pltpu
from jax.sharding import PartitionSpec as P

HEADB = 2
GROUPS = 16
UNROLL = 4
F32 = jnp.float32
I16 = jnp.int16
VMEM = pl.BlockSpec(memory_space=pltpu.VMEM)
SMEM = pl.BlockSpec(memory_space=pltpu.SMEM)


def call(kernel, outs, ins, scratch=(), flops=0):
    bytes_moved = sum(a.size * a.dtype.itemsize for a in (*outs, *ins))
    return pl.pallas_call(
        kernel,
        out_shape=outs,
        in_specs=[SMEM if a.ndim == 1 else VMEM for a in ins],
        out_specs=[VMEM] * len(outs),
        scratch_shapes=list(scratch),
        compiler_params=pltpu.CompilerParams(vmem_limit_bytes=32 * 2**20),
        cost_estimate=pl.CostEstimate(flops=flops, bytes_accessed=bytes_moved, transcendentals=0),
    )(*ins)


def array(shape, dtype=F32):
    return jax.ShapeDtypeStruct(tuple(shape), dtype)


def encode(value):
    rows, width = value.shape
    grouped = value.reshape(GROUPS, rows // GROUPS, width)
    largest = jnp.maximum(jnp.max(jnp.abs(grouped), axis=1), 1e-30)
    power = jnp.ceil(jnp.log2(largest))
    scaled = jnp.round(grouped * jnp.exp2(15.0 - power)[:, None, :])
    codes = jnp.clip(scaled, -32767.0, 32767.0).astype(jnp.int32).astype(I16)
    return codes.reshape(rows, width), power.astype(jnp.int32).astype(I16)


def put_coded(ref, index, value):
    rows = value.shape[0]
    codes, power = encode(value)
    ref[index, :rows, :] = codes
    ref[index, rows:, :] = power


def get_coded(ref, index):
    rows, width = ref.shape[-2] - GROUPS, ref.shape[-1]
    codes = ref[index, :rows, :].astype(jnp.int32).astype(F32)
    power = ref[index, rows:, :].astype(jnp.int32).astype(F32)
    grouped = codes.reshape(GROUPS, rows // GROUPS, width) * jnp.exp2(power - 15.0)[:, None, :]
    return grouped.reshape(rows, width)


def dot(a, b):
    return jnp.dot(a, b, preferred_element_type=F32)


def dot_t(a, b):
    return lax.dot_general(a, b, (((0,), (0,)), ((), ())), preferred_element_type=F32)


class Meta:
    def __init__(self, ref, count, blocks):
        self.ref, self.count, self.blocks = ref, count, blocks
        self.level = ref[2 * count + blocks]
        self.band = ref[2 * count + blocks + 1]

    def row(self, k):
        return self.ref[k]

    def col(self, k):
        return self.ref[self.count + k]

    def perm(self, j):
        return self.ref[2 * self.count + j]

    def low(self):
        return self.band * self.blocks

    def own_row(self, k):
        at = self.row(k) - self.low()
        return (at >= 0) & (at < self.blocks)

    def own_col(self, k):
        at = self.col(k) - self.low()
        return (at >= 0) & (at < self.blocks)

    def near_col(self, k):
        at = self.col(k) - self.low()
        return (at >= -self.blocks) & (at < 2 * self.blocks)

    def x_row(self, k):
        return self.perm(self.row(k) - self.low())

    def x_col(self, k):
        return self.perm(self.col(k) - self.low())


def for_tiles(count, chosen, listed, product, place, acc, trash):
    def note(k, n):
        listed[n] = k
        return n + chosen(k).astype(jnp.int32)

    n = lax.fori_loop(0, count, note, jnp.int32(0))
    unit = acc.shape[1]

    def step(i, carry):
        tiles = [listed[jnp.minimum(i * UNROLL + u, n - 1)] for u in range(UNROLL)]
        products = [product(k) for k in tiles]
        for u in range(UNROLL):
            real = i * UNROLL + u < n
            for part in range(products[u].shape[0] // unit):
                slot = jnp.where(real, place(tiles[u], part), trash)
                acc[slot] += products[u][part * unit : (part + 1) * unit]
        return carry

    lax.fori_loop(0, lax.div(n + UNROLL - 1, jnp.int32(UNROLL)), step, 0)


class Shares:
    def __init__(self, levels, rdev, tile, parts):
        self.share = rdev // levels
        self.unit = min(tile, self.share)
        self.per = self.share // self.unit
        self.m = levels // 2
        self.parts = parts
        self.tile = tile
        self.slots = 2 * parts * self.m * self.per

    def slot(self, level, part, block, piece):
        at = (block * self.tile + piece * self.unit) // self.unit
        owner = lax.div(at, jnp.int32(self.per))
        keep = 1 - ((owner ^ level) & 1)
        return ((keep * self.parts + part) * self.m + (owner >> 1)) * self.per + lax.rem(at, jnp.int32(self.per))


def heads_out_kernel(count, blocks, meta_ref, x, vals, coded, plain, acc, listed):
    meta = Meta(meta_ref, count, blocks)
    acc[...] = jnp.zeros_like(acc)
    for_tiles(
        count,
        lambda k: ~meta.own_row(k),
        listed,
        lambda k: dot(vals[k], x[meta.x_col(k)]),
        lambda k, part: meta.row(k),
        acc,
        2 * HEADB,
    )
    for_tiles(
        count,
        lambda k: meta.own_row(k) & ~meta.near_col(k),
        listed,
        lambda k: dot_t(vals[k], x[meta.x_row(k)]),
        lambda k, part: HEADB + meta.col(k),
        acc,
        2 * HEADB,
    )
    for i in range(2 * HEADB):
        plain[i] = acc[i]
        put_coded(coded, i, acc[i])


def heads_add_kernel(had, came, coded, plain):
    for i in range(had.shape[0]):
        value = had[i] + get_coded(came, i)
        plain[i] = value
        put_coded(coded, i, value)


def halo_out_kernel(count, blocks, shares, meta_ref, near_ref, x, vals, send, keep, own, acc, listed):
    meta = Meta(meta_ref, count, blocks)
    acc[...] = jnp.zeros_like(acc)
    trash = 2 * shares.slots

    def place(k, piece):
        at = meta.col(k) - meta.low()
        is_low, is_high = at < 0, at >= blocks
        block = jnp.where(
            is_low,
            near_ref[jnp.clip(at + blocks, 0, blocks - 1)],
            jnp.where(
                is_high,
                near_ref[blocks + jnp.clip(at - blocks, 0, blocks - 1)],
                meta.perm(jnp.clip(at, 0, blocks - 1)),
            ),
        )
        part = jnp.where(is_low | is_high, is_high.astype(jnp.int32), 1)
        base = jnp.where(is_low | is_high, 0, shares.slots)
        return base + shares.slot(meta.level, part, block, piece)

    for_tiles(
        count,
        lambda k: meta.own_row(k) & meta.near_col(k),
        listed,
        lambda k: dot_t(vals[k], x[meta.x_row(k)]),
        place,
        acc,
        trash,
    )
    for_tiles(
        count,
        lambda k: meta.own_row(k) & meta.own_col(k),
        listed,
        lambda k: dot(vals[k], x[meta.x_col(k)]),
        lambda k, piece: shares.slots + shares.slot(meta.level, 0, meta.x_row(k), piece),
        acc,
        trash,
    )
    half = shares.slots // 2
    send[...] = acc[:half].reshape(send.shape)
    keep[...] = acc[half : 2 * half].reshape(keep.shape)
    own[...] = acc[2 * half : 4 * half]


def own_kernel(count, blocks, shares, meta_ref, near_ref, vals, own, low, high, low2, high2, xh, heads, send, keep, acc, xw, listed):
    meta = Meta(meta_ref, count, blocks)
    half_blocks = blocks // 2
    core = meta.level & 1
    for j in range(half_blocks):
        xw[core * half_blocks + j] = low[j]
        xw[(1 - core) * half_blocks + j] = low2[j]
        xw[blocks + core * half_blocks + j] = high[j]
        xw[blocks + (1 - core) * half_blocks + j] = high2[j]
    for j in range(HEADB):
        xw[2 * blocks + j] = xh[j]
    acc[: shares.slots] = own[...]
    trash = shares.slots

    def source(k):
        at = meta.col(k) - meta.low()
        is_low = (at < 0) & (at >= -blocks)
        is_high = (at >= blocks) & (at < 2 * blocks)
        return jnp.where(
            is_low,
            near_ref[jnp.clip(at + blocks, 0, blocks - 1)],
            jnp.where(
                is_high,
                blocks + near_ref[blocks + jnp.clip(at - blocks, 0, blocks - 1)],
                2 * blocks + jnp.clip(meta.col(k), 0, HEADB - 1),
            ),
        )

    for_tiles(
        count,
        lambda k: meta.own_row(k) & ~meta.own_col(k),
        listed,
        lambda k: dot(vals[k], xw[source(k)]),
        lambda k, piece: shares.slot(meta.level, 0, meta.x_row(k), piece),
        acc,
        trash,
    )
    for_tiles(
        count,
        lambda k: ~meta.own_row(k),
        listed,
        lambda k: dot_t(vals[k], xw[2 * blocks + meta.row(k)]),
        lambda k, piece: shares.slot(meta.level, 1, meta.x_col(k), piece),
        acc,
        trash,
    )

    @pl.when(meta.band == 0)
    def _():
        for part in range(2):
            for h in range(HEADB):
                for piece in range(shares.tile // shares.unit):
                    slot = shares.slot(meta.level, part, meta.perm(h), piece)
                    acc[slot] += heads[part * HEADB + h, piece * shares.unit : (piece + 1) * shares.unit]

    half = shares.slots // 2
    send[...] = acc[:half].reshape(send.shape)
    keep[...] = acc[half : 2 * half].reshape(keep.shape)


def split_kernel(bit, coded_in, meta_ref, had, came, send, keep, at):
    mine = (meta_ref[at] >> bit) & 1
    parts, m, share, width = had.shape
    for part in range(parts):
        for i in range(m // 2):
            for half in range(2):
                j = 2 * i + (mine if half else 1 - mine)
                came_value = get_coded(came, part * m + j) if coded_in else came[part, j]
                value = had[part, j] + came_value
                if half:
                    keep[part, i] = value
                else:
                    put_coded(send, part * (m // 2) + i, value)


def edge_kernel(coded_in, had, came, low, high):
    for part, out in enumerate((low, high)):
        came_value = get_coded(came, part) if coded_in else came[part, 0]
        put_coded(out, 0, had[part, 0] + came_value)


def last_kernel(coded_in, had, came, from_low, from_high, forward, backward):
    came_values = [get_coded(came, part) if coded_in else came[part, 0] for part in range(2)]
    forward[0] = (had[0, 0] + came_values[0]).astype(forward.dtype)
    total = had[1, 0] + came_values[1] + get_coded(from_low, 0) + get_coded(from_high, 0)
    backward[0] = total.astype(backward.dtype)


def over_levels(send, keep, meta, level_at, levels):
    bit, coded = 0, False
    parts, m, share, width = keep.shape
    while True:
        pairs = [(i, i ^ (1 << bit)) for i in range(levels)]
        came = lax.ppermute(send, "level", pairs)
        if m == 1:
            return keep, came, coded
        bit += 1
        send, keep = call(
            functools.partial(split_kernel_at, bit, coded, level_at),
            (array((parts * (m // 2), share + GROUPS, width), I16), array((parts, m // 2, share, width))),
            (meta, keep, came),
        )
        coded = True
        m //= 2


def split_kernel_at(bit, coded, at, meta_ref, had, came, send, keep):
    split_kernel(bit, coded, meta_ref, had, came, send, keep, at)


def on_device(features, block_perm, tile_rows, tile_cols, tile_vals):
    rdev, width = features.shape
    blocks = block_perm.shape[2]
    tile = tile_vals.shape[2]
    count = tile_vals.shape[1]
    levels = lax.axis_size("level")
    bands = lax.axis_size("band")
    level, band = lax.axis_index("level"), lax.axis_index("band")
    up = [(i, i + 1) for i in range(bands - 1)]
    down = [(i + 1, i) for i in range(bands - 1)]
    shares = Shares(levels, rdev, tile, 2)
    share, m, unit = shares.share, shares.m, shares.unit
    level_at = 2 * count + blocks

    perm = block_perm[0, 0]
    vals = tile_vals[0]
    x = features.reshape(blocks, tile, width)
    place = jnp.stack([level, band]).astype(jnp.int32)
    meta = jnp.concatenate([tile_rows[0], tile_cols[0], perm, place])
    near = jnp.concatenate([lax.ppermute(perm, "band", up), lax.ppermute(perm, "band", down)])

    mine = lax.dynamic_slice_in_dim(x, (level & 1) * (blocks // 2), blocks // 2, 0)
    low = lax.ppermute(mine, "band", up)
    high = lax.ppermute(mine, "band", down)
    cores = [(i, i ^ 1) for i in range(levels)]
    low2 = lax.ppermute(low, "level", cores)
    high2 = lax.ppermute(high, "level", cores)

    xh = jnp.concatenate([lax.dynamic_slice_in_dim(x, perm[h], 1, 0) for h in range(HEADB)])
    step = bands // 2
    while step:
        got = lax.ppermute(xh, "band", [(i, i + step) for i in range(0, bands, 2 * step)])
        xh = jnp.where(band % (2 * step) == step, got, xh)
        step //= 2

    coded_heads = array((2 * HEADB, tile + GROUPS, width), I16)
    plain_heads = array((2 * HEADB, tile, width))
    coded, heads = call(
        functools.partial(heads_out_kernel, count, blocks),
        (coded_heads, plain_heads),
        (meta, x, vals),
        (pltpu.VMEM((2 * HEADB + 1, tile, width), F32), pltpu.SMEM((count + 1,), jnp.int32)),
    )
    step = 1
    while step < bands:
        came = lax.ppermute(coded, "band", [(i + step, i) for i in range(0, bands, 2 * step)])
        coded, heads = call(heads_add_kernel, (coded_heads, plain_heads), (heads, came))
        step *= 2

    half_shape = array((2, m, share, width))
    send, keep, own = call(
        functools.partial(halo_out_kernel, count, blocks, shares),
        (half_shape, half_shape, array((shares.slots, unit, width))),
        (meta, near, x, vals),
        (pltpu.VMEM((2 * shares.slots + 1, unit, width), F32), pltpu.SMEM((count + 1,), jnp.int32)),
    )
    had, came, was_coded = over_levels(send, keep, meta, level_at, levels)
    edge = array((1, share + GROUPS, width), I16)
    to_low, to_high = call(functools.partial(edge_kernel, was_coded), (edge, edge), (had, came))
    from_low = lax.ppermute(to_high, "band", up)
    from_high = lax.ppermute(to_low, "band", down)

    send, keep = call(
        functools.partial(own_kernel, count, blocks, shares),
        (half_shape, half_shape),
        (meta, near, vals, own, low, high, low2, high2, xh, heads),
        (
            pltpu.VMEM((shares.slots + 1, unit, width), F32),
            pltpu.VMEM((2 * blocks + HEADB, tile, width), features.dtype),
            pltpu.SMEM((count + 1,), jnp.int32),
        ),
    )
    had, came, was_coded = over_levels(send, keep, meta, level_at, levels)
    out = array((1, share, width), jnp.bfloat16)
    forward, backward = call(
        functools.partial(last_kernel, was_coded), (out, out), (had, came, from_low, from_high)
    )
    return forward, backward


def solution(mesh):
    return jax.shard_map(
        on_device,
        mesh=mesh,
        in_specs=(
            P("band", None),
            P("level", "band", None),
            P("level", "band"),
            P("level", "band"),
            P("level", "band", None, None),
        ),
        out_specs=(P("band", "level", None), P("band", "level", None)),
        check_vma=False,
    )
```

time: 303 us -> 86.8 us (0.29)
  waiting for transfers between devices: 148 us -> 19.1 us
  blocking collectives: 40.7 us -> 0 us
  other arithmetic: 38.6 us -> 0.15 us
  local copies, waits for them, and re-layouts: 36.1 us -> 8.78 us
  starting transfers between devices: 12.2 us -> 38 us
  Pallas kernels: 0 us -> 15.3 us
  matrix products: 11.6 us -> 0 us
  between operations: 14.3 us -> 4.83 us
    psum x2 -> x0, waiting for transfers between devices: 148 us -> none  [the longest x1 75.4 us: on_device(): head_fwd, head_bwd = lax.psum((fwd_head, bwd_window[3 * blocks:]), 'band')]
    psum x1 -> x0, blocking collectives: 40.7 us -> none  [on_device(): fwd_all, bwd_all = lax.psum((fwd_global, bwd_global), 'level')]
    ppermute x4 -> x18, starting transfers between devices: 12.2 us -> 38 us  [the longest x3 11.2 us: on_device(): lax.ppermute(xh, 'band', [(i, i + step) for i in range(0, bands, 2 * step)])]
    scatter-add x2 -> x0, other arithmetic: 22.9 us -> none  [the longest x1 14.1 us: on_device(): jax.ops.segment_sum(prod_bwd, col_slot, num_segments=window_len)]
    ppermute x4 -> x18, waiting for transfers between devices: 0.01 us -> 19.1 us  [the longest x3 7.38 us: on_device(): lax.ppermute(coded, 'band', [(i + step, i) for i in range(0, bands, 2 * s...]
    pallas_call x0 -> x10, Pallas kernels: none -> 15.3 us  [call(): pl.pallas_call(kernel, out_shape=outs, in_specs=[SMEM if a.ndim == 1 else...]
    dot_general x2 -> x0, local copies, waits for them, and re-layouts: 12.2 us -> none  [the longest x1 6.13 us: on_device(): jnp.einsum('kij,kjf->kif', vals, by_col, preferred_element_type=jnp.float32)]
    dot_general x2 -> x0, matrix products: 11.6 us -> none  [the longest x1 6.14 us: on_device(): jnp.einsum('kij,kjf->kif', vals, by_col, preferred_element_type=jnp.float32)]
  transfers between devices with their start and end apart: 6 -> 18, of which waited for: 2 -> 6; matrix products, arithmetic and copies ran while one was open for 10% -> 1% of each run, Pallas kernels for 0% -> 17%
where the time goes in v1:
time: 86.8 us; the launch traced here: 86.2 us
  starting transfers between devices  38 us (44%)
  waiting for transfers between devices  19.1 us (22%)
  Pallas kernels  15.3 us (18%)
  local copies, waits for them, and re-layouts  8.78 us (10%)
  between operations  4.83 us (6%)
    pallas_call x10, Pallas kernels, call(): pl.pallas_call(kernel, out_shape=outs, in_specs=[SMEM if a.ndim == 1 else...  15.3 us
    ppermute x3, starting transfers between devices, on_device(): lax.ppermute(xh, 'band', [(i, i + step) for i in range(0, bands, 2 * step)])  11.2 us
    ppermute x3, waiting for transfers between devices, on_device(): lax.ppermute(coded, 'band', [(i + step, i) for i in range(0, bands, 2 * s...  7.38 us
    unnamed x12, local copies, waits for them, and re-layouts  5.73 us
    ppermute x1, starting transfers between devices, on_device(): lax.ppermute(perm, 'band', up)  5.57 us
    ppermute x4, waiting for transfers between devices, over_levels(): came = lax.ppermute(send, 'level', pairs)  5.33 us
    ppermute x1, waiting for transfers between devices, on_device(): from_high = lax.ppermute(to_low, 'band', down)  5.09 us
    ppermute x1, starting transfers between devices, on_device(): low = lax.ppermute(mine, 'band', up)  4.56 us
  transfers between devices with their start and end apart: 18, of which 6 were waited for; matrix products, arithmetic and copies ran while one was open for 1% of the time, Pallas kernels for 17%

profile of v1, /device:TPU:0, one launch (start us, length us, event | category | flops | bytes accessed | tf_op | source)
XLA Modules:
  0.0 86.2 jit_solution(7452176799205467919)
XLA Ops:
  0.6 0.0 copy-start.5
  0.6 0.0 copy-start.4
  0.7 1.4 %fusion = (s32[1,1,1]{2,1,0:T(1,128)}, s32[1,1,1]{2,1,0:T(1,128)}) fusion(s32[1,1,8]{2,1,0:T(1,128)} %param.6), kind=kLoop, calls=%fused_computation.8 | loop fusion | bytes 16 | tf_op jit(solution)/shard_map/slice | solution.py:360
  5.9 0.9 %constant_dynamic-slice_fusion.1 = (bf16[1,256,128]{2,1,0:T(8,128)(2,1)S(1)}, bf16[1,256,128]{2,1,0:T(8,128)(2,1)S(1)}) fusion(bf16[8,256,128]{2,1,0:T(8,128)(2,1)} %bitcast.12, s32[]{:T(128)S(6)} %select_n.51, s32[]{:T(128)S(6)} %select_n.52), kind=kLoop, calls=%fused_computation.5 | loop fusion | bytes 262152 | tf_op jit(solution)/shard_map/dynamic_slice | solution.py:360
  6.8 5.9 %collective-permute-start.6 = (bf16[2,256,128]{2,1,0:T(8,128)(2,1)S(1)}, bf16[2,256,128]{2,1,0:T(8,128)(2,1)S(1)}, u32[]{:S(2)}, u32[]{:S(2)}) collective-permute-start(bf16[2,256,128]{2,1,0:T(8,128)(2,1)S(1)} %pad_maximum_fusion), channel_id=1, source_target_pairs={{0,4},{8,12},{16,20},{24,28}} | collective-permute-start | bytes 393224 | tf_op jit(solution)/shard_map/ppermute | solution.py:363
  12.8 0.8 concatenate.9.meta_ref
  13.5 0.0 copy-start
  13.5 2.3 %copy-done = bf16[1,36,256,256]{3,2,1,0:T(8,128)(2,1)S(1)} copy-done((bf16[1,36,256,256]{3,2,1,0:T(8,128)(2,1)S(1)}, bf16[1,36,256,256]{3,2,1,0:T(8,128)(2,1)}, u32[]{:S(2)}) %copy-start) | copy-done | bytes 4718616
  15.9 0.0 copy-start.3
  15.9 1.0 %copy-done.3 = bf16[2048,128]{1,0:T(8,128)(2,1)S(1)} copy-done((bf16[2048,128]{1,0:T(8,128)(2,1)S(1)}, bf16[2048,128]{1,0:T(8,128)(2,1)}, u32[]{:S(2)}) %copy-start.3) | copy-done | bytes 524312
  16.9 1.5 %shard_map.69 = (s16[4,272,128]{2,1,0:T(8,128)(2,1)S(1)}, f32[4,256,128]{2,1,0:T(8,128)S(1)}) custom-call(s32[82]{0:T(128)S(1)} %concatenate.9.meta_ref, bf16[8,256,128]{2,1,0:T(8,128)(2,1)S(1)} %bitcast.13, bf16[36,256,256]{2,1,0:T(8,128)(2,1)S(1)} %bitcast.9), custom_call_target="tpu_custom_call" | custom-call | bytes 6046024 | tf_op jit(solution)/shard_map/pallas_call | solution.py:21
  18.4 1.3 %collective-permute-start.9 = (s16[4,272,128]{2,1,0:T(8,128)(2,1)S(1)}, s16[4,272,128]{2,1,0:T(8,128)(2,1)S(1)}, u32[]{:S(2)}, u32[]{:S(2)}) collective-permute-start(s16[4,272,128]{2,1,0:T(8,128)(2,1)S(1)} %get-tuple-element.22), channel_id=1, source_target_pairs={{1,0},{3,2},{5,4},{7,6},{9,8},{11,10},{13,12},{15,14},{17,16},{19,... | collective-permute-start | bytes 835592 | tf_op jit(solution)/shard_map/ppermute | solution.py:377
  19.7 0.0 collective-permute-done.6
  19.8 1.3 %collective-permute-start.7 = (bf16[2,256,128]{2,1,0:T(8,128)(2,1)S(1)}, bf16[2,256,128]{2,1,0:T(8,128)(2,1)S(1)}, u32[]{:S(2)}, u32[]{:S(2)}) collective-permute-start(bf16[2,256,128]{2,1,0:T(8,128)(2,1)S(1)} %broadcast_select_fusion), channel_id=1, source_target_pairs={{0,2},{4,6},{8,10},{12,14},{16,18},{20,22},{24,26},{28,30}} | collective-permute-start | bytes 393224 | tf_op jit(solution)/shard_map/ppermute | solution.py:363
  21.1 7.3 %collective-permute-done.9.came = s16[4,272,128]{2,1,0:T(8,128)(2,1)S(1)} collective-permute-done((s16[4,272,128]{2,1,0:T(8,128)(2,1)S(1)}, s16[4,272,128]{2,1,0:T(8,128)(2,1)S(1)}, u32[]{:S(2)}, u32[]{:S(2)}) %collective-permute-start.9) | collective-permute-done | bytes 278560 | tf_op jit(solution)/shard_map/ppermute | solution.py:377
  28.4 0.3 shard_map.70
  28.8 1.3 %collective-permute-start.10 = (s16[4,272,128]{2,1,0:T(8,128)(2,1)S(1)}, s16[4,272,128]{2,1,0:T(8,128)(2,1)S(1)}, u32[]{:S(2)}, u32[]{:S(2)}) collective-permute-start(s16[4,272,128]{2,1,0:T(8,128)(2,1)S(1)} %get-tuple-element.24), channel_id=1, source_target_pairs={{2,0},{6,4},{10,8},{14,12},{18,16},{22,20},{26,24},{30,28}} | collective-permute-start | bytes 835592 | tf_op jit(solution)/shard_map/ppermute | solution.py:377
  30.1 0.0 copy-done.4
  30.1 1.3 %collective-permute-start.3 = (bf16[4,256,128]{2,1,0:T(8,128)(2,1)S(1)}, bf16[4,256,128]{2,1,0:T(8,128)(2,1)S(1)}, u32[]{:S(2)}, u32[]{:S(2)}) collective-permute-start(bf16[4,256,128]{2,1,0:T(8,128)(2,1)S(1)} %constant_dynamic-slice_fusion.2), channel_id=1, source_target_pairs={{1,0},{2,1},{3,2},{4,3},{5,4},{6,5},{7,6},{9,8},{10,9},{11,10},{12... | collective-permute-start | bytes 786440 | tf_op jit(solution)/shard_map/ppermute | solution.py:355
  31.4 4.6 %collective-permute-start.2 = (bf16[4,256,128]{2,1,0:T(8,128)(2,1)S(1)}, bf16[4,256,128]{2,1,0:T(8,128)(2,1)S(1)}, u32[]{:S(2)}, u32[]{:S(2)}) collective-permute-start(bf16[4,256,128]{2,1,0:T(8,128)(2,1)S(1)} %constant_dynamic-slice_fusion.2), channel_id=1, source_target_pairs={{0,1},{1,2},{2,3},{3,4},{4,5},{5,6},{6,7},{8,9},{9,10},{10,11},{11... | collective-permute-start | bytes 786440 | tf_op jit(solution)/shard_map/ppermute | solution.py:354
  36.0 0.0 collective-permute-done.7
  36.0 4.0 %collective-permute-start.8 = (bf16[2,256,128]{2,1,0:T(8,128)(2,1)S(1)}, bf16[2,256,128]{2,1,0:T(8,128)(2,1)S(1)}, u32[]{:S(2)}, u32[]{:S(2)}) collective-permute-start(bf16[2,256,128]{2,1,0:T(8,128)(2,1)S(1)} %broadcast_select_fusion.1), channel_id=1, source_target_pairs={{0,1},{2,3},{4,5},{6,7},{8,9},{10,11},{12,13},{14,15},{16,17},{18,... | collective-permute-start | bytes 393224 | tf_op jit(solution)/shard_map/ppermute | solution.py:363
  40.0 0.0 copy-done.5
  40.0 1.3 %collective-permute-start.1 = (s32[8]{0:T(128)S(1)}, s32[8]{0:T(128)S(1)}, u32[]{:S(2)}, u32[]{:S(2)}) collective-permute-start(s32[8]{0:T(128)S(1)} %bitcast.17), channel_id=1, source_target_pairs={{1,0},{2,1},{3,2},{4,3},{5,4},{6,5},{7,6},{9,8},{10,9},{11,10},{12... | collective-permute-start | bytes 104 | tf_op jit(solution)/shard_map/ppermute | solution.py:351
  41.4 0.0 collective-permute-done.3.high
  41.4 5.6 %collective-permute-start = (s32[8]{0:T(128)S(1)}, s32[8]{0:T(128)S(1)}, u32[]{:S(2)}, u32[]{:S(2)}) collective-permute-start(s32[8]{0:T(128)S(1)} %bitcast.18), channel_id=1, source_target_pairs={{0,1},{1,2},{2,3},{3,4},{4,5},{5,6},{6,7},{8,9},{9,10},{10,11},{11... | collective-permute-start | bytes 104 | tf_op jit(solution)/shard_map/ppermute | solution.py:351
  46.9 0.1 collective-permute-done.2.low
  47.0 0.0 collective-permute-start.5
  47.0 0.0 collective-permute-done.10.came
  47.0 0.5 collective-permute-start.4
  47.6 0.3 shard_map.71
  47.9 0.0 collective-permute-done.1
  47.9 1.3 %collective-permute-start.11 = (s16[4,272,128]{2,1,0:T(8,128)(2,1)S(1)}, s16[4,272,128]{2,1,0:T(8,128)(2,1)S(1)}, u32[]{:S(2)}, u32[]{:S(2)}) collective-permute-start(s16[4,272,128]{2,1,0:T(8,128)(2,1)S(1)} %get-tuple-element.26), channel_id=1, source_target_pairs={{4,0},{12,8},{20,16},{28,24}} | collective-permute-start | bytes 835592 | tf_op jit(solution)/shard_map/ppermute | solution.py:377
  49.2 0.0 collective-permute-done
  49.2 0.1 pad_add_fusion.near_ref
  49.3 0.0 copy-start.1
  49.3 2.3 %copy-done.1 = bf16[1,36,256,256]{3,2,1,0:T(8,128)(2,1)S(1)} copy-done((bf16[1,36,256,256]{3,2,1,0:T(8,128)(2,1)S(1)}, bf16[1,36,256,256]{3,2,1,0:T(8,128)(2,1)}, u32[]{:S(2)}) %copy-start.1) | copy-done | bytes 4718616
  51.6 0.0 copy-start.2
  51.6 6.9 %shard_map.68 = (f32[2,2,512,128]{3,2,1,0:T(8,128)S(1)}, f32[2,2,512,128]{3,2,1,0:T(8,128)S(1)}, f32[16,256,128]{2,1,0:T(8,128)S(1)}) custom-call(s32[82]{0:T(128)S(1)} %concatenate.9.meta_ref, s32[16]{0:T(128)S(1)} %pad_add_fusion.near_ref, bf16[8,256,128]{2,1,0:T(8,128)(2,1)S(1)} %bitcast.15, bf16[36,256,256]{2,1,0:T(8,128)(2,1)S(1)} %bitcast.10), custom_call_target="tpu_custom_call" | custom-call | bytes 9437576 | tf_op jit(solution)/shard_map/pallas_call | solution.py:21
  58.5 0.8 collective-permute-start.14
  59.3 0.0 collective-permute-done.8
  59.3 0.0 collective-permute-done.11.came
  59.3 1.0 %shard_map.72 = (s16[4,272,128]{2,1,0:T(8,128)(2,1)}, f32[4,256,128]{2,1,0:T(8,128)S(1)}) custom-call(f32[4,256,128]{2,1,0:T(8,128)S(1)} %get-tuple-element.25.had, s16[4,272,128]{2,1,0:T(8,128)(2,1)S(1)} %collective-permute-done.11.came), custom_call_target="tpu_custom_call" | custom-call | bytes 1605632 | tf_op jit(solution)/shard_map/pallas_call | solution.py:21
  60.3 0.0 collective-permute-done.5.high2
  60.3 0.0 collective-permute-done.4.low2
  60.3 0.0 copy-done.2
  60.3 2.6 %shard_map.73 = (f32[2,2,512,128]{3,2,1,0:T(8,128)S(1)}, f32[2,2,512,128]{3,2,1,0:T(8,128)S(1)}) custom-call(s32[82]{0:T(128)S(1)} %concatenate.9.meta_ref, s32[16]{0:T(128)S(1)} %pad_add_fusion.near_ref, bf16[36,256,256]{2,1,0:T(8,128)(2,1)S(1)} %bitcast.11, f32[16,256,128]{2,1,0:T(8,128)S(1)} %get-tuple-element.20.own, ...), custom_call_target="tpu_custom_call" | custom-call | bytes 10617224 | tf_op jit(solution)/shard_map/pallas_call | solution.py:21
  63.0 0.1 collective-permute-start.12
  63.0 0.0 collective-permute-done.14.came
  63.0 0.8 shard_map.75
  63.8 1.6 %collective-permute-start.15 = (s16[2,528,128]{2,1,0:T(8,128)(2,1)S(1)}, s16[2,528,128]{2,1,0:T(8,128)(2,1)S(1)}, u32[]{:S(2)}, u32[]{:S(2)}) collective-permute-start(s16[2,528,128]{2,1,0:T(8,128)(2,1)S(1)} %get-tuple-element.35), channel_id=1, source_target_pairs={{0,16},{8,24},{16,0},{24,8},{1,17},{9,25},{17,1},{25,9},{2,18},{10... | collective-permute-start | bytes 811016 | tf_op jit(solution)/shard_map/ppermute | solution.py:315
  65.5 0.2 collective-permute-done.12.came
  65.7 0.8 shard_map.74
  66.5 1.6 %collective-permute-start.13 = (s16[2,528,128]{2,1,0:T(8,128)(2,1)S(1)}, s16[2,528,128]{2,1,0:T(8,128)(2,1)S(1)}, u32[]{:S(2)}, u32[]{:S(2)}) collective-permute-start(s16[2,528,128]{2,1,0:T(8,128)(2,1)S(1)} %get-tuple-element.31), channel_id=1, source_target_pairs={{0,16},{8,24},{16,0},{24,8},{1,17},{9,25},{17,1},{25,9},{2,18},{10... | collective-permute-start | bytes 811016 | tf_op jit(solution)/shard_map/ppermute | solution.py:315
  68.0 5.1 %collective-permute-done.15.came = s16[2,528,128]{2,1,0:T(8,128)(2,1)S(1)} collective-permute-done((s16[2,528,128]{2,1,0:T(8,128)(2,1)S(1)}, s16[2,528,128]{2,1,0:T(8,128)(2,1)S(1)}, u32[]{:S(2)}, u32[]{:S(2)}) %collective-permute-start.15) | collective-permute-done | bytes 270368 | tf_op jit(solution)/shard_map/ppermute | solution.py:315
  73.2 0.2 shard_map.76
  73.4 4.4 %collective-permute-start.16 = (s16[1,528,128]{2,1,0:T(8,128)(2,1)S(1)}, s16[1,528,128]{2,1,0:T(8,128)(2,1)S(1)}, u32[]{:S(2)}, u32[]{:S(2)}) collective-permute-start(s16[1,528,128]{2,1,0:T(8,128)(2,1)S(1)} %get-tuple-element.36), channel_id=1, source_target_pairs={{0,1},{1,2},{2,3},{3,4},{4,5},{5,6},{6,7},{8,9},{9,10},{10,11},{11... | collective-permute-start | bytes 405512 | tf_op jit(solution)/shard_map/ppermute | solution.py:391
  77.8 1.3 %collective-permute-start.17 = (s16[1,528,128]{2,1,0:T(8,128)(2,1)S(1)}, s16[1,528,128]{2,1,0:T(8,128)(2,1)S(1)}, u32[]{:S(2)}, u32[]{:S(2)}) collective-permute-start(s16[1,528,128]{2,1,0:T(8,128)(2,1)S(1)} %get-tuple-element.37), channel_id=1, source_target_pairs={{1,0},{2,1},{3,2},{4,3},{5,4},{6,5},{7,6},{9,8},{10,9},{11,10},{12... | collective-permute-start | bytes 405512 | tf_op jit(solution)/shard_map/ppermute | solution.py:392
  79.1 1.2 %collective-permute-done.16.from_low = s16[1,528,128]{2,1,0:T(8,128)(2,1)S(1)} collective-permute-done((s16[1,528,128]{2,1,0:T(8,128)(2,1)S(1)}, s16[1,528,128]{2,1,0:T(8,128)(2,1)S(1)}, u32[]{:S(2)}, u32[]{:S(2)}) %collective-permute-start.16) | collective-permute-done | bytes 135200 | tf_op jit(solution)/shard_map/ppermute | solution.py:391
  80.3 5.1 %collective-permute-done.17.from_high = s16[1,528,128]{2,1,0:T(8,128)(2,1)S(1)} collective-permute-done((s16[1,528,128]{2,1,0:T(8,128)(2,1)S(1)}, s16[1,528,128]{2,1,0:T(8,128)(2,1)S(1)}, u32[]{:S(2)}, u32[]{:S(2)}) %collective-permute-start.17) | collective-permute-done | bytes 135200 | tf_op jit(solution)/shard_map/ppermute | solution.py:392
  85.4 0.0 collective-permute-done.13.came
  85.4 0.8 shard_map.77
  (5 shorter events, 0.1 us)
Async XLA Ops:
  0.6 39.4 %copy-start.5 = (s32[1,1,8]{2,1,0:T(1,128)S(1)}, s32[1,1,8]{2,1,0:T(1,128)}, u32[]{:S(2)}) copy-start(s32[1,1,8]{2,1,0:T(1,128)} %param.6) | copy-start | bytes 100
  0.6 29.4 %copy-start.4 = (bf16[2048,128]{1,0:T(8,128)(2,1)S(1)}, bf16[2048,128]{1,0:T(8,128)(2,1)}, u32[]{:S(2)}) copy-start(bf16[2048,128]{1,0:T(8,128)(2,1)} %param.5) | copy-start | bytes 1572868
  6.8 12.9 %collective-permute-start.6 = (bf16[2,256,128]{2,1,0:T(8,128)(2,1)S(1)}, bf16[2,256,128]{2,1,0:T(8,128)(2,1)S(1)}, u32[]{:S(2)}, u32[]{:S(2)}) collective-permute-start(bf16[2,256,128]{2,1,0:T(8,128)(2,1)S(1)} %pad_maximum_fusion), channel_id=1, source_target_pairs={{0,4},{8,12},{16,20},{24,28}} | collective-permute-start | bytes 393224 | tf_op jit(solution)/shard_map/ppermute | solution.py:363
  13.5 2.3 %copy-start = (bf16[1,36,256,256]{3,2,1,0:T(8,128)(2,1)S(1)}, bf16[1,36,256,256]{3,2,1,0:T(8,128)(2,1)}, u32[]{:S(2)}) copy-start(bf16[1,36,256,256]{3,2,1,0:T(8,128)(2,1)} %param.9) | copy-start | bytes 14155780
  15.9 1.0 %copy-start.3 = (bf16[2048,128]{1,0:T(8,128)(2,1)S(1)}, bf16[2048,128]{1,0:T(8,128)(2,1)}, u32[]{:S(2)}) copy-start(bf16[2048,128]{1,0:T(8,128)(2,1)} %param.5) | copy-start | bytes 1572868
  18.4 10.0 %collective-permute-start.9 = (s16[4,272,128]{2,1,0:T(8,128)(2,1)S(1)}, s16[4,272,128]{2,1,0:T(8,128)(2,1)S(1)}, u32[]{:S(2)}, u32[]{:S(2)}) collective-permute-start(s16[4,272,128]{2,1,0:T(8,128)(2,1)S(1)} %get-tuple-element.22), channel_id=1, source_target_pairs={{1,0},{3,2},{5,4},{7,6},{9,8},{11,10},{13,12},{15,14},{17,16},{19,... | collective-permute-start | bytes 835592 | tf_op jit(solution)/shard_map/ppermute | solution.py:377
  19.8 16.2 %collective-permute-start.7 = (bf16[2,256,128]{2,1,0:T(8,128)(2,1)S(1)}, bf16[2,256,128]{2,1,0:T(8,128)(2,1)S(1)}, u32[]{:S(2)}, u32[]{:S(2)}) collective-permute-start(bf16[2,256,128]{2,1,0:T(8,128)(2,1)S(1)} %broadcast_select_fusion), channel_id=1, source_target_pairs={{0,2},{4,6},{8,10},{12,14},{16,18},{20,22},{24,26},{28,30}} | collective-permute-start | bytes 393224 | tf_op jit(solution)/shard_map/ppermute | solution.py:363
  28.8 18.3 %collective-permute-start.10 = (s16[4,272,128]{2,1,0:T(8,128)(2,1)S(1)}, s16[4,272,128]{2,1,0:T(8,128)(2,1)S(1)}, u32[]{:S(2)}, u32[]{:S(2)}) collective-permute-start(s16[4,272,128]{2,1,0:T(8,128)(2,1)S(1)} %get-tuple-element.24), channel_id=1, source_target_pairs={{2,0},{6,4},{10,8},{14,12},{18,16},{22,20},{26,24},{30,28}} | collective-permute-start | bytes 835592 | tf_op jit(solution)/shard_map/ppermute | solution.py:377
  30.1 11.3 %collective-permute-start.3 = (bf16[4,256,128]{2,1,0:T(8,128)(2,1)S(1)}, bf16[4,256,128]{2,1,0:T(8,128)(2,1)S(1)}, u32[]{:S(2)}, u32[]{:S(2)}) collective-permute-start(bf16[4,256,128]{2,1,0:T(8,128)(2,1)S(1)} %constant_dynamic-slice_fusion.2), channel_id=1, source_target_pairs={{1,0},{2,1},{3,2},{4,3},{5,4},{6,5},{7,6},{9,8},{10,9},{11,10},{12... | collective-permute-start | bytes 786440 | tf_op jit(solution)/shard_map/ppermute | solution.py:355
  31.4 15.6 %collective-permute-start.2 = (bf16[4,256,128]{2,1,0:T(8,128)(2,1)S(1)}, bf16[4,256,128]{2,1,0:T(8,128)(2,1)S(1)}, u32[]{:S(2)}, u32[]{:S(2)}) collective-permute-start(bf16[4,256,128]{2,1,0:T(8,128)(2,1)S(1)} %constant_dynamic-slice_fusion.2), channel_id=1, source_target_pairs={{0,1},{1,2},{2,3},{3,4},{4,5},{5,6},{6,7},{8,9},{9,10},{10,11},{11... | collective-permute-start | bytes 786440 | tf_op jit(solution)/shard_map/ppermute | solution.py:354
  36.0 23.2 %collective-permute-start.8 = (bf16[2,256,128]{2,1,0:T(8,128)(2,1)S(1)}, bf16[2,256,128]{2,1,0:T(8,128)(2,1)S(1)}, u32[]{:S(2)}, u32[]{:S(2)}) collective-permute-start(bf16[2,256,128]{2,1,0:T(8,128)(2,1)S(1)} %broadcast_select_fusion.1), channel_id=1, source_target_pairs={{0,1},{2,3},{4,5},{6,7},{8,9},{10,11},{12,13},{14,15},{16,17},{18,... | collective-permute-start | bytes 393224 | tf_op jit(solution)/shard_map/ppermute | solution.py:363
  40.0 7.8 %collective-permute-start.1 = (s32[8]{0:T(128)S(1)}, s32[8]{0:T(128)S(1)}, u32[]{:S(2)}, u32[]{:S(2)}) collective-permute-start(s32[8]{0:T(128)S(1)} %bitcast.17), channel_id=1, source_target_pairs={{1,0},{2,1},{3,2},{4,3},{5,4},{6,5},{7,6},{9,8},{10,9},{11,10},{12... | collective-permute-start | bytes 104 | tf_op jit(solution)/shard_map/ppermute | solution.py:351
  41.4 7.8 %collective-permute-start = (s32[8]{0:T(128)S(1)}, s32[8]{0:T(128)S(1)}, u32[]{:S(2)}, u32[]{:S(2)}) collective-permute-start(s32[8]{0:T(128)S(1)} %bitcast.18), channel_id=1, source_target_pairs={{0,1},{1,2},{2,3},{3,4},{4,5},{5,6},{6,7},{8,9},{9,10},{10,11},{11... | collective-permute-start | bytes 104 | tf_op jit(solution)/shard_map/ppermute | solution.py:351
  47.0 13.3 %collective-permute-start.5 = (bf16[4,256,128]{2,1,0:T(8,128)(2,1)S(1)}, bf16[4,256,128]{2,1,0:T(8,128)(2,1)S(1)}, u32[]{:S(2)}, u32[]{:S(2)}) collective-permute-start(bf16[4,256,128]{2,1,0:T(8,128)(2,1)S(1)} %collective-permute-done.3.high), channel_id=1, source_target_pairs={{0,8},{8,0},{16,24},{24,16},{1,9},{9,1},{17,25},{25,17},{2,10},{10... | collective-permute-start | bytes 786440 | tf_op jit(solution)/shard_map/ppermute | solution.py:358
  47.0 13.3 %collective-permute-start.4 = (bf16[4,256,128]{2,1,0:T(8,128)(2,1)S(1)}, bf16[4,256,128]{2,1,0:T(8,128)(2,1)S(1)}, u32[]{:S(2)}, u32[]{:S(2)}) collective-permute-start(bf16[4,256,128]{2,1,0:T(8,128)(2,1)S(1)} %collective-permute-done.2.low), channel_id=1, source_target_pairs={{0,8},{8,0},{16,24},{24,16},{1,9},{9,1},{17,25},{25,17},{2,10},{10... | collective-permute-start | bytes 786440 | tf_op jit(solution)/shard_map/ppermute | solution.py:357
  47.9 11.4 %collective-permute-start.11 = (s16[4,272,128]{2,1,0:T(8,128)(2,1)S(1)}, s16[4,272,128]{2,1,0:T(8,128)(2,1)S(1)}, u32[]{:S(2)}, u32[]{:S(2)}) collective-permute-start(s16[4,272,128]{2,1,0:T(8,128)(2,1)S(1)} %get-tuple-element.26), channel_id=1, source_target_pairs={{4,0},{12,8},{20,16},{28,24}} | collective-permute-start | bytes 835592 | tf_op jit(solution)/shard_map/ppermute | solution.py:377
  49.3 2.3 %copy-start.1 = (bf16[1,36,256,256]{3,2,1,0:T(8,128)(2,1)S(1)}, bf16[1,36,256,256]{3,2,1,0:T(8,128)(2,1)}, u32[]{:S(2)}) copy-start(bf16[1,36,256,256]{3,2,1,0:T(8,128)(2,1)} %param.9) | copy-start | bytes 14155780
  51.6 8.7 %copy-start.2 = (bf16[1,36,256,256]{3,2,1,0:T(8,128)(2,1)S(1)}, bf16[1,36,256,256]{3,2,1,0:T(8,128)(2,1)}, u32[]{:S(2)}) copy-start(bf16[1,36,256,256]{3,2,1,0:T(8,128)(2,1)} %param.9) | copy-start | bytes 14155780
  58.5 4.5 %collective-permute-start.14 = (f32[2,2,512,128]{3,2,1,0:T(8,128)S(1)}, f32[2,2,512,128]{3,2,1,0:T(8,128)S(1)}, u32[]{:S(2)}, u32[]{:S(2)}) collective-permute-start(f32[2,2,512,128]{3,2,1,0:T(8,128)S(1)} %get-tuple-element.33), channel_id=1, source_target_pairs={{0,8},{8,0},{16,24},{24,16},{1,9},{9,1},{17,25},{25,17},{2,10},{10... | collective-permute-start | bytes 3145736 | tf_op jit(solution)/shard_map/ppermute | solution.py:315
  63.0 2.7 %collective-permute-start.12 = (f32[2,2,512,128]{3,2,1,0:T(8,128)S(1)}, f32[2,2,512,128]{3,2,1,0:T(8,128)S(1)}, u32[]{:S(2)}, u32[]{:S(2)}) collective-permute-start(f32[2,2,512,128]{3,2,1,0:T(8,128)S(1)} %get-tuple-element.29), channel_id=1, source_target_pairs={{0,8},{8,0},{16,24},{24,16},{1,9},{9,1},{17,25},{25,17},{2,10},{10... | collective-permute-start | bytes 3145736 | tf_op jit(solution)/shard_map/ppermute | solution.py:315
  63.8 9.3 %collective-permute-start.15 = (s16[2,528,128]{2,1,0:T(8,128)(2,1)S(1)}, s16[2,528,128]{2,1,0:T(8,128)(2,1)S(1)}, u32[]{:S(2)}, u32[]{:S(2)}) collective-permute-start(s16[2,528,128]{2,1,0:T(8,128)(2,1)S(1)} %get-tuple-element.35), channel_id=1, source_target_pairs={{0,16},{8,24},{16,0},{24,8},{1,17},{9,25},{17,1},{25,9},{2,18},{10... | collective-permute-start | bytes 811016 | tf_op jit(solution)/shard_map/ppermute | solution.py:315
  66.5 18.9 %collective-permute-start.13 = (s16[2,528,128]{2,1,0:T(8,128)(2,1)S(1)}, s16[2,528,128]{2,1,0:T(8,128)(2,1)S(1)}, u32[]{:S(2)}, u32[]{:S(2)}) collective-permute-start(s16[2,528,128]{2,1,0:T(8,128)(2,1)S(1)} %get-tuple-element.31), channel_id=1, source_target_pairs={{0,16},{8,24},{16,0},{24,8},{1,17},{9,25},{17,1},{25,9},{2,18},{10... | collective-permute-start | bytes 811016 | tf_op jit(solution)/shard_map/ppermute | solution.py:315
  73.4 6.9 %collective-permute-start.16 = (s16[1,528,128]{2,1,0:T(8,128)(2,1)S(1)}, s16[1,528,128]{2,1,0:T(8,128)(2,1)S(1)}, u32[]{:S(2)}, u32[]{:S(2)}) collective-permute-start(s16[1,528,128]{2,1,0:T(8,128)(2,1)S(1)} %get-tuple-element.36), channel_id=1, source_target_pairs={{0,1},{1,2},{2,3},{3,4},{4,5},{5,6},{6,7},{8,9},{9,10},{10,11},{11... | collective-permute-start | bytes 405512 | tf_op jit(solution)/shard_map/ppermute | solution.py:391
  77.8 7.6 %collective-permute-start.17 = (s16[1,528,128]{2,1,0:T(8,128)(2,1)S(1)}, s16[1,528,128]{2,1,0:T(8,128)(2,1)S(1)}, u32[]{:S(2)}, u32[]{:S(2)}) collective-permute-start(s16[1,528,128]{2,1,0:T(8,128)(2,1)S(1)} %get-tuple-element.37), channel_id=1, source_target_pairs={{1,0},{2,1},{3,2},{4,3},{5,4},{6,5},{7,6},{9,8},{10,9},{11,10},{12... | collective-permute-start | bytes 405512 | tf_op jit(solution)/shard_map/ppermute | solution.py:392

commit v2 on v0

v2 whole, which is shorter than its diff:
```python
import functools
import math

import jax
import jax.numpy as jnp
from jax import lax
from jax.experimental import pallas as pl
from jax.experimental.pallas import tpu as pltpu
from jax.sharding import PartitionSpec as P

HEADB = 2
GROUPS = 16
UNROLL = 4
VMEM_LIMIT = 24 * 2**20
F32 = jnp.float32
I16 = jnp.int16
VMEM = pl.BlockSpec(memory_space=pltpu.VMEM)
ANY = pl.BlockSpec(memory_space=pl.ANY)
HBM = pl.BlockSpec(memory_space=pltpu.HBM)
SMEM = pl.BlockSpec(memory_space=pltpu.SMEM)


def call(kernel, outs, ins, scratch=(), after=(), in_hbm=0):
    bytes_moved = sum(math.prod(a.shape) * a.dtype.itemsize for a in (*outs, *ins))

    def body(*refs):
        kernel(*refs[: len(ins)], *refs[len(ins) + len(after) :])

    return pl.pallas_call(
        body,
        out_shape=outs,
        in_specs=[HBM] * in_hbm + [SMEM if a.ndim == 1 else VMEM for a in ins[in_hbm:]] + [ANY] * len(after),
        out_specs=[SMEM if len(a.shape) == 1 else VMEM for a in outs],
        scratch_shapes=list(scratch),
        compiler_params=pltpu.CompilerParams(vmem_limit_bytes=VMEM_LIMIT),
        cost_estimate=pl.CostEstimate(flops=0, bytes_accessed=bytes_moved, transcendentals=0),
    )(*ins, *after)


def array(shape, dtype=F32):
    return jax.ShapeDtypeStruct(tuple(shape), dtype)


def encode(value):
    rows, width = value.shape
    grouped = value.reshape(GROUPS, rows // GROUPS, width)
    largest = jnp.maximum(jnp.max(jnp.abs(grouped), axis=1), 1e-30)
    power = jnp.ceil(jnp.log2(largest))
    scaled = jnp.round(grouped * jnp.exp2(15.0 - power)[:, None, :])
    codes = jnp.clip(scaled, -32767.0, 32767.0).astype(jnp.int32).astype(I16)
    return codes.reshape(rows, width), power.astype(jnp.int32).astype(I16)


def put_coded(ref, index, value):
    rows = value.shape[0]
    codes, power = encode(value)
    ref[index, :rows, :] = codes
    ref[index, rows:, :] = power


def get_coded(ref, index):
    rows, width = ref.shape[-2] - GROUPS, ref.shape[-1]
    codes = ref[index, :rows, :].astype(jnp.int32).astype(F32)
    power = ref[index, rows:, :].astype(jnp.int32).astype(F32)
    grouped = codes.reshape(GROUPS, rows // GROUPS, width) * jnp.exp2(power - 15.0)[:, None, :]
    return grouped.reshape(rows, width)


def dot(a, b):
    return jnp.dot(a, b, preferred_element_type=F32)


def dot_t(a, b):
    return lax.dot_general(a, b, (((0,), (0,)), ((), ())), preferred_element_type=F32)


HEAD_ROW, HEAD_COL, NEAR, OWN, REMOTE = range(5)


def packed(k, source, target):
    return k | (source << 8) | (target << 16)


def write_plan(count, blocks, rows, cols, perm, plan):
    low = lax.axis_index("band") * blocks
    n = [jnp.int32(0)] * 5
    for k in range(count):
        row, col = rows[0, k] - low, cols[0, k] - low
        own_row = (row >= 0) & (row < blocks)
        own_col = (col >= 0) & (col < blocks)
        near = (col >= -blocks) & (col < 2 * blocks)
        x_row = perm[0, 0, jnp.clip(row, 0, blocks - 1)]
        x_col = perm[0, 0, jnp.clip(col, 0, blocks - 1)]
        near_at = jnp.where(near, col + blocks, 3 * blocks + cols[0, k])
        for which, chosen, source, target in (
            (HEAD_ROW, ~own_row, x_col, rows[0, k]),
            (HEAD_COL, own_row & ~near, x_row, HEADB + cols[0, k]),
            (NEAR, own_row & near & ~own_col, x_row, near_at),
            (OWN, own_row & own_col, x_row, x_col),
            (REMOTE, own_row & ~own_col, near_at, x_row),
        ):
            plan[which * count + n[which]] = packed(k, source, target)
            n[which] = n[which] + chosen.astype(jnp.int32)
    for which in range(5):
        plan[5 * count + which] = n[which]


def for_tiles(count, plan, vals, which, jobs, acc, trash):
    n = plan[5 * count + which]
    unit = acc.shape[1]

    def step(i, carry):
        entries = []
        for u in range(UNROLL):
            real = i * UNROLL + u < n
            e = plan[which * count + jnp.minimum(i * UNROLL + u, n - 1)]
            entries.append((real, e & 255, (e >> 8) & 255, e >> 16))
        products = [[product(vals[k], s, t) for product, _ in jobs] for _, k, s, t in entries]
        for values, (real, _, s, t) in zip(products, entries):
            for value, (_, place) in zip(values, jobs):
                for piece in range(value.shape[0] // unit):
                    slot = jnp.where(real, place(s, t, piece), trash)
                    acc[slot] += value[piece * unit : (piece + 1) * unit]
        return carry

    lax.fori_loop(0, (n + UNROLL - 1) // UNROLL, step, 0)


class Shares:
    def __init__(self, levels, rdev, tile, parts):
        self.share = rdev // levels
        self.unit = min(tile, self.share)
        self.per = self.share // self.unit
        self.m = levels // 2
        self.parts = parts
        self.tile = tile
        self.pieces = tile // self.unit
        self.slots = 2 * parts * self.m * self.per

    def slot(self, part, block, piece):
        at = block * self.pieces + piece
        owner = at // self.per
        keep = 1 - ((owner ^ lax.axis_index("level")) & 1)
        return ((keep * self.parts + part) * self.m + (owner >> 1)) * self.per + at % self.per


def sides(band):
    odd = band & 1
    return 1 - odd, odd


def heads_out_kernel(count, blocks, rows_hbm, cols_hbm, perm_hbm, x_hbm, vals_hbm, plan, coded, plain, head_x, mine, x, vals, acc, rows, cols, perm, few):
    copies = [
        pltpu.make_async_copy(a, b, few.at[i])
        for i, (a, b) in enumerate(((rows_hbm, rows), (cols_hbm, cols), (perm_hbm, perm), (x_hbm, x), (vals_hbm, vals)))
    ]
    for copy in copies:
        copy.start()
    acc[...] = jnp.zeros_like(acc)
    for copy in copies[:3]:
        copy.wait()
    write_plan(count, blocks, rows, cols, perm, plan)
    copies[3].wait()
    for h in range(HEADB):
        head_x[h] = x[perm[0, 0, h]]
    core = lax.axis_index("level") & 1
    for j in range(blocks // 2):
        mine[j] = x[core * (blocks // 2) + j]
    copies[4].wait()
    target = lambda s, t, piece: t
    for_tiles(count, plan, vals, HEAD_ROW, [(lambda v, s, t: dot(v, x[s]), target)], acc, 2 * HEADB)
    for_tiles(count, plan, vals, HEAD_COL, [(lambda v, s, t: dot_t(v, x[s]), target)], acc, 2 * HEADB)
    for i in range(2 * HEADB):
        plain[i] = acc[i]
        put_coded(coded, i, acc[i])


def receives(step):
    return lax.axis_index("band") % (2 * step) == step


def heads_add_kernel(step, had, came, head_x, head_got, coded, plain, head_out):
    for i in range(had.shape[0]):
        value = had[i] + get_coded(came, i)
        plain[i] = value
        put_coded(coded, i, value)
    head_out[...] = jnp.where(receives(step), head_got[...], head_x[...])


def halo_out_kernel(count, blocks, shares, x, vals, plan, near, send, keep, acc, table):
    acc[...] = jnp.zeros_like(acc)
    for part, side in enumerate(sides(lax.axis_index("band"))):
        for j in range(blocks):
            for piece in range(shares.pieces):
                table[(part * 2 * blocks + j) * shares.pieces + piece] = shares.slot(
                    part, near[side * blocks + j], piece
                )
    near_slot = lambda s, t, piece: table[t * shares.pieces + piece]
    for_tiles(count, plan, vals, NEAR, [(lambda v, s, t: dot_t(v, x[s]), near_slot)], acc, shares.slots)
    half = shares.slots // 2
    send[...] = acc[:half].reshape(send.shape)
    keep[...] = acc[half : 2 * half].reshape(keep.shape)


def own_kernel(count, shares, x, vals, plan, own, acc):
    acc[...] = jnp.zeros_like(acc)
    forward = (lambda v, s, t: dot(v, x[t]), lambda s, t, piece: shares.slot(0, s, piece))
    backward = (lambda v, s, t: dot_t(v, x[s]), lambda s, t, piece: shares.slot(1, t, piece))
    for_tiles(count, plan, vals, OWN, [forward, backward], acc, shares.slots)
    own[...] = acc[: shares.slots]


def remote_kernel(count, blocks, shares, vals, plan, near, own, pair, pair2, other, other2, head_x, head_got, send, keep, acc, xw, table):
    half_blocks = blocks // 2
    core = lax.axis_index("level") & 1
    for j in range(half_blocks):
        for at, (mine, swapped) in enumerate(((pair, pair2), (other, other2))):
            xw[at * blocks + core * half_blocks + j] = mine[j]
            xw[at * blocks + (1 - core) * half_blocks + j] = swapped[j]
    for j in range(HEADB):
        xw[2 * blocks + j] = jnp.where(receives(1), head_got[j], head_x[j])
        table[3 * blocks + j] = 2 * blocks + j
    for part, side in enumerate(sides(lax.axis_index("band"))):
        for j in range(blocks):
            table[part * 2 * blocks + j] = side * blocks + near[side * blocks + j]
    acc[: shares.slots] = own[...]
    forward = (lambda v, s, t: dot(v, xw[table[s]]), lambda s, t, piece: shares.slot(0, t, piece))
    backward = (lambda v, s, t: dot_t(v, xw[2 * blocks + t]), lambda s, t, piece: shares.slot(1, s, piece))
    for_tiles(count, plan, vals, REMOTE, [forward], acc, shares.slots)
    for_tiles(count, plan, vals, HEAD_ROW, [backward], acc, shares.slots)
    half = shares.slots // 2
    send[...] = acc[:half].reshape(send.shape)
    keep[...] = acc[half : 2 * half].reshape(keep.shape)


def heads_in_kernel(shares, perm, send_in, keep_in, had, came, send, keep):
    send[...] = send_in[...]
    keep[...] = keep_in[...]

    @pl.when(lax.axis_index("band") == 0)
    def _():
        half = shares.slots // 2
        for part in range(2):
            for h in range(HEADB):
                value = had[part * HEADB + h] + get_coded(came, part * HEADB + h)
                for piece in range(shares.pieces):
                    slot = shares.slot(part, perm[h], piece)
                    some = value[piece * shares.unit : (piece + 1) * shares.unit]

                    @pl.when(slot < half)
                    def _():
                        send[slot] += some

                    @pl.when(slot >= half)
                    def _():
                        keep[slot - half] += some


def split_kernel(bit, coded_in, had, came, send, keep):
    mine = (lax.axis_index("level") >> bit) & 1
    parts, m, share, width = had.shape
    for part in range(parts):
        for i in range(m // 2):
            for half in range(2):
                j = 2 * i + (mine if half else 1 - mine)
                came_value = get_coded(came, part * m + j) if coded_in else came[part, j]
                value = had[part, j] + came_value
                if half:
                    keep[part, i] = value
                else:
                    put_coded(send, part * (m // 2) + i, value)


def edge_kernel(coded_in, had, came, relayed, direct):
    odd = lax.axis_index("band") & 1
    for side, part in ((0, 1 - odd), (1, odd)):
        came_value = get_coded(came, part) if coded_in else came[part, 0]
        value = had[part, 0] + came_value
        if side:
            put_coded(relayed, 0, value)
        else:
            direct[0] = value


def relay_kernel(direct, came, out):
    put_coded(out, 0, direct[0] + get_coded(came, 0))


def last_kernel(coded_in, had, came, from_near, forward, backward):
    came_values = [get_coded(came, part) if coded_in else came[part, 0] for part in range(2)]
    forward[0] = (had[0, 0] + came_values[0]).astype(forward.dtype)
    backward[0] = (had[1, 0] + came_values[1] + get_coded(from_near, 0)).astype(backward.dtype)


def over_levels(send, keep, levels, after=()):
    bit, coded = 0, False
    parts, m, share, width = keep.shape
    while True:
        pairs = [(i, i ^ (1 << bit)) for i in range(levels)]
        came = lax.ppermute(send, "level", pairs)
        if m == 1:
            return keep, came, coded
        bit += 1
        send, keep = call(
            functools.partial(split_kernel, bit, coded),
            (array((parts * (m // 2), share + GROUPS, width), I16), array((parts, m // 2, share, width))),
            (keep, came),
            after=after,
        )
        coded = True
        m //= 2


def on_device(features, block_perm, tile_rows, tile_cols, tile_vals):
    rdev, width = features.shape
    blocks = block_perm.shape[2]
    tile = tile_vals.shape[2]
    count = tile_vals.shape[1]
    levels = lax.axis_size("level")
    bands = lax.axis_size("band")
    band = lax.axis_index("band")
    cores = [(i, i ^ 1) for i in range(levels)]
    pairs = [(i, i ^ 1) for i in range(bands)]
    outward = [(i, i + 2 if i % 2 else i - 2) for i in range(bands)]
    outward = [(i, j) for i, j in outward if 0 <= j < bands]
    inward = [(j, i) for i, j in outward]
    shares = Shares(levels, rdev, tile, 2)
    share, m, unit = shares.share, shares.m, shares.unit

    perm = block_perm[0, 0]
    vals = tile_vals[0]
    x = features.reshape(blocks, tile, width)
    pair_perm = lax.ppermute(perm, "band", pairs)
    other_perm = lax.ppermute(pair_perm, "band", inward)
    near = jnp.concatenate([pair_perm, other_perm])

    coded_heads = array((2 * HEADB, tile + GROUPS, width), I16)
    plain_heads = array((2 * HEADB, tile, width))
    in_hbm = lambda a: pltpu.with_memory_space_constraint(a, pltpu.HBM)
    plan, coded, heads, xh, mine, x, vals = call(
        functools.partial(heads_out_kernel, count, blocks),
        (
            array((5 * count + 5,), jnp.int32),
            coded_heads,
            plain_heads,
            array((HEADB, tile, width), x.dtype),
            array((blocks // 2, tile, width), x.dtype),
            pltpu.VMEM(x.shape, x.dtype),
            pltpu.VMEM(vals.shape, vals.dtype),
        ),
        tuple(in_hbm(a) for a in (tile_rows, tile_cols, block_perm, x, vals)),
        (
            pltpu.VMEM((2 * HEADB + 1, tile, width), F32),
            pltpu.SMEM(tile_rows.shape, jnp.int32),
            pltpu.SMEM(tile_cols.shape, jnp.int32),
            pltpu.SMEM(block_perm.shape, jnp.int32),
            pltpu.SemaphoreType.DMA((5,)),
        ),
        in_hbm=5,
        after=(pair_perm,),
    )
    x, vals = (pltpu.with_memory_space_constraint(a, pltpu.VMEM) for a in (x, vals))

    pair_x = lax.ppermute(mine, "band", pairs)
    other_x = lax.ppermute(pair_x, "band", inward)
    pair_x2 = lax.ppermute(pair_x, "level", cores)
    other_x2 = lax.ppermute(other_x, "level", cores)

    half_shape = array((2, m, share, width))
    halo_out = functools.partial(
        call,
        functools.partial(halo_out_kernel, count, blocks, shares),
        (half_shape, half_shape),
        (x, vals, plan, near),
        (
            pltpu.VMEM((shares.slots + 1, unit, width), F32),
            pltpu.SMEM((3 * blocks * shares.pieces,), jnp.int32),
        ),
    )
    own = call(
        functools.partial(own_kernel, count, shares),
        (array((shares.slots, unit, width)),),
        (x, vals, plan),
        (pltpu.VMEM((shares.slots + 1, unit, width), F32),),
    )[0]

    order = [1 << i for i in range(1, bands.bit_length() - 1)] + [1]
    fences = [(near, pair_x), (other_x,)] + [()] * bands
    done = 0
    for at, bit in enumerate(order):
        step = bands >> (at + 1)
        senders = [i for i in range(bands) if i & bit and not i & done]
        done |= bit
        came = lax.ppermute(coded, "band", [(i, i - bit) for i in senders])
        got = lax.ppermute(xh, "band", [(i, i + step) for i in range(0, bands, 2 * step)])
        if at == 1:
            halo_send, halo_keep = halo_out(after=(coded,))
            halo = over_levels(halo_send, halo_keep, levels)
            fences[1] += (halo_send, own)
        if bit != order[-1]:
            coded, heads, xh = call(
                functools.partial(heads_add_kernel, step),
                (coded_heads, plain_heads, array(xh.shape, xh.dtype)),
                (heads, came, xh, got),
                after=fences[at],
            )

    halo_had, halo_came, halo_coded = halo
    relayed, direct = call(
        functools.partial(edge_kernel, halo_coded),
        (array((1, share + GROUPS, width), I16), array((1, share, width))),
        (halo_had, halo_came),
    )
    relayed = lax.ppermute(relayed, "band", outward)
    to_pair = call(relay_kernel, (array((1, share + GROUPS, width), I16),), (direct, relayed))[0]
    from_near = lax.ppermute(to_pair, "band", pairs)

    send, keep = call(
        functools.partial(remote_kernel, count, blocks, shares),
        (half_shape, half_shape),
        (vals, plan, near, own, pair_x, pair_x2, other_x, other_x2, xh, got),
        (
            pltpu.VMEM((shares.slots + 1, unit, width), F32),
            pltpu.VMEM((2 * blocks + HEADB, tile, width), features.dtype),
            pltpu.SMEM((3 * blocks + HEADB,), jnp.int32),
        ),
        after=(relayed,),
    )
    flat = array((shares.slots // 2, unit, width))
    send, keep = call(
        functools.partial(heads_in_kernel, shares),
        (flat, flat),
        (perm, send.reshape(flat.shape), keep.reshape(flat.shape), heads, came),
        after=(to_pair,),
    )
    had, came, was_coded = over_levels(send.reshape(half_shape.shape), keep.reshape(half_shape.shape), levels)
    out = array((1, share, width), jnp.bfloat16)
    forward, backward = call(functools.partial(last_kernel, was_coded), (out, out), (had, came, from_near))
    return forward, backward


def solution(mesh):
    return jax.shard_map(
        on_device,
        mesh=mesh,
        in_specs=(
            P("band", None),
            P("level", "band", None),
            P("level", "band"),
            P("level", "band"),
            P("level", "band", None, None),
        ),
        out_specs=(P("band", "level", None), P("band", "level", None)),
        check_vma=False,
    )
```

time: 303 us -> 66.9 us (0.22)
  waiting for transfers between devices: 148 us -> 11.8 us
  blocking collectives: 40.7 us -> 0 us
  other arithmetic: 38.6 us -> 0.07 us
  local copies, waits for them, and re-layouts: 36.1 us -> 0.01 us
  starting transfers between devices: 12.2 us -> 39.1 us
  Pallas kernels: 0 us -> 13.9 us
  between operations: 14.3 us -> 0.86 us
  matrix products: 11.6 us -> 0 us
    psum x2 -> x0, waiting for transfers between devices: 148 us -> none  [the longest x1 75.4 us: on_device(): head_fwd, head_bwd = lax.psum((fwd_head, bwd_window[3 * blocks:]), 'band')]
    psum x1 -> x0, blocking collectives: 40.7 us -> none  [on_device(): fwd_all, bwd_all = lax.psum((fwd_global, bwd_global), 'level')]
    ppermute x4 -> x18, starting transfers between devices: 12.2 us -> 39.1 us  [the longest x3 14.2 us: on_device(): lax.ppermute(xh, 'band', [(i, i + step) for i in range(0, bands, 2 * step)])]
    scatter-add x2 -> x0, other arithmetic: 22.9 us -> none  [the longest x1 14.1 us: on_device(): jax.ops.segment_sum(prod_bwd, col_slot, num_segments=window_len)]
    pallas_call x0 -> x12, Pallas kernels: none -> 13.9 us  [call(): pl.pallas_call(body, out_shape=outs, in_specs=[HBM] * in_hbm + [SMEM if a...]
    dot_general x2 -> x0, local copies, waits for them, and re-layouts: 12.2 us -> none  [the longest x1 6.13 us: on_device(): jnp.einsum('kij,kjf->kif', vals, by_col, preferred_element_type=jnp.float32)]
    ppermute x4 -> x18, waiting for transfers between devices: 0.01 us -> 11.8 us  [the longest x1 3.6 us: on_device(): from_near = lax.ppermute(to_pair, 'band', pairs)]
    dot_general x2 -> x0, matrix products: 11.6 us -> none  [the longest x1 6.14 us: on_device(): jnp.einsum('kij,kjf->kif', vals, by_col, preferred_element_type=jnp.float32)]
  transfers between devices with their start and end apart: 6 -> 18, of which waited for: 2 -> 6; matrix products, arithmetic and copies ran while one was open for 10% -> 0% of each run, Pallas kernels for 0% -> 11%
where the time goes in v2:
time: 66.9 us; the launch traced here: 65.8 us
  starting transfers between devices  39.1 us (58%)
  Pallas kernels  13.9 us (21%)
  waiting for transfers between devices  11.8 us (18%)
  between operations  0.86 us (1%)
    ppermute x3, starting transfers between devices, on_device(): lax.ppermute(xh, 'band', [(i, i + step) for i in range(0, bands, 2 * step)])  14.2 us
    pallas_call x12, Pallas kernels, call(): pl.pallas_call(body, out_shape=outs, in_specs=[HBM] * in_hbm + [SMEM if a...  13.9 us
    ppermute x1, starting transfers between devices, on_device(): other_x = lax.ppermute(pair_x, 'band', inward)  4.69 us
    ppermute x1, starting transfers between devices, on_device(): from_near = lax.ppermute(to_pair, 'band', pairs)  4.23 us
    ppermute x3, starting transfers between devices, on_device(): came = lax.ppermute(coded, 'band', [(i, i - bit) for i in senders])  3.88 us
    ppermute x1, waiting for transfers between devices, on_device(): from_near = lax.ppermute(to_pair, 'band', pairs)  3.6 us
    ppermute x4, starting transfers between devices, over_levels(): came = lax.ppermute(send, 'level', pairs)  3.26 us
    ppermute x1, starting transfers between devices, on_device(): pair_perm = lax.ppermute(perm, 'band', pairs)  3.03 us
  transfers between devices with their start and end apart: 18, of which 6 were waited for; matrix products, arithmetic and copies ran while one was open for 0% of the time, Pallas kernels for 11%

profile of v2, /device:TPU:0, one launch (start us, length us, event | category | flops | bytes accessed | tf_op | source)
XLA Modules:
  0.0 65.8 jit_solution(10816432628211794443)
XLA Ops:
  0.6 3.0 %collective-permute-start = (s32[8]{0:T(128)}, s32[8]{0:T(128)S(1)}, u32[]{:S(2)}, u32[]{:S(2)}) collective-permute-start(s32[8]{0:T(128)} %bitcast.10), channel_id=1, source_target_pairs={{0,1},{1,0},{2,3},{3,2},{4,5},{5,4},{6,7},{7,6},{8,9},{9,8},{10,11... | collective-permute-start | bytes 104 | tf_op jit(solution)/shard_map/ppermute | solution.py:333
  3.7 1.7 %collective-permute-done.refs_5_ = s32[8]{0:T(128)S(1)} collective-permute-done((s32[8]{0:T(128)}, s32[8]{0:T(128)S(1)}, u32[]{:S(2)}, u32[]{:S(2)}) %collective-permute-start) | collective-permute-done | bytes 64 | tf_op jit(solution)/shard_map/ppermute | solution.py:333
  5.3 3.2 %shard_map.68 = (s32[185]{0:T(256)S(1)}, s16[4,272,128]{2,1,0:T(8,128)(2,1)S(1)}, f32[4,256,128]{2,1,0:T(8,128)S(1)}, bf16[2,256,128]{2,1,0:T(8,128)(2,1)S(1)}, ...) custom-call(s32[1,36]{1,0:T(1,128)} %refs_0_.1, ...), custom_call_target="tpu_custom_call" | custom-call | bytes 11682852 | tf_op jit(solution)/shard_map/pallas_call | solution.py:29
  8.5 1.3 %collective-permute-start.6 = (s16[4,272,128]{2,1,0:T(8,128)(2,1)S(1)}, s16[4,272,128]{2,1,0:T(8,128)(2,1)S(1)}, u32[]{:S(2)}, u32[]{:S(2)}) collective-permute-start(s16[4,272,128]{2,1,0:T(8,128)(2,1)S(1)} %get-tuple-element.32), channel_id=1, source_target_pairs={{2,0},{3,1},{6,4},{7,5},{10,8},{11,9},{14,12},{15,13},{18,16},{19,... | collective-permute-start | bytes 835592 | tf_op jit(solution)/shard_map/ppermute | solution.py:394
  9.8 2.7 %collective-permute-start.2 = (bf16[4,256,128]{2,1,0:T(8,128)(2,1)S(1)}, bf16[4,256,128]{2,1,0:T(8,128)(2,1)S(1)}, u32[]{:S(2)}, u32[]{:S(2)}) collective-permute-start(bf16[4,256,128]{2,1,0:T(8,128)(2,1)S(1)} %get-tuple-element.30), channel_id=1, source_target_pairs={{0,1},{1,0},{2,3},{3,2},{4,5},{5,4},{6,7},{7,6},{8,9},{9,8},{10,11... | collective-permute-start | bytes 786440 | tf_op jit(solution)/shard_map/ppermute | solution.py:364
  12.5 5.2 %collective-permute-start.7 = (bf16[2,256,128]{2,1,0:T(8,128)(2,1)S(1)}, bf16[2,256,128]{2,1,0:T(8,128)(2,1)S(1)}, u32[]{:S(2)}, u32[]{:S(2)}) collective-permute-start(bf16[2,256,128]{2,1,0:T(8,128)(2,1)S(1)} %get-tuple-element.33.refs_2_), channel_id=1, source_target_pairs={{0,4},{8,12},{16,20},{24,28}} | collective-permute-start | bytes 393224 | tf_op jit(solution)/shard_map/ppermute | solution.py:395
  17.7 1.3 %collective-permute-start.1 = (s32[8]{0:T(128)S(1)}, s32[8]{0:T(128)S(1)}, u32[]{:S(2)}, u32[]{:S(2)}) collective-permute-start(s32[8]{0:T(128)S(1)} %collective-permute-done.refs_5_), channel_id=1, source_target_pairs={{3,1},{0,2},{5,3},{2,4},{7,5},{4,6},{11,9},{8,10},{13,11},{10,12},... | collective-permute-start | bytes 104 | tf_op jit(solution)/shard_map/ppermute | solution.py:334
  19.0 1.3 %collective-permute-done.1 = s32[8]{0:T(128)S(1)} collective-permute-done((s32[8]{0:T(128)S(1)}, s32[8]{0:T(128)S(1)}, u32[]{:S(2)}, u32[]{:S(2)}) %collective-permute-start.1) | collective-permute-done | bytes 64 | tf_op jit(solution)/shard_map/ppermute | solution.py:334
  20.3 0.1 pad_add_fusion.refs_4_.refs_3_.refs_2_
  20.3 0.0 collective-permute-done.7.refs_3_
  20.3 0.0 collective-permute-done.2.refs_5_.refs_4_
  20.3 0.0 collective-permute-done.6.refs_1_
  20.3 0.3 shard_map.70
  20.7 1.5 %shard_map.71 = (f32[2,2,512,128]{3,2,1,0:T(8,128)S(1)}, f32[2,2,512,128]{3,2,1,0:T(8,128)S(1)}) custom-call(bf16[8,256,128]{2,1,0:T(8,128)(2,1)S(1)} %get-tuple-element.29.refs_0_, bf16[36,256,256]{2,1,0:T(8,128)(2,1)S(1)} %get-tuple-element.27.refs_1_.refs_0_, s32[185]{0:T(256)S(1)} %get-tuple-element.28.refs_2_.refs_1_, ...), custom_call_target="tpu_custom_call" | custom-call | bytes 7340836 | tf_op jit(solution)/shard_map/pallas_call | solution.py:29
  22.2 0.1 collective-permute-start.11
  22.3 1.3 %collective-permute-start.8 = (s16[4,272,128]{2,1,0:T(8,128)(2,1)S(1)}, s16[4,272,128]{2,1,0:T(8,128)(2,1)S(1)}, u32[]{:S(2)}, u32[]{:S(2)}) collective-permute-start(s16[4,272,128]{2,1,0:T(8,128)(2,1)S(1)} %get-tuple-element.35.refs_4_), channel_id=1, source_target_pairs={{4,0},{5,1},{12,8},{13,9},{20,16},{21,17},{28,24},{29,25}} | collective-permute-start | bytes 835592 | tf_op jit(solution)/shard_map/ppermute | solution.py:394
  23.6 4.7 %collective-permute-start.4 = (bf16[4,256,128]{2,1,0:T(8,128)(2,1)S(1)}, bf16[4,256,128]{2,1,0:T(8,128)(2,1)S(1)}, u32[]{:S(2)}, u32[]{:S(2)}) collective-permute-start(bf16[4,256,128]{2,1,0:T(8,128)(2,1)S(1)} %collective-permute-done.2.refs_5_.refs_4_), channel_id=1, source_target_pairs={{3,1},{0,2},{5,3},{2,4},{7,5},{4,6},{11,9},{8,10},{13,11},{10,12},... | collective-permute-start | bytes 786440 | tf_op jit(solution)/shard_map/ppermute | solution.py:365
  28.3 3.6 %collective-permute-start.9 = (bf16[2,256,128]{2,1,0:T(8,128)(2,1)S(1)}, bf16[2,256,128]{2,1,0:T(8,128)(2,1)S(1)}, u32[]{:S(2)}, u32[]{:S(2)}) collective-permute-start(bf16[2,256,128]{2,1,0:T(8,128)(2,1)S(1)} %get-tuple-element.36.refs_2_), channel_id=1, source_target_pairs={{0,2},{4,6},{8,10},{12,14},{16,18},{20,22},{24,26},{28,30}} | collective-permute-start | bytes 393224 | tf_op jit(solution)/shard_map/ppermute | solution.py:395
  31.9 0.0 collective-permute-done.11.refs_1_
  31.9 0.3 shard_map.73
  32.2 1.6 %collective-permute-start.12 = (s16[2,528,128]{2,1,0:T(8,128)(2,1)S(1)}, s16[2,528,128]{2,1,0:T(8,128)(2,1)S(1)}, u32[]{:S(2)}, u32[]{:S(2)}) collective-permute-start(s16[2,528,128]{2,1,0:T(8,128)(2,1)S(1)} %get-tuple-element.41), channel_id=1, source_target_pairs={{0,16},{8,24},{16,0},{24,8},{1,17},{9,25},{17,1},{25,9},{2,18},{10... | collective-permute-start | bytes 811016 | tf_op jit(solution)/shard_map/ppermute | solution.py:300
  33.7 4.5 %shard_map.69.refs_6_.refs_3_ = f32[16,256,128]{2,1,0:T(8,128)S(1)} custom-call(bf16[8,256,128]{2,1,0:T(8,128)(2,1)S(1)} %get-tuple-element.29.refs_0_, bf16[36,256,256]{2,1,0:T(8,128)(2,1)S(1)} %get-tuple-element.27.refs_1_.refs_0_, s32[185]{0:T(256)S(1)} %get-tuple-element.28.refs_2_.refs_1_), custom_call_target="tpu_custom_call" | custom-call | bytes 7340772 | tf_op jit(solution)/shard_map/pallas_call | solution.py:29
  38.3 0.0 collective-permute-done.9.refs_3_
  38.3 0.0 collective-permute-done.4.refs_4_.refs_6_
  38.3 0.0 collective-permute-done.8.refs_1_
  38.3 0.3 shard_map.72
  38.6 1.3 %collective-permute-start.14 = (s16[4,272,128]{2,1,0:T(8,128)(2,1)S(1)}, s16[4,272,128]{2,1,0:T(8,128)(2,1)S(1)}, u32[]{:S(2)}, u32[]{:S(2)}) collective-permute-start(s16[4,272,128]{2,1,0:T(8,128)(2,1)S(1)} %get-tuple-element.46), channel_id=1, source_target_pairs={{1,0},{9,8},{17,16},{25,24}} | collective-permute-start | bytes 835592 | tf_op jit(solution)/shard_map/ppermute | solution.py:394
  39.9 0.1 collective-permute-start.3
  40.0 0.5 collective-permute-start.5
  40.5 0.0 collective-permute-done.12.refs_1_
  40.5 0.0 copy-start
  40.5 0.2 shard_map.74
  40.7 1.3 %collective-permute-start.13 = (s16[1,528,128]{2,1,0:T(8,128)(2,1)S(1)}, s16[1,528,128]{2,1,0:T(8,128)(2,1)S(1)}, u32[]{:S(2)}, u32[]{:S(2)}) collective-permute-start(s16[1,528,128]{2,1,0:T(8,128)(2,1)S(1)} %get-tuple-element.42), channel_id=1, source_target_pairs={{1,3},{2,0},{3,5},{4,2},{5,7},{6,4},{9,11},{10,8},{11,13},{12,10},... | collective-permute-start | bytes 405512 | tf_op jit(solution)/shard_map/ppermute | solution.py:414
  42.0 5.4 %collective-permute-start.10 = (bf16[2,256,128]{2,1,0:T(8,128)(2,1)S(1)}, bf16[2,256,128]{2,1,0:T(8,128)(2,1)S(1)}, u32[]{:S(2)}, u32[]{:S(2)}) collective-permute-start(bf16[2,256,128]{2,1,0:T(8,128)(2,1)S(1)} %get-tuple-element.38.refs_8_), channel_id=1, source_target_pairs={{0,1},{2,3},{4,5},{6,7},{8,9},{10,11},{12,13},{14,15},{16,17},{18,... | collective-permute-start | bytes 393224 | tf_op jit(solution)/shard_map/ppermute | solution.py:395
  47.5 0.7 %collective-permute-done.13.refs_10_.refs_1_ = s16[1,528,128]{2,1,0:T(8,128)(2,1)S(1)} collective-permute-done((s16[1,528,128]{2,1,0:T(8,128)(2,1)S(1)}, s16[1,528,128]{2,1,0:T(8,128)(2,1)S(1)}, u32[]{:S(2)}, u32[]{:S(2)}) %collective-permute-start.13) | collective-permute-done | bytes 135200 | tf_op jit(solution)/shard_map/ppermute | solution.py:414
  48.2 0.1 shard_map.76.refs_5_
  48.3 0.0 collective-permute-done.3.refs_5_
  48.3 1.8 %collective-permute-done.10.refs_9_ = bf16[2,256,128]{2,1,0:T(8,128)(2,1)S(1)} collective-permute-done((bf16[2,256,128]{2,1,0:T(8,128)(2,1)S(1)}, bf16[2,256,128]{2,1,0:T(8,128)(2,1)S(1)}, u32[]{:S(2)}, u32[]{:S(2)}) %collective-permute-start.10) | collective-permute-done | bytes 131104 | tf_op jit(solution)/shard_map/ppermute | solution.py:395
  50.2 0.0 collective-permute-done.5.refs_7_
  50.2 1.6 %shard_map.75 = (f32[2,2,512,128]{3,2,1,0:T(8,128)S(1)}, f32[2,2,512,128]{3,2,1,0:T(8,128)S(1)}) custom-call(bf16[36,256,256]{2,1,0:T(8,128)(2,1)S(1)} %get-tuple-element.27.refs_1_.refs_0_, s32[185]{0:T(256)S(1)} %get-tuple-element.28.refs_2_.refs_1_, s32[16]{0:T(128)S(1)} %pad_add_fusion.refs_4_.refs_3_.refs_2_, ...), custom_call_target="tpu_custom_call" | custom-call | bytes 10224420 | tf_op jit(solution)/shard_map/pallas_call | solution.py:29
  51.7 0.0 collective-permute-done.14.refs_4_
  51.7 0.0 copy-done
  51.8 0.8 %shard_map.77 = (f32[8,256,128]{2,1,0:T(8,128)S(1)}, f32[8,256,128]{2,1,0:T(8,128)S(1)}) custom-call(s32[8]{0:T(128)S(1)} %bitcast.11, f32[8,256,128]{2,1,0:T(8,128)S(1)} %bitcast.7, f32[8,256,128]{2,1,0:T(8,128)S(1)} %bitcast.8, f32[4,256,128]{2,1,0:T(8,128)S(1)} %get-tuple-element.45.refs_3_, s16[4,272,128]{2,1,0:T(8,128)(2,1)S(1)} %collective-permute-done.14.refs_4_, ...), custom_call_target="tpu_custom_call" | custom-call | bytes 4997152 | tf_op jit(solution)/shard_map/pallas_call | solution.py:29
  52.6 0.1 collective-permute-start.15
  52.7 2.6 %collective-permute-done.15.refs_1_ = f32[2,2,512,128]{3,2,1,0:T(8,128)S(1)} collective-permute-done((f32[2,2,512,128]{3,2,1,0:T(8,128)S(1)}, f32[2,2,512,128]{3,2,1,0:T(8,128)S(1)}, u32[]{:S(2)}, u32[]{:S(2)}) %collective-permute-start.15) | collective-permute-done | bytes 1048608 | tf_op jit(solution)/shard_map/ppermute | solution.py:300
  55.3 0.3 shard_map.78
  55.6 1.6 %collective-permute-start.16 = (s16[2,528,128]{2,1,0:T(8,128)(2,1)S(1)}, s16[2,528,128]{2,1,0:T(8,128)(2,1)S(1)}, u32[]{:S(2)}, u32[]{:S(2)}) collective-permute-start(s16[2,528,128]{2,1,0:T(8,128)(2,1)S(1)} %get-tuple-element.51), channel_id=1, source_target_pairs={{0,16},{8,24},{16,0},{24,8},{1,17},{9,25},{17,1},{25,9},{2,18},{10... | collective-permute-start | bytes 811016 | tf_op jit(solution)/shard_map/ppermute | solution.py:300
  57.1 4.2 %collective-permute-start.17 = (s16[1,528,128]{2,1,0:T(8,128)(2,1)S(1)}, s16[1,528,128]{2,1,0:T(8,128)(2,1)S(1)}, u32[]{:S(2)}, u32[]{:S(2)}) collective-permute-start(s16[1,528,128]{2,1,0:T(8,128)(2,1)S(1)} %shard_map.76.refs_5_), channel_id=1, source_target_pairs={{0,1},{1,0},{2,3},{3,2},{4,5},{5,4},{6,7},{7,6},{8,9},{9,8},{10,11... | collective-permute-start | bytes 405512 | tf_op jit(solution)/shard_map/ppermute | solution.py:416
  61.4 3.6 %collective-permute-done.17.refs_2_ = s16[1,528,128]{2,1,0:T(8,128)(2,1)S(1)} collective-permute-done((s16[1,528,128]{2,1,0:T(8,128)(2,1)S(1)}, s16[1,528,128]{2,1,0:T(8,128)(2,1)S(1)}, u32[]{:S(2)}, u32[]{:S(2)}) %collective-permute-start.17) | collective-permute-done | bytes 135200 | tf_op jit(solution)/shard_map/ppermute | solution.py:416
  65.0 0.0 collective-permute-done.16.refs_1_
  65.0 0.8 %shard_map.79 = (bf16[1,512,128]{2,1,0:T(8,128)(2,1)}, bf16[1,512,128]{2,1,0:T(8,128)(2,1)}) custom-call(f32[2,1,512,128]{3,2,1,0:T(8,128)S(1)} %get-tuple-element.50.refs_0_, s16[2,528,128]{2,1,0:T(8,128)(2,1)S(1)} %collective-permute-done.16.refs_1_, s16[1,528,128]{2,1,0:T(8,128)(2,1)S(1)} %collective-permute-done.17.refs_2_), custom_call_target="tpu_custom_call" | custom-call | bytes 1191936 | tf_op jit(solution)/shard_map/pallas_call | solution.py:29
Async XLA Ops:
  0.6 4.7 %collective-permute-start = (s32[8]{0:T(128)}, s32[8]{0:T(128)S(1)}, u32[]{:S(2)}, u32[]{:S(2)}) collective-permute-start(s32[8]{0:T(128)} %bitcast.10), channel_id=1, source_target_pairs={{0,1},{1,0},{2,3},{3,2},{4,5},{5,4},{6,7},{7,6},{8,9},{9,8},{10,11... | collective-permute-start | bytes 104 | tf_op jit(solution)/shard_map/ppermute | solution.py:333
  8.5 11.9 %collective-permute-start.6 = (s16[4,272,128]{2,1,0:T(8,128)(2,1)S(1)}, s16[4,272,128]{2,1,0:T(8,128)(2,1)S(1)}, u32[]{:S(2)}, u32[]{:S(2)}) collective-permute-start(s16[4,272,128]{2,1,0:T(8,128)(2,1)S(1)} %get-tuple-element.32), channel_id=1, source_target_pairs={{2,0},{3,1},{6,4},{7,5},{10,8},{11,9},{14,12},{15,13},{18,16},{19,... | collective-permute-start | bytes 835592 | tf_op jit(solution)/shard_map/ppermute | solution.py:394
  9.8 10.5 %collective-permute-start.2 = (bf16[4,256,128]{2,1,0:T(8,128)(2,1)S(1)}, bf16[4,256,128]{2,1,0:T(8,128)(2,1)S(1)}, u32[]{:S(2)}, u32[]{:S(2)}) collective-permute-start(bf16[4,256,128]{2,1,0:T(8,128)(2,1)S(1)} %get-tuple-element.30), channel_id=1, source_target_pairs={{0,1},{1,0},{2,3},{3,2},{4,5},{5,4},{6,7},{7,6},{8,9},{9,8},{10,11... | collective-permute-start | bytes 786440 | tf_op jit(solution)/shard_map/ppermute | solution.py:364
  12.5 7.8 %collective-permute-start.7 = (bf16[2,256,128]{2,1,0:T(8,128)(2,1)S(1)}, bf16[2,256,128]{2,1,0:T(8,128)(2,1)S(1)}, u32[]{:S(2)}, u32[]{:S(2)}) collective-permute-start(bf16[2,256,128]{2,1,0:T(8,128)(2,1)S(1)} %get-tuple-element.33.refs_2_), channel_id=1, source_target_pairs={{0,4},{8,12},{16,20},{24,28}} | collective-permute-start | bytes 393224 | tf_op jit(solution)/shard_map/ppermute | solution.py:395
  17.7 2.6 %collective-permute-start.1 = (s32[8]{0:T(128)S(1)}, s32[8]{0:T(128)S(1)}, u32[]{:S(2)}, u32[]{:S(2)}) collective-permute-start(s32[8]{0:T(128)S(1)} %collective-permute-done.refs_5_), channel_id=1, source_target_pairs={{3,1},{0,2},{5,3},{2,4},{7,5},{4,6},{11,9},{8,10},{13,11},{10,12},... | collective-permute-start | bytes 104 | tf_op jit(solution)/shard_map/ppermute | solution.py:334
  22.2 9.7 %collective-permute-start.11 = (f32[2,2,512,128]{3,2,1,0:T(8,128)S(1)}, f32[2,2,512,128]{3,2,1,0:T(8,128)S(1)}, u32[]{:S(2)}, u32[]{:S(2)}) collective-permute-start(f32[2,2,512,128]{3,2,1,0:T(8,128)S(1)} %get-tuple-element.37.refs_5_), channel_id=1, source_target_pairs={{0,8},{8,0},{16,24},{24,16},{1,9},{9,1},{17,25},{25,17},{2,10},{10... | collective-permute-start | bytes 3145736 | tf_op jit(solution)/shard_map/ppermute | solution.py:300
  22.3 16.0 %collective-permute-start.8 = (s16[4,272,128]{2,1,0:T(8,128)(2,1)S(1)}, s16[4,272,128]{2,1,0:T(8,128)(2,1)S(1)}, u32[]{:S(2)}, u32[]{:S(2)}) collective-permute-start(s16[4,272,128]{2,1,0:T(8,128)(2,1)S(1)} %get-tuple-element.35.refs_4_), channel_id=1, source_target_pairs={{4,0},{5,1},{12,8},{13,9},{20,16},{21,17},{28,24},{29,25}} | collective-permute-start | bytes 835592 | tf_op jit(solution)/shard_map/ppermute | solution.py:394
  23.6 14.7 %collective-permute-start.4 = (bf16[4,256,128]{2,1,0:T(8,128)(2,1)S(1)}, bf16[4,256,128]{2,1,0:T(8,128)(2,1)S(1)}, u32[]{:S(2)}, u32[]{:S(2)}) collective-permute-start(bf16[4,256,128]{2,1,0:T(8,128)(2,1)S(1)} %collective-permute-done.2.refs_5_.refs_4_), channel_id=1, source_target_pairs={{3,1},{0,2},{5,3},{2,4},{7,5},{4,6},{11,9},{8,10},{13,11},{10,12},... | collective-permute-start | bytes 786440 | tf_op jit(solution)/shard_map/ppermute | solution.py:365
  28.3 10.0 %collective-permute-start.9 = (bf16[2,256,128]{2,1,0:T(8,128)(2,1)S(1)}, bf16[2,256,128]{2,1,0:T(8,128)(2,1)S(1)}, u32[]{:S(2)}, u32[]{:S(2)}) collective-permute-start(bf16[2,256,128]{2,1,0:T(8,128)(2,1)S(1)} %get-tuple-element.36.refs_2_), channel_id=1, source_target_pairs={{0,2},{4,6},{8,10},{12,14},{16,18},{20,22},{24,26},{28,30}} | collective-permute-start | bytes 393224 | tf_op jit(solution)/shard_map/ppermute | solution.py:395
  32.2 8.4 %collective-permute-start.12 = (s16[2,528,128]{2,1,0:T(8,128)(2,1)S(1)}, s16[2,528,128]{2,1,0:T(8,128)(2,1)S(1)}, u32[]{:S(2)}, u32[]{:S(2)}) collective-permute-start(s16[2,528,128]{2,1,0:T(8,128)(2,1)S(1)} %get-tuple-element.41), channel_id=1, source_target_pairs={{0,16},{8,24},{16,0},{24,8},{1,17},{9,25},{17,1},{25,9},{2,18},{10... | collective-permute-start | bytes 811016 | tf_op jit(solution)/shard_map/ppermute | solution.py:300
  38.6 13.1 %collective-permute-start.14 = (s16[4,272,128]{2,1,0:T(8,128)(2,1)S(1)}, s16[4,272,128]{2,1,0:T(8,128)(2,1)S(1)}, u32[]{:S(2)}, u32[]{:S(2)}) collective-permute-start(s16[4,272,128]{2,1,0:T(8,128)(2,1)S(1)} %get-tuple-element.46), channel_id=1, source_target_pairs={{1,0},{9,8},{17,16},{25,24}} | collective-permute-start | bytes 835592 | tf_op jit(solution)/shard_map/ppermute | solution.py:394
  39.9 8.4 %collective-permute-start.3 = (bf16[4,256,128]{2,1,0:T(8,128)(2,1)S(1)}, bf16[4,256,128]{2,1,0:T(8,128)(2,1)S(1)}, u32[]{:S(2)}, u32[]{:S(2)}) collective-permute-start(bf16[4,256,128]{2,1,0:T(8,128)(2,1)S(1)} %collective-permute-done.2.refs_5_.refs_4_), channel_id=1, source_target_pairs={{0,8},{8,0},{16,24},{24,16},{1,9},{9,1},{17,25},{25,17},{2,10},{10... | collective-permute-start | bytes 786440 | tf_op jit(solution)/shard_map/ppermute | solution.py:366
  40.0 10.1 %collective-permute-start.5 = (bf16[4,256,128]{2,1,0:T(8,128)(2,1)S(1)}, bf16[4,256,128]{2,1,0:T(8,128)(2,1)S(1)}, u32[]{:S(2)}, u32[]{:S(2)}) collective-permute-start(bf16[4,256,128]{2,1,0:T(8,128)(2,1)S(1)} %collective-permute-done.4.refs_4_.refs_6_), channel_id=1, source_target_pairs={{0,8},{8,0},{16,24},{24,16},{1,9},{9,1},{17,25},{25,17},{2,10},{10... | collective-permute-start | bytes 786440 | tf_op jit(solution)/shard_map/ppermute | solution.py:367
  40.5 11.2 %copy-start = (s32[1,1,8]{2,1,0:T(1,128)S(1)}, s32[1,1,8]{2,1,0:T(1,128)}, u32[]{:S(2)}) copy-start(s32[1,1,8]{2,1,0:T(1,128)} %refs_2_.1) | copy-start | bytes 100
  40.7 7.4 %collective-permute-start.13 = (s16[1,528,128]{2,1,0:T(8,128)(2,1)S(1)}, s16[1,528,128]{2,1,0:T(8,128)(2,1)S(1)}, u32[]{:S(2)}, u32[]{:S(2)}) collective-permute-start(s16[1,528,128]{2,1,0:T(8,128)(2,1)S(1)} %get-tuple-element.42), channel_id=1, source_target_pairs={{1,3},{2,0},{3,5},{4,2},{5,7},{6,4},{9,11},{10,8},{11,13},{12,10},... | collective-permute-start | bytes 405512 | tf_op jit(solution)/shard_map/ppermute | solution.py:414
  42.0 8.1 %collective-permute-start.10 = (bf16[2,256,128]{2,1,0:T(8,128)(2,1)S(1)}, bf16[2,256,128]{2,1,0:T(8,128)(2,1)S(1)}, u32[]{:S(2)}, u32[]{:S(2)}) collective-permute-start(bf16[2,256,128]{2,1,0:T(8,128)(2,1)S(1)} %get-tuple-element.38.refs_8_), channel_id=1, source_target_pairs={{0,1},{2,3},{4,5},{6,7},{8,9},{10,11},{12,13},{14,15},{16,17},{18,... | collective-permute-start | bytes 393224 | tf_op jit(solution)/shard_map/ppermute | solution.py:395
  52.6 2.7 %collective-permute-start.15 = (f32[2,2,512,128]{3,2,1,0:T(8,128)S(1)}, f32[2,2,512,128]{3,2,1,0:T(8,128)S(1)}, u32[]{:S(2)}, u32[]{:S(2)}) collective-permute-start(f32[2,2,512,128]{3,2,1,0:T(8,128)S(1)} %bitcast.12), channel_id=1, source_target_pairs={{0,8},{8,0},{16,24},{24,16},{1,9},{9,1},{17,25},{25,17},{2,10},{10... | collective-permute-start | bytes 3145736 | tf_op jit(solution)/shard_map/ppermute | solution.py:300
  55.6 9.4 %collective-permute-start.16 = (s16[2,528,128]{2,1,0:T(8,128)(2,1)S(1)}, s16[2,528,128]{2,1,0:T(8,128)(2,1)S(1)}, u32[]{:S(2)}, u32[]{:S(2)}) collective-permute-start(s16[2,528,128]{2,1,0:T(8,128)(2,1)S(1)} %get-tuple-element.51), channel_id=1, source_target_pairs={{0,16},{8,24},{16,0},{24,8},{1,17},{9,25},{17,1},{25,9},{2,18},{10... | collective-permute-start | bytes 811016 | tf_op jit(solution)/shard_map/ppermute | solution.py:300
  57.1 7.8 %collective-permute-start.17 = (s16[1,528,128]{2,1,0:T(8,128)(2,1)S(1)}, s16[1,528,128]{2,1,0:T(8,128)(2,1)S(1)}, u32[]{:S(2)}, u32[]{:S(2)}) collective-permute-start(s16[1,528,128]{2,1,0:T(8,128)(2,1)S(1)} %shard_map.76.refs_5_), channel_id=1, source_target_pairs={{0,1},{1,0},{2,3},{3,2},{4,5},{5,4},{6,7},{7,6},{8,9},{9,8},{10,11... | collective-permute-start | bytes 405512 | tf_op jit(solution)/shard_map/ppermute | solution.py:416

commit v3 on v2

--- a/solution.py
+++ b/solution.py
@@ -11,6 +11,7 @@
 HEADB = 2
 GROUPS = 16
 UNROLL = 4
+PAD_ROWS = 128
 VMEM_LIMIT = 24 * 2**20
 F32 = jnp.float32
 I16 = jnp.int16
@@ -20,21 +21,23 @@
 SMEM = pl.BlockSpec(memory_space=pltpu.SMEM)
 
 
-def call(kernel, outs, ins, scratch=(), after=(), in_hbm=0):
+def call(kernel, outs, ins, scratch=(), after=(), in_hbm=0, through=()):
     bytes_moved = sum(math.prod(a.shape) * a.dtype.itemsize for a in (*outs, *ins))
 
     def body(*refs):
-        kernel(*refs[: len(ins)], *refs[len(ins) + len(after) :])
+        outputs = len(ins) + len(after) + len(through)
+        kernel(*refs[: len(ins)], *refs[outputs : outputs + len(outs)], *refs[outputs + len(outs) + len(through) :])
 
     return pl.pallas_call(
         body,
-        out_shape=outs,
-        in_specs=[HBM] * in_hbm + [SMEM if a.ndim == 1 else VMEM for a in ins[in_hbm:]] + [ANY] * len(after),
-        out_specs=[SMEM if len(a.shape) == 1 else VMEM for a in outs],
+        out_shape=[*outs, *(array(a.shape, a.dtype) for a in through)],
+        in_specs=[HBM] * in_hbm + [SMEM if a.ndim == 1 else VMEM for a in ins[in_hbm:]] + [ANY] * len((*after, *through)),
+        out_specs=[SMEM if len(a.shape) == 1 else VMEM for a in outs] + [ANY] * len(through),
+        input_output_aliases={len(ins) + len(after) + i: len(outs) + i for i in range(len(through))},
         scratch_shapes=list(scratch),
         compiler_params=pltpu.CompilerParams(vmem_limit_bytes=VMEM_LIMIT),
         cost_estimate=pl.CostEstimate(flops=0, bytes_accessed=bytes_moved, transcendentals=0),
-    )(*ins, *after)
+    )(*ins, *after, *through)
 
 
 def array(shape, dtype=F32):
@@ -149,7 +152,7 @@
     return 1 - odd, odd
 
 
-def heads_out_kernel(count, blocks, rows_hbm, cols_hbm, perm_hbm, x_hbm, vals_hbm, plan, coded, plain, head_x, mine, x, vals, acc, rows, cols, perm, few):
+def heads_out_kernel(count, blocks, rows_hbm, cols_hbm, perm_hbm, x_hbm, vals_hbm, plan, coded, plain, head_x, x, vals, acc, rows, cols, perm, few):
     copies = [
         pltpu.make_async_copy(a, b, few.at[i])
         for i, (a, b) in enumerate(((rows_hbm, rows), (cols_hbm, cols), (perm_hbm, perm), (x_hbm, x), (vals_hbm, vals)))
@@ -163,9 +166,6 @@
     copies[3].wait()
     for h in range(HEADB):
         head_x[h] = x[perm[0, 0, h]]
-    core = lax.axis_index("level") & 1
-    for j in range(blocks // 2):
-        mine[j] = x[core * (blocks // 2) + j]
     copies[4].wait()
     target = lambda s, t, piece: t
     for_tiles(count, plan, vals, HEAD_ROW, [(lambda v, s, t: dot(v, x[s]), target)], acc, 2 * HEADB)
@@ -175,16 +175,15 @@
         put_coded(coded, i, acc[i])
 
 
-def receives(step):
-    return lax.axis_index("band") % (2 * step) == step
-
-
-def heads_add_kernel(step, had, came, head_x, head_got, coded, plain, head_out):
+def heads_take_kernel(step, head_x, head_got, out):
+    out[...] = jnp.where(lax.axis_index("band") % (2 * step) == step, head_got[...], head_x[...])
+
+
+def heads_add_kernel(had, came, coded, plain):
     for i in range(had.shape[0]):
         value = had[i] + get_coded(came, i)
         plain[i] = value
         put_coded(coded, i, value)
-    head_out[...] = jnp.where(receives(step), head_got[...], head_x[...])
 
 
 def halo_out_kernel(count, blocks, shares, x, vals, plan, near, send, keep, acc, table):
@@ -210,15 +209,16 @@
     own[...] = acc[: shares.slots]
 
 
-def remote_kernel(count, blocks, shares, vals, plan, near, own, pair, pair2, other, other2, head_x, head_got, send, keep, acc, xw, table):
+def remote_kernel(count, blocks, shares, vals, plan, near, own, pair, pair2, other, other2, head_x, send, keep, acc, xw, table):
     half_blocks = blocks // 2
+    tile = xw.shape[1]
     core = lax.axis_index("level") & 1
     for j in range(half_blocks):
         for at, (mine, swapped) in enumerate(((pair, pair2), (other, other2))):
-            xw[at * blocks + core * half_blocks + j] = mine[j]
-            xw[at * blocks + (1 - core) * half_blocks + j] = swapped[j]
+            xw[at * blocks + core * half_blocks + j] = mine[j * tile : (j + 1) * tile]
+            xw[at * blocks + (1 - core) * half_blocks + j] = swapped[j * tile : (j + 1) * tile]
     for j in range(HEADB):
-        xw[2 * blocks + j] = jnp.where(receives(1), head_got[j], head_x[j])
+        xw[2 * blocks + j] = head_x[j]
         table[3 * blocks + j] = 2 * blocks + j
     for part, side in enumerate(sides(lax.axis_index("band"))):
         for j in range(blocks):
@@ -330,21 +330,25 @@
     perm = block_perm[0, 0]
     vals = tile_vals[0]
     x = features.reshape(blocks, tile, width)
-    pair_perm = lax.ppermute(perm, "band", pairs)
-    other_perm = lax.ppermute(pair_perm, "band", inward)
-    near = jnp.concatenate([pair_perm, other_perm])
+    half = lax.dynamic_slice_in_dim(features, (lax.axis_index("level") & 1) * (rdev // 2), rdev // 2, 0)
+    order_row = jnp.pad(perm.astype(features.dtype)[None], ((0, PAD_ROWS - 1), (0, width - blocks)))
+    mine = jnp.concatenate([half, order_row])
+    pair_x = lax.ppermute(mine, "band", pairs)
+    other_x = lax.ppermute(pair_x, "band", inward)
+    pair_x2 = lax.ppermute(pair_x, "level", cores)
+    other_x2 = lax.ppermute(other_x, "level", cores)
+    near = jnp.concatenate([a[rdev // 2, :blocks] for a in (pair_x, other_x)]).astype(jnp.int32)
 
     coded_heads = array((2 * HEADB, tile + GROUPS, width), I16)
     plain_heads = array((2 * HEADB, tile, width))
     in_hbm = lambda a: pltpu.with_memory_space_constraint(a, pltpu.HBM)
-    plan, coded, heads, xh, mine, x, vals = call(
+    plan, coded, heads, xh, x, vals = call(
         functools.partial(heads_out_kernel, count, blocks),
         (
             array((5 * count + 5,), jnp.int32),
             coded_heads,
             plain_heads,
             array((HEADB, tile, width), x.dtype),
-            array((blocks // 2, tile, width), x.dtype),
             pltpu.VMEM(x.shape, x.dtype),
             pltpu.VMEM(vals.shape, vals.dtype),
         ),
@@ -357,14 +361,8 @@
             pltpu.SemaphoreType.DMA((5,)),
         ),
         in_hbm=5,
-        after=(pair_perm,),
     )
     x, vals = (pltpu.with_memory_space_constraint(a, pltpu.VMEM) for a in (x, vals))
-
-    pair_x = lax.ppermute(mine, "band", pairs)
-    other_x = lax.ppermute(pair_x, "band", inward)
-    pair_x2 = lax.ppermute(pair_x, "level", cores)
-    other_x2 = lax.ppermute(other_x, "level", cores)
 
     half_shape = array((2, m, share, width))
     halo_out = functools.partial(
@@ -385,7 +383,8 @@
     )[0]
 
     order = [1 << i for i in range(1, bands.bit_length() - 1)] + [1]
-    fences = [(near, pair_x), (other_x,)] + [()] * bands
+    halo_send = halo_keep = None
+    fences = [(pair_x,), (own,)] + [()] * bands
     done = 0
     for at, bit in enumerate(order):
         step = bands >> (at + 1)
@@ -394,46 +393,49 @@
         came = lax.ppermute(coded, "band", [(i, i - bit) for i in senders])
         got = lax.ppermute(xh, "band", [(i, i + step) for i in range(0, bands, 2 * step)])
         if at == 1:
-            halo_send, halo_keep = halo_out(after=(coded,))
-            halo = over_levels(halo_send, halo_keep, levels)
-            fences[1] += (halo_send, own)
+            halo_send, halo_keep = halo_out(after=(coded, got))
         if bit != order[-1]:
-            coded, heads, xh = call(
-                functools.partial(heads_add_kernel, step),
-                (coded_heads, plain_heads, array(xh.shape, xh.dtype)),
-                (heads, came, xh, got),
+            coded, heads, *passed = call(
+                heads_add_kernel,
+                (coded_heads, plain_heads),
+                (heads, came),
                 after=fences[at],
+                through=(halo_send,) if at == 1 else (),
             )
-
-    halo_had, halo_came, halo_coded = halo
-    relayed, direct = call(
-        functools.partial(edge_kernel, halo_coded),
-        (array((1, share + GROUPS, width), I16), array((1, share, width))),
-        (halo_had, halo_came),
-    )
-    relayed = lax.ppermute(relayed, "band", outward)
-    to_pair = call(relay_kernel, (array((1, share + GROUPS, width), I16),), (direct, relayed))[0]
-    from_near = lax.ppermute(to_pair, "band", pairs)
+            halo_send = passed[0] if passed else halo_send
+        xh = call(
+            functools.partial(heads_take_kernel, step), (array(xh.shape, xh.dtype),), (xh, got), after=(coded,)
+        )[0]
+    halo_had, halo_came, halo_coded = over_levels(halo_send, halo_keep, levels)
 
     send, keep = call(
         functools.partial(remote_kernel, count, blocks, shares),
         (half_shape, half_shape),
-        (vals, plan, near, own, pair_x, pair_x2, other_x, other_x2, xh, got),
+        (vals, plan, near, own, pair_x, pair_x2, other_x, other_x2, xh),
         (
             pltpu.VMEM((shares.slots + 1, unit, width), F32),
             pltpu.VMEM((2 * blocks + HEADB, tile, width), features.dtype),
             pltpu.SMEM((3 * blocks + HEADB,), jnp.int32),
         ),
-        after=(relayed,),
+        after=(halo_had,),
     )
     flat = array((shares.slots // 2, unit, width))
     send, keep = call(
         functools.partial(heads_in_kernel, shares),
         (flat, flat),
         (perm, send.reshape(flat.shape), keep.reshape(flat.shape), heads, came),
-        after=(to_pair,),
-    )
-    had, came, was_coded = over_levels(send.reshape(half_shape.shape), keep.reshape(half_shape.shape), levels)
+        after=(halo_came,),
+    )
+    relayed, direct = call(
+        functools.partial(edge_kernel, halo_coded),
+        (array((1, share + GROUPS, width), I16), array((1, share, width))),
+        (halo_had, halo_came),
+    )
+    had, came, was_coded = over_levels(send.reshape(half_shape.shape), keep.reshape(half_shape.shape), levels, after=(direct,))
+    relayed = lax.ppermute(relayed, "band", outward)
+    to_pair = call(relay_kernel, (array((1, share + GROUPS, width), I16),), (direct, relayed))[0]
+    from_near = lax.ppermute(to_pair, "band", pairs)
+
     out = array((1, share, width), jnp.bfloat16)
     forward, backward = call(functools.partial(last_kernel, was_coded), (out, out), (had, came, from_near))
     return forward, backward

time: 66.9 us -> 61.6 us (0.921); the launches traced: 65.8 us -> 61.2 us
  starting transfers between devices: 39.1 us -> 26.4 us
  waiting for transfers between devices: 11.8 us -> 18.2 us
  local copies, waits for them, and re-layouts: 0.01 us -> 0.98 us
  other arithmetic: 0.07 us -> 0.76 us
    ppermute x2 -> x0, starting transfers between devices: 4.32 us -> none  [the longest x1 3.03 us: on_device(): pair_perm = lax.ppermute(perm, 'band', pairs)]
    ppermute x1, starting transfers between devices: 4.69 us -> 1.31 us  [on_device(): other_x = lax.ppermute(pair_x, 'band', inward)]
    ppermute x1, waiting for transfers between devices: 0.71 us -> 3.96 us  [on_device(): relayed = lax.ppermute(relayed, 'band', outward)]
    ppermute x3, waiting for transfers between devices: 0.01 us -> 3.26 us  [on_device(): came = lax.ppermute(coded, 'band', [(i, i - bit) for i in senders])]
    ppermute x3, starting transfers between devices: 14.2 us -> 11.2 us  [on_device(): lax.ppermute(xh, 'band', [(i, i + step) for i in range(0, bands, 2 * step)])]
    ppermute x3, waiting for transfers between devices: 1.84 us -> 4.82 us  [on_device(): lax.ppermute(xh, 'band', [(i, i + step) for i in range(0, bands, 2 * step)])]
    ppermute x2 -> x0, waiting for transfers between devices: 2.93 us -> none  [the longest x1 1.66 us: on_device(): pair_perm = lax.ppermute(perm, 'band', pairs)]
    ppermute x1, starting transfers between devices: 4.23 us -> 1.8 us  [on_device(): from_near = lax.ppermute(to_pair, 'band', pairs)]
  transfers between devices with their start and end apart: 18 -> 16, of which waited for: 6 -> 8; matrix products, arithmetic and copies ran while one was open for 0% -> 0% of each run, Pallas kernels for 11% -> 20%
where the time goes in v3:
time: 61.6 us; the launch traced here: 61.2 us
  starting transfers between devices  26.4 us (43%)
  waiting for transfers between devices  18.2 us (30%)
  Pallas kernels  14 us (23%)
  local copies, waits for them, and re-layouts  0.98 us (2%)
  between operations  0.88 us (1%)
  other arithmetic  0.76 us (1%)
    pallas_call x15, Pallas kernels, call(): pl.pallas_call(body, out_shape=[*outs, *(array(a.shape, a.dtype) for a in...  14 us
    ppermute x3, starting transfers between devices, on_device(): lax.ppermute(xh, 'band', [(i, i + step) for i in range(0, bands, 2 * step)])  11.2 us
    ppermute x3, waiting for transfers between devices, on_device(): lax.ppermute(xh, 'band', [(i, i + step) for i in range(0, bands, 2 * step)])  4.82 us
    ppermute x1, waiting for transfers between devices, on_device(): relayed = lax.ppermute(relayed, 'band', outward)  3.96 us
    ppermute x3, starting transfers between devices, on_device(): came = lax.ppermute(coded, 'band', [(i, i - bit) for i in senders])  3.86 us
    ppermute x1, waiting for transfers between devices, on_device(): from_near = lax.ppermute(to_pair, 'band', pairs)  3.66 us
    ppermute x4, starting transfers between devices, over_levels(): came = lax.ppermute(send, 'level', pairs)  3.36 us
    ppermute x3, waiting for transfers between devices, on_device(): came = lax.ppermute(coded, 'band', [(i, i - bit) for i in senders])  3.26 us
  transfers between devices with their start and end apart: 16, of which 8 were waited for; matrix products, arithmetic and copies ran while one was open for 0% of the time, Pallas kernels for 20%

profile of v3, /device:TPU:0, one launch (start us, length us, event | category | flops | bytes accessed | tf_op | source)
XLA Modules:
  0.0 61.2 jit_solution(17642831050548631021)
XLA Ops:
  0.6 0.7 %convert_bitcast_fusion = bf16[1,8]{1,0:T(2,128)(2,1)S(1)} fusion(s32[1,1,8]{2,1,0:T(1,128)} %refs_2_.1), kind=kLoop, calls=%fused_computation.6 | loop fusion | flops 8 | bytes 48 | tf_op jit(solution)/shard_map/convert_element_type | solution.py:334
  1.3 1.0 %constant_dynamic-slice_fusion = bf16[1024,128]{1,0:T(8,128)(2,1)S(1)} fusion(bf16[2048,128]{1,0:T(8,128)(2,1)} %param.5, s32[]{:T(128)S(6)} %select_n.3), kind=kLoop, calls=%fused_computation.7 | loop fusion | bytes 524292 | tf_op jit(solution)/shard_map/dynamic_slice | solution.py:333
  2.3 3.0 %collective-permute-start = (bf16[1152,128]{1,0:T(8,128)(2,1)S(1)}, bf16[1152,128]{1,0:T(8,128)(2,1)S(1)}, u32[]{:S(2)}, u32[]{:S(2)}) collective-permute-start(bf16[1152,128]{1,0:T(8,128)(2,1)S(1)} %fusion.1), channel_id=1, source_target_pairs={{0,1},{1,0},{2,3},{3,2},{4,5},{5,4},{6,7},{7,6},{8,9},{9,8},{10,11... | collective-permute-start | bytes 884744 | tf_op jit(solution)/shard_map/ppermute | solution.py:336
  5.3 3.2 %shard_map.68 = (s32[185]{0:T(256)S(1)}, s16[4,272,128]{2,1,0:T(8,128)(2,1)S(1)}, f32[4,256,128]{2,1,0:T(8,128)S(1)}, bf16[2,256,128]{2,1,0:T(8,128)(2,1)S(1)}, ...) custom-call(s32[1,36]{1,0:T(1,128)} %refs_0_.1, s32[1,36]{1,0:T(1,128)} %refs_1_.1, ...), custom_call_target="tpu_custom_call" | custom-call | bytes 11420708 | tf_op jit(solution)/shard_map/pallas_call | solution.py:31
  8.5 1.3 %collective-permute-start.5 = (s16[4,272,128]{2,1,0:T(8,128)(2,1)S(1)}, s16[4,272,128]{2,1,0:T(8,128)(2,1)S(1)}, u32[]{:S(2)}, u32[]{:S(2)}) collective-permute-start(s16[4,272,128]{2,1,0:T(8,128)(2,1)S(1)} %get-tuple-element.30), channel_id=1, source_target_pairs={{2,0},{3,1},{6,4},{7,5},{10,8},{11,9},{14,12},{15,13},{18,16},{19,... | collective-permute-start | bytes 835592 | tf_op jit(solution)/shard_map/ppermute | solution.py:393
  9.8 5.8 %collective-permute-start.4 = (bf16[2,256,128]{2,1,0:T(8,128)(2,1)S(1)}, bf16[2,256,128]{2,1,0:T(8,128)(2,1)S(1)}, u32[]{:S(2)}, u32[]{:S(2)}) collective-permute-start(bf16[2,256,128]{2,1,0:T(8,128)(2,1)S(1)} %get-tuple-element.28.refs_0_), channel_id=1, source_target_pairs={{0,4},{8,12},{16,20},{24,28}} | collective-permute-start | bytes 393224 | tf_op jit(solution)/shard_map/ppermute | solution.py:394
  15.6 0.0 collective-permute-done.refs_2_.refs_4_
  15.6 1.3 %collective-permute-start.1 = (bf16[1152,128]{1,0:T(8,128)(2,1)S(1)}, bf16[1152,128]{1,0:T(8,128)(2,1)S(1)}, u32[]{:S(2)}, u32[]{:S(2)}) collective-permute-start(bf16[1152,128]{1,0:T(8,128)(2,1)S(1)} %collective-permute-done.refs_2_.refs_4_), channel_id=1, source_target_pairs={{3,1},{0,2},{5,3},{2,4},{7,5},{4,6},{11,9},{8,10},{13,11},{10,12},... | collective-permute-start | bytes 884744 | tf_op jit(solution)/shard_map/ppermute | solution.py:337
  16.9 4.5 %shard_map.69.refs_2_.refs_3_ = f32[16,256,128]{2,1,0:T(8,128)S(1)} custom-call(bf16[8,256,128]{2,1,0:T(8,128)(2,1)S(1)} %get-tuple-element.27.refs_0_, bf16[36,256,256]{2,1,0:T(8,128)(2,1)S(1)} %get-tuple-element.25.refs_1_.refs_0_, s32[185]{0:T(256)S(1)} %get-tuple-element.26.refs_2_.refs_1_), custom_call_target="tpu_custom_call" | custom-call | bytes 7340772 | tf_op jit(solution)/shard_map/pallas_call | solution.py:31
  21.5 0.0 collective-permute-done.5.refs_1_
  21.5 0.3 shard_map.70
  21.8 1.3 %collective-permute-start.7 = (s16[4,272,128]{2,1,0:T(8,128)(2,1)S(1)}, s16[4,272,128]{2,1,0:T(8,128)(2,1)S(1)}, u32[]{:S(2)}, u32[]{:S(2)}) collective-permute-start(s16[4,272,128]{2,1,0:T(8,128)(2,1)S(1)} %get-tuple-element.31.refs_2_.refs_4_), channel_id=1, source_target_pairs={{4,0},{5,1},{12,8},{13,9},{20,16},{21,17},{28,24},{29,25}} | collective-permute-start | bytes 835592 | tf_op jit(solution)/shard_map/ppermute | solution.py:393
  23.1 0.0 collective-permute-done.4.refs_1_
  23.2 1.3 %collective-permute-start.6 = (bf16[2,256,128]{2,1,0:T(8,128)(2,1)S(1)}, bf16[2,256,128]{2,1,0:T(8,128)(2,1)S(1)}, u32[]{:S(2)}, u32[]{:S(2)}) collective-permute-start(bf16[2,256,128]{2,1,0:T(8,128)(2,1)S(1)} %shard_map.71.refs_0_), channel_id=1, source_target_pairs={{0,2},{4,6},{8,10},{12,14},{16,18},{20,22},{24,26},{28,30}} | collective-permute-start | bytes 393224 | tf_op jit(solution)/shard_map/ppermute | solution.py:394
  24.5 0.6 collective-permute-done.1.refs_6_
  25.0 0.1 maximum_convert_fusion.refs_3_.refs_2_
  25.1 2.1 %collective-permute-done.6.refs_5_.refs_1_ = bf16[2,256,128]{2,1,0:T(8,128)(2,1)S(1)} collective-permute-done((bf16[2,256,128]{2,1,0:T(8,128)(2,1)S(1)}, bf16[2,256,128]{2,1,0:T(8,128)(2,1)S(1)}, u32[]{:S(2)}, u32[]{:S(2)}) %collective-permute-start.6) | collective-permute-done | bytes 131104 | tf_op jit(solution)/shard_map/ppermute | solution.py:394
  27.2 1.5 %shard_map.72 = (f32[2,2,512,128]{3,2,1,0:T(8,128)S(1)}, f32[2,2,512,128]{3,2,1,0:T(8,128)S(1)}) custom-call(bf16[8,256,128]{2,1,0:T(8,128)(2,1)S(1)} %get-tuple-element.27.refs_0_, bf16[36,256,256]{2,1,0:T(8,128)(2,1)S(1)} %get-tuple-element.25.refs_1_.refs_0_, s32[185]{0:T(256)S(1)} %get-tuple-element.26.refs_2_.refs_1_, ...), custom_call_target="tpu_custom_call" | custom-call | bytes 7340836 | tf_op jit(solution)/shard_map/pallas_call | solution.py:31
  28.7 3.3 %collective-permute-done.7.refs_1_ = s16[4,272,128]{2,1,0:T(8,128)(2,1)S(1)} collective-permute-done((s16[4,272,128]{2,1,0:T(8,128)(2,1)S(1)}, s16[4,272,128]{2,1,0:T(8,128)(2,1)S(1)}, u32[]{:S(2)}, u32[]{:S(2)}) %collective-permute-start.7) | collective-permute-done | bytes 278560 | tf_op jit(solution)/shard_map/ppermute | solution.py:393
  32.0 0.3 shard_map.73
  32.3 0.1 collective-permute-start.9
  32.4 0.5 collective-permute-start.2
  32.9 0.1 collective-permute-start.3
  32.9 1.3 %collective-permute-start.10 = (s16[4,272,128]{2,1,0:T(8,128)(2,1)S(1)}, s16[4,272,128]{2,1,0:T(8,128)(2,1)S(1)}, u32[]{:S(2)}, u32[]{:S(2)}) collective-permute-start(s16[4,272,128]{2,1,0:T(8,128)(2,1)S(1)} %get-tuple-element.34.refs_2_), channel_id=1, source_target_pairs={{1,0},{9,8},{17,16},{25,24}} | collective-permute-start | bytes 835592 | tf_op jit(solution)/shard_map/ppermute | solution.py:393
  34.2 0.8 %collective-permute-done.9.refs_1_ = f32[2,2,512,128]{3,2,1,0:T(8,128)S(1)} collective-permute-done((f32[2,2,512,128]{3,2,1,0:T(8,128)S(1)}, f32[2,2,512,128]{3,2,1,0:T(8,128)S(1)}, u32[]{:S(2)}, u32[]{:S(2)}) %collective-permute-start.9) | collective-permute-done | bytes 1048608 | tf_op jit(solution)/shard_map/ppermute | solution.py:300
  35.0 0.3 shard_map.76
  35.3 2.0 %collective-permute-start.11 = (s16[2,528,128]{2,1,0:T(8,128)(2,1)S(1)}, s16[2,528,128]{2,1,0:T(8,128)(2,1)S(1)}, u32[]{:S(2)}, u32[]{:S(2)}) collective-permute-start(s16[2,528,128]{2,1,0:T(8,128)(2,1)S(1)} %get-tuple-element.41), channel_id=1, source_target_pairs={{0,16},{8,24},{16,0},{24,8},{1,17},{9,25},{17,1},{25,9},{2,18},{10... | collective-permute-start | bytes 811016 | tf_op jit(solution)/shard_map/ppermute | solution.py:300
  37.3 0.0 copy-start
  37.3 4.1 %collective-permute-start.8 = (bf16[2,256,128]{2,1,0:T(8,128)(2,1)S(1)}, bf16[2,256,128]{2,1,0:T(8,128)(2,1)S(1)}, u32[]{:S(2)}, u32[]{:S(2)}) collective-permute-start(bf16[2,256,128]{2,1,0:T(8,128)(2,1)S(1)} %shard_map.74.refs_0_), channel_id=1, source_target_pairs={{0,1},{2,3},{4,5},{6,7},{8,9},{10,11},{12,13},{14,15},{16,17},{18,... | collective-permute-start | bytes 393224 | tf_op jit(solution)/shard_map/ppermute | solution.py:394
  41.4 2.8 %collective-permute-done.8.refs_1_ = bf16[2,256,128]{2,1,0:T(8,128)(2,1)S(1)} collective-permute-done((bf16[2,256,128]{2,1,0:T(8,128)(2,1)S(1)}, bf16[2,256,128]{2,1,0:T(8,128)(2,1)S(1)}, u32[]{:S(2)}, u32[]{:S(2)}) %collective-permute-start.8) | collective-permute-done | bytes 131104 | tf_op jit(solution)/shard_map/ppermute | solution.py:394
  44.2 0.0 collective-permute-done.2.refs_5_
  44.2 0.0 collective-permute-done.3.refs_7_
  44.2 1.5 %shard_map.77 = (f32[2,2,512,128]{3,2,1,0:T(8,128)S(1)}, f32[2,2,512,128]{3,2,1,0:T(8,128)S(1)}) custom-call(bf16[36,256,256]{2,1,0:T(8,128)(2,1)S(1)} %get-tuple-element.25.refs_1_.refs_0_, s32[185]{0:T(256)S(1)} %get-tuple-element.26.refs_2_.refs_1_, s32[16]{0:T(128)S(1)} %maximum_convert_fusion.refs_3_.refs_2_, ...), custom_call_target="tpu_custom_call" | custom-call | bytes 10224420 | tf_op jit(solution)/shard_map/pallas_call | solution.py:31
  45.8 0.0 collective-permute-done.10.refs_4_
  45.8 0.0 collective-permute-done.11.refs_5_.refs_1_
  45.8 0.0 copy-done
  45.8 0.8 %shard_map.78 = (f32[8,256,128]{2,1,0:T(8,128)S(1)}, f32[8,256,128]{2,1,0:T(8,128)S(1)}) custom-call(s32[8]{0:T(128)S(1)} %bitcast.16, f32[8,256,128]{2,1,0:T(8,128)S(1)} %bitcast.14, f32[8,256,128]{2,1,0:T(8,128)S(1)} %bitcast.15, f32[4,256,128]{2,1,0:T(8,128)S(1)} %get-tuple-element.40.refs_3_, s16[4,272,128]{2,1,0:T(8,128)(2,1)S(1)} %collective-permute-done.10.refs_4_, ...), custom_call_target="tpu_custom_call" | custom-call | bytes 4997152 | tf_op jit(solution)/shard_map/pallas_call | solution.py:31
  46.7 0.1 collective-permute-start.12
  46.7 0.2 shard_map.79
  46.9 1.3 %collective-permute-start.14 = (s16[1,528,128]{2,1,0:T(8,128)(2,1)S(1)}, s16[1,528,128]{2,1,0:T(8,128)(2,1)S(1)}, u32[]{:S(2)}, u32[]{:S(2)}) collective-permute-start(s16[1,528,128]{2,1,0:T(8,128)(2,1)S(1)} %get-tuple-element.47), channel_id=1, source_target_pairs={{1,3},{2,0},{3,5},{4,2},{5,7},{6,4},{9,11},{10,8},{11,13},{12,10},... | collective-permute-start | bytes 405512 | tf_op jit(solution)/shard_map/ppermute | solution.py:435
  48.2 1.1 %collective-permute-done.12.refs_1_ = f32[2,2,512,128]{3,2,1,0:T(8,128)S(1)} collective-permute-done((f32[2,2,512,128]{3,2,1,0:T(8,128)S(1)}, f32[2,2,512,128]{3,2,1,0:T(8,128)S(1)}, u32[]{:S(2)}, u32[]{:S(2)}) %collective-permute-start.12) | collective-permute-done | bytes 1048608 | tf_op jit(solution)/shard_map/ppermute | solution.py:300
  49.4 0.3 shard_map.80
  49.6 1.2 %collective-permute-start.13 = (s16[2,528,128]{2,1,0:T(8,128)(2,1)S(1)}, s16[2,528,128]{2,1,0:T(8,128)(2,1)S(1)}, u32[]{:S(2)}, u32[]{:S(2)}) collective-permute-start(s16[2,528,128]{2,1,0:T(8,128)(2,1)S(1)} %get-tuple-element.46), channel_id=1, source_target_pairs={{0,16},{8,24},{16,0},{24,8},{1,17},{9,25},{17,1},{25,9},{2,18},{10... | collective-permute-start | bytes 811016 | tf_op jit(solution)/shard_map/ppermute | solution.py:300
  50.9 4.0 %collective-permute-done.14.refs_1_ = s16[1,528,128]{2,1,0:T(8,128)(2,1)S(1)} collective-permute-done((s16[1,528,128]{2,1,0:T(8,128)(2,1)S(1)}, s16[1,528,128]{2,1,0:T(8,128)(2,1)S(1)}, u32[]{:S(2)}, u32[]{:S(2)}) %collective-permute-start.14) | collective-permute-done | bytes 135200 | tf_op jit(solution)/shard_map/ppermute | solution.py:435
  54.8 0.1 shard_map.81
  54.9 1.8 %collective-permute-start.15 = (s16[1,528,128]{2,1,0:T(8,128)(2,1)S(1)}, s16[1,528,128]{2,1,0:T(8,128)(2,1)S(1)}, u32[]{:S(2)}, u32[]{:S(2)}) collective-permute-start(s16[1,528,128]{2,1,0:T(8,128)(2,1)S(1)} %shard_map.81), channel_id=1, source_target_pairs={{0,1},{1,0},{2,3},{3,2},{4,5},{5,4},{6,7},{7,6},{8,9},{9,8},{10,11... | collective-permute-start | bytes 405512 | tf_op jit(solution)/shard_map/ppermute | solution.py:437
  56.8 3.7 %collective-permute-done.15.refs_2_ = s16[1,528,128]{2,1,0:T(8,128)(2,1)S(1)} collective-permute-done((s16[1,528,128]{2,1,0:T(8,128)(2,1)S(1)}, s16[1,528,128]{2,1,0:T(8,128)(2,1)S(1)}, u32[]{:S(2)}, u32[]{:S(2)}) %collective-permute-start.15) | collective-permute-done | bytes 135200 | tf_op jit(solution)/shard_map/ppermute | solution.py:437
  60.4 0.0 collective-permute-done.13.refs_1_
  60.4 0.8 %shard_map.82 = (bf16[1,512,128]{2,1,0:T(8,128)(2,1)}, bf16[1,512,128]{2,1,0:T(8,128)(2,1)}) custom-call(f32[2,1,512,128]{3,2,1,0:T(8,128)S(1)} %get-tuple-element.45.refs_0_, s16[2,528,128]{2,1,0:T(8,128)(2,1)S(1)} %collective-permute-done.13.refs_1_, s16[1,528,128]{2,1,0:T(8,128)(2,1)S(1)} %collective-permute-done.15.refs_2_), custom_call_target="tpu_custom_call" | custom-call | bytes 1191936 | tf_op jit(solution)/shard_map/pallas_call | solution.py:31
  (6 shorter events, 0.1 us)
Async XLA Ops:
  2.3 13.3 %collective-permute-start = (bf16[1152,128]{1,0:T(8,128)(2,1)S(1)}, bf16[1152,128]{1,0:T(8,128)(2,1)S(1)}, u32[]{:S(2)}, u32[]{:S(2)}) collective-permute-start(bf16[1152,128]{1,0:T(8,128)(2,1)S(1)} %fusion.1), channel_id=1, source_target_pairs={{0,1},{1,0},{2,3},{3,2},{4,5},{5,4},{6,7},{7,6},{8,9},{9,8},{10,11... | collective-permute-start | bytes 884744 | tf_op jit(solution)/shard_map/ppermute | solution.py:336
  8.5 13.0 %collective-permute-start.5 = (s16[4,272,128]{2,1,0:T(8,128)(2,1)S(1)}, s16[4,272,128]{2,1,0:T(8,128)(2,1)S(1)}, u32[]{:S(2)}, u32[]{:S(2)}) collective-permute-start(s16[4,272,128]{2,1,0:T(8,128)(2,1)S(1)} %get-tuple-element.30), channel_id=1, source_target_pairs={{2,0},{3,1},{6,4},{7,5},{10,8},{11,9},{14,12},{15,13},{18,16},{19,... | collective-permute-start | bytes 835592 | tf_op jit(solution)/shard_map/ppermute | solution.py:393
  9.8 13.3 %collective-permute-start.4 = (bf16[2,256,128]{2,1,0:T(8,128)(2,1)S(1)}, bf16[2,256,128]{2,1,0:T(8,128)(2,1)S(1)}, u32[]{:S(2)}, u32[]{:S(2)}) collective-permute-start(bf16[2,256,128]{2,1,0:T(8,128)(2,1)S(1)} %get-tuple-element.28.refs_0_), channel_id=1, source_target_pairs={{0,4},{8,12},{16,20},{24,28}} | collective-permute-start | bytes 393224 | tf_op jit(solution)/shard_map/ppermute | solution.py:394
  15.6 9.4 %collective-permute-start.1 = (bf16[1152,128]{1,0:T(8,128)(2,1)S(1)}, bf16[1152,128]{1,0:T(8,128)(2,1)S(1)}, u32[]{:S(2)}, u32[]{:S(2)}) collective-permute-start(bf16[1152,128]{1,0:T(8,128)(2,1)S(1)} %collective-permute-done.refs_2_.refs_4_), channel_id=1, source_target_pairs={{3,1},{0,2},{5,3},{2,4},{7,5},{4,6},{11,9},{8,10},{13,11},{10,12},... | collective-permute-start | bytes 884744 | tf_op jit(solution)/shard_map/ppermute | solution.py:337
  21.8 10.2 %collective-permute-start.7 = (s16[4,272,128]{2,1,0:T(8,128)(2,1)S(1)}, s16[4,272,128]{2,1,0:T(8,128)(2,1)S(1)}, u32[]{:S(2)}, u32[]{:S(2)}) collective-permute-start(s16[4,272,128]{2,1,0:T(8,128)(2,1)S(1)} %get-tuple-element.31.refs_2_.refs_4_), channel_id=1, source_target_pairs={{4,0},{5,1},{12,8},{13,9},{20,16},{21,17},{28,24},{29,25}} | collective-permute-start | bytes 835592 | tf_op jit(solution)/shard_map/ppermute | solution.py:393
  23.2 4.0 %collective-permute-start.6 = (bf16[2,256,128]{2,1,0:T(8,128)(2,1)S(1)}, bf16[2,256,128]{2,1,0:T(8,128)(2,1)S(1)}, u32[]{:S(2)}, u32[]{:S(2)}) collective-permute-start(bf16[2,256,128]{2,1,0:T(8,128)(2,1)S(1)} %shard_map.71.refs_0_), channel_id=1, source_target_pairs={{0,2},{4,6},{8,10},{12,14},{16,18},{20,22},{24,26},{28,30}} | collective-permute-start | bytes 393224 | tf_op jit(solution)/shard_map/ppermute | solution.py:394
  32.3 2.7 %collective-permute-start.9 = (f32[2,2,512,128]{3,2,1,0:T(8,128)S(1)}, f32[2,2,512,128]{3,2,1,0:T(8,128)S(1)}, u32[]{:S(2)}, u32[]{:S(2)}) collective-permute-start(f32[2,2,512,128]{3,2,1,0:T(8,128)S(1)} %get-tuple-element.36), channel_id=1, source_target_pairs={{0,8},{8,0},{16,24},{24,16},{1,9},{9,1},{17,25},{25,17},{2,10},{10... | collective-permute-start | bytes 3145736 | tf_op jit(solution)/shard_map/ppermute | solution.py:300
  32.4 11.8 %collective-permute-start.2 = (bf16[1152,128]{1,0:T(8,128)(2,1)S(1)}, bf16[1152,128]{1,0:T(8,128)(2,1)S(1)}, u32[]{:S(2)}, u32[]{:S(2)}) collective-permute-start(bf16[1152,128]{1,0:T(8,128)(2,1)S(1)} %collective-permute-done.refs_2_.refs_4_), channel_id=1, source_target_pairs={{0,8},{8,0},{16,24},{24,16},{1,9},{9,1},{17,25},{25,17},{2,10},{10... | collective-permute-start | bytes 884744 | tf_op jit(solution)/shard_map/ppermute | solution.py:338
  32.9 11.4 %collective-permute-start.3 = (bf16[1152,128]{1,0:T(8,128)(2,1)S(1)}, bf16[1152,128]{1,0:T(8,128)(2,1)S(1)}, u32[]{:S(2)}, u32[]{:S(2)}) collective-permute-start(bf16[1152,128]{1,0:T(8,128)(2,1)S(1)} %collective-permute-done.1.refs_6_), channel_id=1, source_target_pairs={{0,8},{8,0},{16,24},{24,16},{1,9},{9,1},{17,25},{25,17},{2,10},{10... | collective-permute-start | bytes 884744 | tf_op jit(solution)/shard_map/ppermute | solution.py:339
  32.9 12.8 %collective-permute-start.10 = (s16[4,272,128]{2,1,0:T(8,128)(2,1)S(1)}, s16[4,272,128]{2,1,0:T(8,128)(2,1)S(1)}, u32[]{:S(2)}, u32[]{:S(2)}) collective-permute-start(s16[4,272,128]{2,1,0:T(8,128)(2,1)S(1)} %get-tuple-element.34.refs_2_), channel_id=1, source_target_pairs={{1,0},{9,8},{17,16},{25,24}} | collective-permute-start | bytes 835592 | tf_op jit(solution)/shard_map/ppermute | solution.py:393
  35.3 10.5 %collective-permute-start.11 = (s16[2,528,128]{2,1,0:T(8,128)(2,1)S(1)}, s16[2,528,128]{2,1,0:T(8,128)(2,1)S(1)}, u32[]{:S(2)}, u32[]{:S(2)}) collective-permute-start(s16[2,528,128]{2,1,0:T(8,128)(2,1)S(1)} %get-tuple-element.41), channel_id=1, source_target_pairs={{0,16},{8,24},{16,0},{24,8},{1,17},{9,25},{17,1},{25,9},{2,18},{10... | collective-permute-start | bytes 811016 | tf_op jit(solution)/shard_map/ppermute | solution.py:300
  37.3 8.5 %copy-start = (s32[1,1,8]{2,1,0:T(1,128)S(1)}, s32[1,1,8]{2,1,0:T(1,128)}, u32[]{:S(2)}) copy-start(s32[1,1,8]{2,1,0:T(1,128)} %refs_2_.1) | copy-start | bytes 100
  37.3 6.8 %collective-permute-start.8 = (bf16[2,256,128]{2,1,0:T(8,128)(2,1)S(1)}, bf16[2,256,128]{2,1,0:T(8,128)(2,1)S(1)}, u32[]{:S(2)}, u32[]{:S(2)}) collective-permute-start(bf16[2,256,128]{2,1,0:T(8,128)(2,1)S(1)} %shard_map.74.refs_0_), channel_id=1, source_target_pairs={{0,1},{2,3},{4,5},{6,7},{8,9},{10,11},{12,13},{14,15},{16,17},{18,... | collective-permute-start | bytes 393224 | tf_op jit(solution)/shard_map/ppermute | solution.py:394
  46.7 2.7 %collective-permute-start.12 = (f32[2,2,512,128]{3,2,1,0:T(8,128)S(1)}, f32[2,2,512,128]{3,2,1,0:T(8,128)S(1)}, u32[]{:S(2)}, u32[]{:S(2)}) collective-permute-start(f32[2,2,512,128]{3,2,1,0:T(8,128)S(1)} %bitcast.17), channel_id=1, source_target_pairs={{0,8},{8,0},{16,24},{24,16},{1,9},{9,1},{17,25},{25,17},{2,10},{10... | collective-permute-start | bytes 3145736 | tf_op jit(solution)/shard_map/ppermute | solution.py:300
  46.9 7.9 %collective-permute-start.14 = (s16[1,528,128]{2,1,0:T(8,128)(2,1)S(1)}, s16[1,528,128]{2,1,0:T(8,128)(2,1)S(1)}, u32[]{:S(2)}, u32[]{:S(2)}) collective-permute-start(s16[1,528,128]{2,1,0:T(8,128)(2,1)S(1)} %get-tuple-element.47), channel_id=1, source_target_pairs={{1,3},{2,0},{3,5},{4,2},{5,7},{6,4},{9,11},{10,8},{11,13},{12,10},... | collective-permute-start | bytes 405512 | tf_op jit(solution)/shard_map/ppermute | solution.py:435
  49.6 10.8 %collective-permute-start.13 = (s16[2,528,128]{2,1,0:T(8,128)(2,1)S(1)}, s16[2,528,128]{2,1,0:T(8,128)(2,1)S(1)}, u32[]{:S(2)}, u32[]{:S(2)}) collective-permute-start(s16[2,528,128]{2,1,0:T(8,128)(2,1)S(1)} %get-tuple-element.46), channel_id=1, source_target_pairs={{0,16},{8,24},{16,0},{24,8},{1,17},{9,25},{17,1},{25,9},{2,18},{10... | collective-permute-start | bytes 811016 | tf_op jit(solution)/shard_map/ppermute | solution.py:300
  54.9 5.5 %collective-permute-start.15 = (s16[1,528,128]{2,1,0:T(8,128)(2,1)S(1)}, s16[1,528,128]{2,1,0:T(8,128)(2,1)S(1)}, u32[]{:S(2)}, u32[]{:S(2)}) collective-permute-start(s16[1,528,128]{2,1,0:T(8,128)(2,1)S(1)} %shard_map.81), channel_id=1, source_target_pairs={{0,1},{1,0},{2,3},{3,2},{4,5},{5,4},{6,7},{7,6},{8,9},{9,8},{10,11... | collective-permute-start | bytes 405512 | tf_op jit(solution)/shard_map/ppermute | solution.py:437

commit v4 on v3

--- a/solution.py
+++ b/solution.py
@@ -209,7 +209,9 @@
     own[...] = acc[: shares.slots]
 
 
-def remote_kernel(count, blocks, shares, vals, plan, near, own, pair, pair2, other, other2, head_x, send, keep, acc, xw, table):
+def remote_kernel(
+    count, blocks, shares, vals, plan, near, perm, own, pair, pair2, other, other2, head_x, heads, came, send, keep, acc, xw, table
+):
     half_blocks = blocks // 2
     tile = xw.shape[1]
     core = lax.axis_index("level") & 1
@@ -228,32 +230,18 @@
     backward = (lambda v, s, t: dot_t(v, xw[2 * blocks + t]), lambda s, t, piece: shares.slot(1, s, piece))
     for_tiles(count, plan, vals, REMOTE, [forward], acc, shares.slots)
     for_tiles(count, plan, vals, HEAD_ROW, [backward], acc, shares.slots)
+
+    @pl.when(lax.axis_index("band") == 0)
+    def _():
+        for part in range(2):
+            for h in range(HEADB):
+                value = heads[part * HEADB + h] + get_coded(came, part * HEADB + h)
+                for piece in range(shares.pieces):
+                    acc[shares.slot(part, perm[h], piece)] += value[piece * shares.unit : (piece + 1) * shares.unit]
+
     half = shares.slots // 2
     send[...] = acc[:half].reshape(send.shape)
     keep[...] = acc[half : 2 * half].reshape(keep.shape)
-
-
-def heads_in_kernel(shares, perm, send_in, keep_in, had, came, send, keep):
-    send[...] = send_in[...]
-    keep[...] = keep_in[...]
-
-    @pl.when(lax.axis_index("band") == 0)
-    def _():
-        half = shares.slots // 2
-        for part in range(2):
-            for h in range(HEADB):
-                value = had[part * HEADB + h] + get_coded(came, part * HEADB + h)
-                for piece in range(shares.pieces):
-                    slot = shares.slot(part, perm[h], piece)
-                    some = value[piece * shares.unit : (piece + 1) * shares.unit]
-
-                    @pl.when(slot < half)
-                    def _():
-                        send[slot] += some
-
-                    @pl.when(slot >= half)
-                    def _():
-                        keep[slot - half] += some
 
 
 def split_kernel(bit, coded_in, had, came, send, keep):
@@ -411,19 +399,12 @@
     send, keep = call(
         functools.partial(remote_kernel, count, blocks, shares),
         (half_shape, half_shape),
-        (vals, plan, near, own, pair_x, pair_x2, other_x, other_x2, xh),
+        (vals, plan, near, perm, own, pair_x, pair_x2, other_x, other_x2, xh, heads, came),
         (
             pltpu.VMEM((shares.slots + 1, unit, width), F32),
             pltpu.VMEM((2 * blocks + HEADB, tile, width), features.dtype),
             pltpu.SMEM((3 * blocks + HEADB,), jnp.int32),
         ),
-        after=(halo_had,),
-    )
-    flat = array((shares.slots // 2, unit, width))
-    send, keep = call(
-        functools.partial(heads_in_kernel, shares),
-        (flat, flat),
-        (perm, send.reshape(flat.shape), keep.reshape(flat.shape), heads, came),
         after=(halo_came,),
     )
     relayed, direct = call(
@@ -431,7 +412,7 @@
         (array((1, share + GROUPS, width), I16), array((1, share, width))),
         (halo_had, halo_came),
     )
-    had, came, was_coded = over_levels(send.reshape(half_shape.shape), keep.reshape(half_shape.shape), levels, after=(direct,))
+    had, came, was_coded = over_levels(send, keep, levels, after=(direct,))
     relayed = lax.ppermute(relayed, "band", outward)
     to_pair = call(relay_kernel, (array((1, share + GROUPS, width), I16),), (direct, relayed))[0]
     from_near = lax.ppermute(to_pair, "band", pairs)

time: 61.6 us -> 61 us (level)
  waiting for transfers between devices: 18.2 us -> 19.3 us
  starting transfers between devices: 26.4 us -> 25.4 us
    ppermute x4, starting transfers between devices: 3.36 us -> 2.08 us  [over_levels(): came = lax.ppermute(send, 'level', pairs)]
    ppermute x3, starting transfers between devices: 11.2 us -> 12.1 us  [on_device(): lax.ppermute(xh, 'band', [(i, i + step) for i in range(0, bands, 2 * step)])]
    ppermute x1, starting transfers between devices: 1.8 us -> 1.12 us  [on_device(): from_near = lax.ppermute(to_pair, 'band', pairs)]
    pallas_call x15 -> x14, Pallas kernels: 14 us -> 13.4 us  [call(): pl.pallas_call(body, out_shape=[*outs, *(array(a.shape, a.dtype) for a in...]
  transfers between devices with their start and end apart: 16 -> 16, of which waited for: 8 -> 9; matrix products, arithmetic and copies ran while one was open for 0% -> 0% of each run, Pallas kernels for 20% -> 17%
where the time goes in v4:
time: 61 us; the launch traced here: 60.7 us
  starting transfers between devices  25.4 us (42%)
  waiting for transfers between devices  19.3 us (32%)
  Pallas kernels  13.4 us (22%)
  local copies, waits for them, and re-layouts  0.98 us (2%)
  between operations  0.85 us (1%)
  other arithmetic  0.76 us (1%)
    pallas_call x14, Pallas kernels, call(): pl.pallas_call(body, out_shape=[*outs, *(array(a.shape, a.dtype) for a in...  13.4 us
    ppermute x3, starting transfers between devices, on_device(): lax.ppermute(xh, 'band', [(i, i + step) for i in range(0, bands, 2 * step)])  12.1 us
    ppermute x3, waiting for transfers between devices, on_device(): lax.ppermute(xh, 'band', [(i, i + step) for i in range(0, bands, 2 * step)])  5.28 us
    ppermute x1, waiting for transfers between devices, on_device(): from_near = lax.ppermute(to_pair, 'band', pairs)  4.13 us
    ppermute x1, waiting for transfers between devices, on_device(): relayed = lax.ppermute(relayed, 'band', outward)  3.88 us
    ppermute x3, starting transfers between devices, on_device(): came = lax.ppermute(coded, 'band', [(i, i - bit) for i in senders])  3.86 us
    ppermute x3, waiting for transfers between devices, on_device(): came = lax.ppermute(coded, 'band', [(i, i - bit) for i in senders])  3.47 us
    ppermute x1, starting transfers between devices, on_device(): pair_x = lax.ppermute(mine, 'band', pairs)  3.03 us
  transfers between devices with their start and end apart: 16, of which 9 were waited for; matrix products, arithmetic and copies ran while one was open for 0% of the time, Pallas kernels for 17%

profile of v4, /device:TPU:0, one launch (start us, length us, event | category | flops | bytes accessed | tf_op | source)
XLA Modules:
  0.0 60.7 jit_solution(13849615743074985553)
XLA Ops:
  0.6 0.7 %convert_bitcast_fusion = bf16[1,8]{1,0:T(2,128)(2,1)S(1)} fusion(s32[1,1,8]{2,1,0:T(1,128)} %refs_2_.1), kind=kLoop, calls=%fused_computation.6 | loop fusion | flops 8 | bytes 48 | tf_op jit(solution)/shard_map/convert_element_type | solution.py:322
  1.3 1.0 %constant_dynamic-slice_fusion = bf16[1024,128]{1,0:T(8,128)(2,1)S(1)} fusion(bf16[2048,128]{1,0:T(8,128)(2,1)} %param.5, s32[]{:T(128)S(6)} %select_n.3), kind=kLoop, calls=%fused_computation.7 | loop fusion | bytes 524292 | tf_op jit(solution)/shard_map/dynamic_slice | solution.py:321
  2.3 3.0 %collective-permute-start = (bf16[1152,128]{1,0:T(8,128)(2,1)S(1)}, bf16[1152,128]{1,0:T(8,128)(2,1)S(1)}, u32[]{:S(2)}, u32[]{:S(2)}) collective-permute-start(bf16[1152,128]{1,0:T(8,128)(2,1)S(1)} %fusion.1), channel_id=1, source_target_pairs={{0,1},{1,0},{2,3},{3,2},{4,5},{5,4},{6,7},{7,6},{8,9},{9,8},{10,11... | collective-permute-start | bytes 884744 | tf_op jit(solution)/shard_map/ppermute | solution.py:324
  5.3 3.2 %shard_map.68 = (s32[185]{0:T(256)S(1)}, s16[4,272,128]{2,1,0:T(8,128)(2,1)S(1)}, f32[4,256,128]{2,1,0:T(8,128)S(1)}, bf16[2,256,128]{2,1,0:T(8,128)(2,1)S(1)}, ...) custom-call(s32[1,36]{1,0:T(1,128)} %refs_0_.1, s32[1,36]{1,0:T(1,128)} %refs_1_.1, ...), custom_call_target="tpu_custom_call" | custom-call | bytes 11420708 | tf_op jit(solution)/shard_map/pallas_call | solution.py:31
  8.5 1.3 %collective-permute-start.5 = (s16[4,272,128]{2,1,0:T(8,128)(2,1)S(1)}, s16[4,272,128]{2,1,0:T(8,128)(2,1)S(1)}, u32[]{:S(2)}, u32[]{:S(2)}) collective-permute-start(s16[4,272,128]{2,1,0:T(8,128)(2,1)S(1)} %get-tuple-element.28), channel_id=1, source_target_pairs={{2,0},{3,1},{6,4},{7,5},{10,8},{11,9},{14,12},{15,13},{18,16},{19,... | collective-permute-start | bytes 835592 | tf_op jit(solution)/shard_map/ppermute | solution.py:381
  9.8 5.8 %collective-permute-start.4 = (bf16[2,256,128]{2,1,0:T(8,128)(2,1)S(1)}, bf16[2,256,128]{2,1,0:T(8,128)(2,1)S(1)}, u32[]{:S(2)}, u32[]{:S(2)}) collective-permute-start(bf16[2,256,128]{2,1,0:T(8,128)(2,1)S(1)} %get-tuple-element.26.refs_0_), channel_id=1, source_target_pairs={{0,4},{8,12},{16,20},{24,28}} | collective-permute-start | bytes 393224 | tf_op jit(solution)/shard_map/ppermute | solution.py:382
  15.6 0.0 collective-permute-done.refs_2_.refs_5_
  15.6 1.3 %collective-permute-start.1 = (bf16[1152,128]{1,0:T(8,128)(2,1)S(1)}, bf16[1152,128]{1,0:T(8,128)(2,1)S(1)}, u32[]{:S(2)}, u32[]{:S(2)}) collective-permute-start(bf16[1152,128]{1,0:T(8,128)(2,1)S(1)} %collective-permute-done.refs_2_.refs_5_), channel_id=1, source_target_pairs={{3,1},{0,2},{5,3},{2,4},{7,5},{4,6},{11,9},{8,10},{13,11},{10,12},... | collective-permute-start | bytes 884744 | tf_op jit(solution)/shard_map/ppermute | solution.py:325
  16.9 4.1 %shard_map.69.refs_2_.refs_4_ = f32[16,256,128]{2,1,0:T(8,128)S(1)} custom-call(bf16[8,256,128]{2,1,0:T(8,128)(2,1)S(1)} %get-tuple-element.25.refs_0_, bf16[36,256,256]{2,1,0:T(8,128)(2,1)S(1)} %get-tuple-element.23.refs_1_.refs_0_, s32[185]{0:T(256)S(1)} %get-tuple-element.24.refs_2_.refs_1_), custom_call_target="tpu_custom_call" | custom-call | bytes 7340772 | tf_op jit(solution)/shard_map/pallas_call | solution.py:31
  21.0 0.0 collective-permute-done.5.refs_1_
  21.0 0.3 shard_map.70
  21.3 1.3 %collective-permute-start.7 = (s16[4,272,128]{2,1,0:T(8,128)(2,1)S(1)}, s16[4,272,128]{2,1,0:T(8,128)(2,1)S(1)}, u32[]{:S(2)}, u32[]{:S(2)}) collective-permute-start(s16[4,272,128]{2,1,0:T(8,128)(2,1)S(1)} %get-tuple-element.29.refs_2_.refs_4_), channel_id=1, source_target_pairs={{4,0},{5,1},{12,8},{13,9},{20,16},{21,17},{28,24},{29,25}} | collective-permute-start | bytes 835592 | tf_op jit(solution)/shard_map/ppermute | solution.py:381
  22.6 0.0 collective-permute-done.4.refs_1_
  22.7 1.3 %collective-permute-start.6 = (bf16[2,256,128]{2,1,0:T(8,128)(2,1)S(1)}, bf16[2,256,128]{2,1,0:T(8,128)(2,1)S(1)}, u32[]{:S(2)}, u32[]{:S(2)}) collective-permute-start(bf16[2,256,128]{2,1,0:T(8,128)(2,1)S(1)} %shard_map.71.refs_0_), channel_id=1, source_target_pairs={{0,2},{4,6},{8,10},{12,14},{16,18},{20,22},{24,26},{28,30}} | collective-permute-start | bytes 393224 | tf_op jit(solution)/shard_map/ppermute | solution.py:382
  24.0 0.6 collective-permute-done.1.refs_7_
  24.6 0.1 maximum_convert_fusion.refs_3_.refs_2_
  24.7 2.5 %collective-permute-done.6.refs_5_.refs_1_ = bf16[2,256,128]{2,1,0:T(8,128)(2,1)S(1)} collective-permute-done((bf16[2,256,128]{2,1,0:T(8,128)(2,1)S(1)}, bf16[2,256,128]{2,1,0:T(8,128)(2,1)S(1)}, u32[]{:S(2)}, u32[]{:S(2)}) %collective-permute-start.6) | collective-permute-done | bytes 131104 | tf_op jit(solution)/shard_map/ppermute | solution.py:382
  27.2 1.9 %shard_map.72 = (f32[2,2,512,128]{3,2,1,0:T(8,128)S(1)}, f32[2,2,512,128]{3,2,1,0:T(8,128)S(1)}) custom-call(bf16[8,256,128]{2,1,0:T(8,128)(2,1)S(1)} %get-tuple-element.25.refs_0_, bf16[36,256,256]{2,1,0:T(8,128)(2,1)S(1)} %get-tuple-element.23.refs_1_.refs_0_, s32[185]{0:T(256)S(1)} %get-tuple-element.24.refs_2_.refs_1_, ...), custom_call_target="tpu_custom_call" | custom-call | bytes 7340836 | tf_op jit(solution)/shard_map/pallas_call | solution.py:31
  29.1 0.0 copy-start
  29.1 3.3 %collective-permute-done.7.refs_1_ = s16[4,272,128]{2,1,0:T(8,128)(2,1)S(1)} collective-permute-done((s16[4,272,128]{2,1,0:T(8,128)(2,1)S(1)}, s16[4,272,128]{2,1,0:T(8,128)(2,1)S(1)}, u32[]{:S(2)}, u32[]{:S(2)}) %collective-permute-start.7) | collective-permute-done | bytes 278560 | tf_op jit(solution)/shard_map/ppermute | solution.py:381
  32.4 0.3 shard_map.73
  32.8 0.1 collective-permute-start.10
  32.8 0.5 collective-permute-start.2
  33.3 0.1 collective-permute-start.3
  33.4 1.3 %collective-permute-start.9 = (s16[4,272,128]{2,1,0:T(8,128)(2,1)S(1)}, s16[4,272,128]{2,1,0:T(8,128)(2,1)S(1)}, u32[]{:S(2)}, u32[]{:S(2)}) collective-permute-start(s16[4,272,128]{2,1,0:T(8,128)(2,1)S(1)} %get-tuple-element.32.refs_2_), channel_id=1, source_target_pairs={{1,0},{9,8},{17,16},{25,24}} | collective-permute-start | bytes 835592 | tf_op jit(solution)/shard_map/ppermute | solution.py:381
  34.7 0.8 %collective-permute-done.10.refs_1_ = f32[2,2,512,128]{3,2,1,0:T(8,128)S(1)} collective-permute-done((f32[2,2,512,128]{3,2,1,0:T(8,128)S(1)}, f32[2,2,512,128]{3,2,1,0:T(8,128)S(1)}, u32[]{:S(2)}, u32[]{:S(2)}) %collective-permute-start.10) | collective-permute-done | bytes 1048608 | tf_op jit(solution)/shard_map/ppermute | solution.py:288
  35.5 0.3 shard_map.76
  35.7 0.6 %collective-permute-start.11 = (s16[2,528,128]{2,1,0:T(8,128)(2,1)S(1)}, s16[2,528,128]{2,1,0:T(8,128)(2,1)S(1)}, u32[]{:S(2)}, u32[]{:S(2)}) collective-permute-start(s16[2,528,128]{2,1,0:T(8,128)(2,1)S(1)} %get-tuple-element.36), channel_id=1, source_target_pairs={{0,16},{8,24},{16,0},{24,8},{1,17},{9,25},{17,1},{25,9},{2,18},{10... | collective-permute-start | bytes 811016 | tf_op jit(solution)/shard_map/ppermute | solution.py:288
  36.4 5.0 %collective-permute-start.8 = (bf16[2,256,128]{2,1,0:T(8,128)(2,1)S(1)}, bf16[2,256,128]{2,1,0:T(8,128)(2,1)S(1)}, u32[]{:S(2)}, u32[]{:S(2)}) collective-permute-start(bf16[2,256,128]{2,1,0:T(8,128)(2,1)S(1)} %shard_map.74.refs_0_), channel_id=1, source_target_pairs={{0,1},{2,3},{4,5},{6,7},{8,9},{10,11},{12,13},{14,15},{16,17},{18,... | collective-permute-start | bytes 393224 | tf_op jit(solution)/shard_map/ppermute | solution.py:382
  41.4 2.8 %collective-permute-done.8.refs_1_ = bf16[2,256,128]{2,1,0:T(8,128)(2,1)S(1)} collective-permute-done((bf16[2,256,128]{2,1,0:T(8,128)(2,1)S(1)}, bf16[2,256,128]{2,1,0:T(8,128)(2,1)S(1)}, u32[]{:S(2)}, u32[]{:S(2)}) %collective-permute-start.8) | collective-permute-done | bytes 131104 | tf_op jit(solution)/shard_map/ppermute | solution.py:382
  44.2 0.0 collective-permute-done.2.refs_6_
  44.2 0.1 collective-permute-done.9.refs_11_
  44.4 0.0 collective-permute-done.3.refs_8_
  44.4 0.0 collective-permute-done.11.refs_12_.refs_1_
  44.4 0.0 copy-done
  44.4 2.0 %shard_map.77 = (f32[2,2,512,128]{3,2,1,0:T(8,128)S(1)}, f32[2,2,512,128]{3,2,1,0:T(8,128)S(1)}) custom-call(bf16[36,256,256]{2,1,0:T(8,128)(2,1)S(1)} %get-tuple-element.23.refs_1_.refs_0_, s32[185]{0:T(256)S(1)} %get-tuple-element.24.refs_2_.refs_1_, s32[16]{0:T(128)S(1)} %maximum_convert_fusion.refs_3_.refs_2_, s32[8]{0:T(128)S(1)} %bitcast.9, ...), custom_call_target="tpu_custom_call" | custom-call | bytes 11027268 | tf_op jit(solution)/shard_map/pallas_call | solution.py:31
  46.4 0.1 collective-permute-start.12
  46.4 0.2 shard_map.78
  46.7 1.3 %collective-permute-start.14 = (s16[1,528,128]{2,1,0:T(8,128)(2,1)S(1)}, s16[1,528,128]{2,1,0:T(8,128)(2,1)S(1)}, u32[]{:S(2)}, u32[]{:S(2)}) collective-permute-start(s16[1,528,128]{2,1,0:T(8,128)(2,1)S(1)} %get-tuple-element.43), channel_id=1, source_target_pairs={{1,3},{2,0},{3,5},{4,2},{5,7},{6,4},{9,11},{10,8},{11,13},{12,10},... | collective-permute-start | bytes 405512 | tf_op jit(solution)/shard_map/ppermute | solution.py:416
  48.0 1.1 %collective-permute-done.12.refs_1_ = f32[2,2,512,128]{3,2,1,0:T(8,128)S(1)} collective-permute-done((f32[2,2,512,128]{3,2,1,0:T(8,128)S(1)}, f32[2,2,512,128]{3,2,1,0:T(8,128)S(1)}, u32[]{:S(2)}, u32[]{:S(2)}) %collective-permute-start.12) | collective-permute-done | bytes 1048608 | tf_op jit(solution)/shard_map/ppermute | solution.py:288
  49.1 0.2 shard_map.79
  49.3 1.3 %collective-permute-start.13 = (s16[2,528,128]{2,1,0:T(8,128)(2,1)S(1)}, s16[2,528,128]{2,1,0:T(8,128)(2,1)S(1)}, u32[]{:S(2)}, u32[]{:S(2)}) collective-permute-start(s16[2,528,128]{2,1,0:T(8,128)(2,1)S(1)} %get-tuple-element.42), channel_id=1, source_target_pairs={{0,16},{8,24},{16,0},{24,8},{1,17},{9,25},{17,1},{25,9},{2,18},{10... | collective-permute-start | bytes 811016 | tf_op jit(solution)/shard_map/ppermute | solution.py:288
  50.6 3.9 %collective-permute-done.14.refs_1_ = s16[1,528,128]{2,1,0:T(8,128)(2,1)S(1)} collective-permute-done((s16[1,528,128]{2,1,0:T(8,128)(2,1)S(1)}, s16[1,528,128]{2,1,0:T(8,128)(2,1)S(1)}, u32[]{:S(2)}, u32[]{:S(2)}) %collective-permute-start.14) | collective-permute-done | bytes 135200 | tf_op jit(solution)/shard_map/ppermute | solution.py:416
  54.5 0.1 shard_map.80
  54.7 1.1 %collective-permute-start.15 = (s16[1,528,128]{2,1,0:T(8,128)(2,1)S(1)}, s16[1,528,128]{2,1,0:T(8,128)(2,1)S(1)}, u32[]{:S(2)}, u32[]{:S(2)}) collective-permute-start(s16[1,528,128]{2,1,0:T(8,128)(2,1)S(1)} %shard_map.80), channel_id=1, source_target_pairs={{0,1},{1,0},{2,3},{3,2},{4,5},{5,4},{6,7},{7,6},{8,9},{9,8},{10,11... | collective-permute-start | bytes 405512 | tf_op jit(solution)/shard_map/ppermute | solution.py:418
  55.8 4.1 %collective-permute-done.15.refs_2_ = s16[1,528,128]{2,1,0:T(8,128)(2,1)S(1)} collective-permute-done((s16[1,528,128]{2,1,0:T(8,128)(2,1)S(1)}, s16[1,528,128]{2,1,0:T(8,128)(2,1)S(1)}, u32[]{:S(2)}, u32[]{:S(2)}) %collective-permute-start.15) | collective-permute-done | bytes 135200 | tf_op jit(solution)/shard_map/ppermute | solution.py:418
  59.9 0.0 collective-permute-done.13.refs_1_
  59.9 0.8 %shard_map.81 = (bf16[1,512,128]{2,1,0:T(8,128)(2,1)}, bf16[1,512,128]{2,1,0:T(8,128)(2,1)}) custom-call(f32[2,1,512,128]{3,2,1,0:T(8,128)S(1)} %get-tuple-element.41.refs_0_, s16[2,528,128]{2,1,0:T(8,128)(2,1)S(1)} %collective-permute-done.13.refs_1_, s16[1,528,128]{2,1,0:T(8,128)(2,1)S(1)} %collective-permute-done.15.refs_2_), custom_call_target="tpu_custom_call" | custom-call | bytes 1191936 | tf_op jit(solution)/shard_map/pallas_call | solution.py:31
  (6 shorter events, 0.1 us)
Async XLA Ops:
  2.3 13.3 %collective-permute-start = (bf16[1152,128]{1,0:T(8,128)(2,1)S(1)}, bf16[1152,128]{1,0:T(8,128)(2,1)S(1)}, u32[]{:S(2)}, u32[]{:S(2)}) collective-permute-start(bf16[1152,128]{1,0:T(8,128)(2,1)S(1)} %fusion.1), channel_id=1, source_target_pairs={{0,1},{1,0},{2,3},{3,2},{4,5},{5,4},{6,7},{7,6},{8,9},{9,8},{10,11... | collective-permute-start | bytes 884744 | tf_op jit(solution)/shard_map/ppermute | solution.py:324
  8.5 12.5 %collective-permute-start.5 = (s16[4,272,128]{2,1,0:T(8,128)(2,1)S(1)}, s16[4,272,128]{2,1,0:T(8,128)(2,1)S(1)}, u32[]{:S(2)}, u32[]{:S(2)}) collective-permute-start(s16[4,272,128]{2,1,0:T(8,128)(2,1)S(1)} %get-tuple-element.28), channel_id=1, source_target_pairs={{2,0},{3,1},{6,4},{7,5},{10,8},{11,9},{14,12},{15,13},{18,16},{19,... | collective-permute-start | bytes 835592 | tf_op jit(solution)/shard_map/ppermute | solution.py:381
  9.8 12.9 %collective-permute-start.4 = (bf16[2,256,128]{2,1,0:T(8,128)(2,1)S(1)}, bf16[2,256,128]{2,1,0:T(8,128)(2,1)S(1)}, u32[]{:S(2)}, u32[]{:S(2)}) collective-permute-start(bf16[2,256,128]{2,1,0:T(8,128)(2,1)S(1)} %get-tuple-element.26.refs_0_), channel_id=1, source_target_pairs={{0,4},{8,12},{16,20},{24,28}} | collective-permute-start | bytes 393224 | tf_op jit(solution)/shard_map/ppermute | solution.py:382
  15.6 9.0 %collective-permute-start.1 = (bf16[1152,128]{1,0:T(8,128)(2,1)S(1)}, bf16[1152,128]{1,0:T(8,128)(2,1)S(1)}, u32[]{:S(2)}, u32[]{:S(2)}) collective-permute-start(bf16[1152,128]{1,0:T(8,128)(2,1)S(1)} %collective-permute-done.refs_2_.refs_5_), channel_id=1, source_target_pairs={{3,1},{0,2},{5,3},{2,4},{7,5},{4,6},{11,9},{8,10},{13,11},{10,12},... | collective-permute-start | bytes 884744 | tf_op jit(solution)/shard_map/ppermute | solution.py:325
  21.3 11.1 %collective-permute-start.7 = (s16[4,272,128]{2,1,0:T(8,128)(2,1)S(1)}, s16[4,272,128]{2,1,0:T(8,128)(2,1)S(1)}, u32[]{:S(2)}, u32[]{:S(2)}) collective-permute-start(s16[4,272,128]{2,1,0:T(8,128)(2,1)S(1)} %get-tuple-element.29.refs_2_.refs_4_), channel_id=1, source_target_pairs={{4,0},{5,1},{12,8},{13,9},{20,16},{21,17},{28,24},{29,25}} | collective-permute-start | bytes 835592 | tf_op jit(solution)/shard_map/ppermute | solution.py:381
  22.7 4.5 %collective-permute-start.6 = (bf16[2,256,128]{2,1,0:T(8,128)(2,1)S(1)}, bf16[2,256,128]{2,1,0:T(8,128)(2,1)S(1)}, u32[]{:S(2)}, u32[]{:S(2)}) collective-permute-start(bf16[2,256,128]{2,1,0:T(8,128)(2,1)S(1)} %shard_map.71.refs_0_), channel_id=1, source_target_pairs={{0,2},{4,6},{8,10},{12,14},{16,18},{20,22},{24,26},{28,30}} | collective-permute-start | bytes 393224 | tf_op jit(solution)/shard_map/ppermute | solution.py:382
  29.1 15.3 %copy-start = (s32[1,1,8]{2,1,0:T(1,128)S(1)}, s32[1,1,8]{2,1,0:T(1,128)}, u32[]{:S(2)}) copy-start(s32[1,1,8]{2,1,0:T(1,128)} %refs_2_.1) | copy-start | bytes 100
  32.8 2.7 %collective-permute-start.10 = (f32[2,2,512,128]{3,2,1,0:T(8,128)S(1)}, f32[2,2,512,128]{3,2,1,0:T(8,128)S(1)}, u32[]{:S(2)}, u32[]{:S(2)}) collective-permute-start(f32[2,2,512,128]{3,2,1,0:T(8,128)S(1)} %get-tuple-element.35), channel_id=1, source_target_pairs={{0,8},{8,0},{16,24},{24,16},{1,9},{9,1},{17,25},{25,17},{2,10},{10... | collective-permute-start | bytes 3145736 | tf_op jit(solution)/shard_map/ppermute | solution.py:288
  32.8 11.4 %collective-permute-start.2 = (bf16[1152,128]{1,0:T(8,128)(2,1)S(1)}, bf16[1152,128]{1,0:T(8,128)(2,1)S(1)}, u32[]{:S(2)}, u32[]{:S(2)}) collective-permute-start(bf16[1152,128]{1,0:T(8,128)(2,1)S(1)} %collective-permute-done.refs_2_.refs_5_), channel_id=1, source_target_pairs={{0,8},{8,0},{16,24},{24,16},{1,9},{9,1},{17,25},{25,17},{2,10},{10... | collective-permute-start | bytes 884744 | tf_op jit(solution)/shard_map/ppermute | solution.py:326
  33.3 11.0 %collective-permute-start.3 = (bf16[1152,128]{1,0:T(8,128)(2,1)S(1)}, bf16[1152,128]{1,0:T(8,128)(2,1)S(1)}, u32[]{:S(2)}, u32[]{:S(2)}) collective-permute-start(bf16[1152,128]{1,0:T(8,128)(2,1)S(1)} %collective-permute-done.1.refs_7_), channel_id=1, source_target_pairs={{0,8},{8,0},{16,24},{24,16},{1,9},{9,1},{17,25},{25,17},{2,10},{10... | collective-permute-start | bytes 884744 | tf_op jit(solution)/shard_map/ppermute | solution.py:327
  33.4 11.0 %collective-permute-start.9 = (s16[4,272,128]{2,1,0:T(8,128)(2,1)S(1)}, s16[4,272,128]{2,1,0:T(8,128)(2,1)S(1)}, u32[]{:S(2)}, u32[]{:S(2)}) collective-permute-start(s16[4,272,128]{2,1,0:T(8,128)(2,1)S(1)} %get-tuple-element.32.refs_2_), channel_id=1, source_target_pairs={{1,0},{9,8},{17,16},{25,24}} | collective-permute-start | bytes 835592 | tf_op jit(solution)/shard_map/ppermute | solution.py:381
  35.7 8.6 %collective-permute-start.11 = (s16[2,528,128]{2,1,0:T(8,128)(2,1)S(1)}, s16[2,528,128]{2,1,0:T(8,128)(2,1)S(1)}, u32[]{:S(2)}, u32[]{:S(2)}) collective-permute-start(s16[2,528,128]{2,1,0:T(8,128)(2,1)S(1)} %get-tuple-element.36), channel_id=1, source_target_pairs={{0,16},{8,24},{16,0},{24,8},{1,17},{9,25},{17,1},{25,9},{2,18},{10... | collective-permute-start | bytes 811016 | tf_op jit(solution)/shard_map/ppermute | solution.py:288
  36.4 7.8 %collective-permute-start.8 = (bf16[2,256,128]{2,1,0:T(8,128)(2,1)S(1)}, bf16[2,256,128]{2,1,0:T(8,128)(2,1)S(1)}, u32[]{:S(2)}, u32[]{:S(2)}) collective-permute-start(bf16[2,256,128]{2,1,0:T(8,128)(2,1)S(1)} %shard_map.74.refs_0_), channel_id=1, source_target_pairs={{0,1},{2,3},{4,5},{6,7},{8,9},{10,11},{12,13},{14,15},{16,17},{18,... | collective-permute-start | bytes 393224 | tf_op jit(solution)/shard_map/ppermute | solution.py:382
  46.4 2.7 %collective-permute-start.12 = (f32[2,2,512,128]{3,2,1,0:T(8,128)S(1)}, f32[2,2,512,128]{3,2,1,0:T(8,128)S(1)}, u32[]{:S(2)}, u32[]{:S(2)}) collective-permute-start(f32[2,2,512,128]{3,2,1,0:T(8,128)S(1)} %get-tuple-element.38), channel_id=1, source_target_pairs={{0,8},{8,0},{16,24},{24,16},{1,9},{9,1},{17,25},{25,17},{2,10},{10... | collective-permute-start | bytes 3145736 | tf_op jit(solution)/shard_map/ppermute | solution.py:288
  46.7 7.9 %collective-permute-start.14 = (s16[1,528,128]{2,1,0:T(8,128)(2,1)S(1)}, s16[1,528,128]{2,1,0:T(8,128)(2,1)S(1)}, u32[]{:S(2)}, u32[]{:S(2)}) collective-permute-start(s16[1,528,128]{2,1,0:T(8,128)(2,1)S(1)} %get-tuple-element.43), channel_id=1, source_target_pairs={{1,3},{2,0},{3,5},{4,2},{5,7},{6,4},{9,11},{10,8},{11,13},{12,10},... | collective-permute-start | bytes 405512 | tf_op jit(solution)/shard_map/ppermute | solution.py:416
  49.3 10.6 %collective-permute-start.13 = (s16[2,528,128]{2,1,0:T(8,128)(2,1)S(1)}, s16[2,528,128]{2,1,0:T(8,128)(2,1)S(1)}, u32[]{:S(2)}, u32[]{:S(2)}) collective-permute-start(s16[2,528,128]{2,1,0:T(8,128)(2,1)S(1)} %get-tuple-element.42), channel_id=1, source_target_pairs={{0,16},{8,24},{16,0},{24,8},{1,17},{9,25},{17,1},{25,9},{2,18},{10... | collective-permute-start | bytes 811016 | tf_op jit(solution)/shard_map/ppermute | solution.py:288
  54.7 5.3 %collective-permute-start.15 = (s16[1,528,128]{2,1,0:T(8,128)(2,1)S(1)}, s16[1,528,128]{2,1,0:T(8,128)(2,1)S(1)}, u32[]{:S(2)}, u32[]{:S(2)}) collective-permute-start(s16[1,528,128]{2,1,0:T(8,128)(2,1)S(1)} %shard_map.80), channel_id=1, source_target_pairs={{0,1},{1,0},{2,3},{3,2},{4,5},{5,4},{6,7},{7,6},{8,9},{9,8},{10,11... | collective-permute-start | bytes 405512 | tf_op jit(solution)/shard_map/ppermute | solution.py:418

commit v5 on v4

--- a/solution.py
+++ b/solution.py
@@ -10,7 +10,7 @@
 
 HEADB = 2
 GROUPS = 16
-UNROLL = 4
+UNROLL = 8
 PAD_ROWS = 128
 VMEM_LIMIT = 24 * 2**20
 F32 = jnp.float32

time: 61 us -> 60.3 us (0.989)
  Pallas kernels: 13.4 us -> 12.4 us
    ppermute x1, waiting for transfers between devices: 0.57 us -> 2.76 us  [on_device(): other_x = lax.ppermute(pair_x, 'band', inward)]
    ppermute x3, waiting for transfers between devices: 3.47 us -> 1.96 us  [on_device(): came = lax.ppermute(coded, 'band', [(i, i - bit) for i in senders])]
    ppermute x4, starting transfers between devices: 2.08 us -> 3.39 us  [over_levels(): came = lax.ppermute(send, 'level', pairs)]
    ppermute x3, waiting for transfers between devices: 5.28 us -> 4.06 us  [on_device(): lax.ppermute(xh, 'band', [(i, i + step) for i in range(0, bands, 2 * step)])]
    pallas_call x14, Pallas kernels: 13.4 us -> 12.4 us  [call(): pl.pallas_call(body, out_shape=[*outs, *(array(a.shape, a.dtype) for a in...]
    ppermute x3, starting transfers between devices: 12.1 us -> 11.5 us  [on_device(): lax.ppermute(xh, 'band', [(i, i + step) for i in range(0, bands, 2 * step)])]
  transfers between devices with their start and end apart: 16 -> 16, of which waited for: 9 -> 8; matrix products, arithmetic and copies ran while one was open for 0% -> 0% of each run, Pallas kernels for 17% -> 15%
where the time goes in v5:
time: 60.3 us; the launch traced here: 60.2 us
  starting transfers between devices  25.5 us (42%)
  waiting for transfers between devices  19.7 us (33%)
  Pallas kernels  12.4 us (21%)
  local copies, waits for them, and re-layouts  0.98 us (2%)
  between operations  0.88 us (1%)
  other arithmetic  0.76 us (1%)
    pallas_call x14, Pallas kernels, call(): pl.pallas_call(body, out_shape=[*outs, *(array(a.shape, a.dtype) for a in...  12.4 us
    ppermute x3, starting transfers between devices, on_device(): lax.ppermute(xh, 'band', [(i, i + step) for i in range(0, bands, 2 * step)])  11.5 us
    ppermute x1, waiting for transfers between devices, on_device(): from_near = lax.ppermute(to_pair, 'band', pairs)  4.72 us
    ppermute x1, waiting for transfers between devices, on_device(): relayed = lax.ppermute(relayed, 'band', outward)  4.24 us
    ppermute x3, waiting for transfers between devices, on_device(): lax.ppermute(xh, 'band', [(i, i + step) for i in range(0, bands, 2 * step)])  4.06 us
    ppermute x3, starting transfers between devices, on_device(): came = lax.ppermute(coded, 'band', [(i, i - bit) for i in senders])  3.86 us
    ppermute x4, starting transfers between devices, over_levels(): came = lax.ppermute(send, 'level', pairs)  3.39 us
    ppermute x1, starting transfers between devices, on_device(): pair_x = lax.ppermute(mine, 'band', pairs)  3.03 us
  transfers between devices with their start and end apart: 16, of which 8 were waited for; matrix products, arithmetic and copies ran while one was open for 0% of the time, Pallas kernels for 15%

profile of v5, /device:TPU:0, one launch (start us, length us, event | category | flops | bytes accessed | tf_op | source)
XLA Modules:
  0.0 60.2 jit_solution(14980605442011786095)
XLA Ops:
  0.6 0.7 %convert_bitcast_fusion = bf16[1,8]{1,0:T(2,128)(2,1)S(1)} fusion(s32[1,1,8]{2,1,0:T(1,128)} %refs_2_.1), kind=kLoop, calls=%fused_computation.6 | loop fusion | flops 8 | bytes 48 | tf_op jit(solution)/shard_map/convert_element_type | solution.py:322
  1.3 1.0 %constant_dynamic-slice_fusion = bf16[1024,128]{1,0:T(8,128)(2,1)S(1)} fusion(bf16[2048,128]{1,0:T(8,128)(2,1)} %param.5, s32[]{:T(128)S(6)} %select_n.3), kind=kLoop, calls=%fused_computation.7 | loop fusion | bytes 524292 | tf_op jit(solution)/shard_map/dynamic_slice | solution.py:321
  2.3 3.0 %collective-permute-start = (bf16[1152,128]{1,0:T(8,128)(2,1)S(1)}, bf16[1152,128]{1,0:T(8,128)(2,1)S(1)}, u32[]{:S(2)}, u32[]{:S(2)}) collective-permute-start(bf16[1152,128]{1,0:T(8,128)(2,1)S(1)} %fusion.1), channel_id=1, source_target_pairs={{0,1},{1,0},{2,3},{3,2},{4,5},{5,4},{6,7},{7,6},{8,9},{9,8},{10,11... | collective-permute-start | bytes 884744 | tf_op jit(solution)/shard_map/ppermute | solution.py:324
  5.3 3.2 %shard_map.68 = (s32[185]{0:T(256)S(1)}, s16[4,272,128]{2,1,0:T(8,128)(2,1)S(1)}, f32[4,256,128]{2,1,0:T(8,128)S(1)}, bf16[2,256,128]{2,1,0:T(8,128)(2,1)S(1)}, ...) custom-call(s32[1,36]{1,0:T(1,128)} %refs_0_.1, s32[1,36]{1,0:T(1,128)} %refs_1_.1, ...), custom_call_target="tpu_custom_call" | custom-call | bytes 11420708 | tf_op jit(solution)/shard_map/pallas_call | solution.py:31
  8.5 1.3 %collective-permute-start.5 = (s16[4,272,128]{2,1,0:T(8,128)(2,1)S(1)}, s16[4,272,128]{2,1,0:T(8,128)(2,1)S(1)}, u32[]{:S(2)}, u32[]{:S(2)}) collective-permute-start(s16[4,272,128]{2,1,0:T(8,128)(2,1)S(1)} %get-tuple-element.28), channel_id=1, source_target_pairs={{2,0},{3,1},{6,4},{7,5},{10,8},{11,9},{14,12},{15,13},{18,16},{19,... | collective-permute-start | bytes 835592 | tf_op jit(solution)/shard_map/ppermute | solution.py:381
  9.8 5.5 %collective-permute-start.4 = (bf16[2,256,128]{2,1,0:T(8,128)(2,1)S(1)}, bf16[2,256,128]{2,1,0:T(8,128)(2,1)S(1)}, u32[]{:S(2)}, u32[]{:S(2)}) collective-permute-start(bf16[2,256,128]{2,1,0:T(8,128)(2,1)S(1)} %get-tuple-element.26.refs_0_), channel_id=1, source_target_pairs={{0,4},{8,12},{16,20},{24,28}} | collective-permute-start | bytes 393224 | tf_op jit(solution)/shard_map/ppermute | solution.py:382
  15.3 0.0 collective-permute-done.refs_2_.refs_5_
  15.3 1.3 %collective-permute-start.1 = (bf16[1152,128]{1,0:T(8,128)(2,1)S(1)}, bf16[1152,128]{1,0:T(8,128)(2,1)S(1)}, u32[]{:S(2)}, u32[]{:S(2)}) collective-permute-start(bf16[1152,128]{1,0:T(8,128)(2,1)S(1)} %collective-permute-done.refs_2_.refs_5_), channel_id=1, source_target_pairs={{3,1},{0,2},{5,3},{2,4},{7,5},{4,6},{11,9},{8,10},{13,11},{10,12},... | collective-permute-start | bytes 884744 | tf_op jit(solution)/shard_map/ppermute | solution.py:325
  16.6 3.1 %shard_map.69.refs_2_.refs_4_ = f32[16,256,128]{2,1,0:T(8,128)S(1)} custom-call(bf16[8,256,128]{2,1,0:T(8,128)(2,1)S(1)} %get-tuple-element.25.refs_0_, bf16[36,256,256]{2,1,0:T(8,128)(2,1)S(1)} %get-tuple-element.23.refs_1_.refs_0_, s32[185]{0:T(256)S(1)} %get-tuple-element.24.refs_2_.refs_1_), custom_call_target="tpu_custom_call" | custom-call | bytes 7340772 | tf_op jit(solution)/shard_map/pallas_call | solution.py:31
  19.7 0.0 collective-permute-done.5.refs_1_
  19.7 0.3 shard_map.70
  20.0 1.3 %collective-permute-start.7 = (s16[4,272,128]{2,1,0:T(8,128)(2,1)S(1)}, s16[4,272,128]{2,1,0:T(8,128)(2,1)S(1)}, u32[]{:S(2)}, u32[]{:S(2)}) collective-permute-start(s16[4,272,128]{2,1,0:T(8,128)(2,1)S(1)} %get-tuple-element.29.refs_2_.refs_4_), channel_id=1, source_target_pairs={{4,0},{5,1},{12,8},{13,9},{20,16},{21,17},{28,24},{29,25}} | collective-permute-start | bytes 835592 | tf_op jit(solution)/shard_map/ppermute | solution.py:381
  21.3 0.0 collective-permute-done.4.refs_1_
  21.4 1.3 %collective-permute-start.6 = (bf16[2,256,128]{2,1,0:T(8,128)(2,1)S(1)}, bf16[2,256,128]{2,1,0:T(8,128)(2,1)S(1)}, u32[]{:S(2)}, u32[]{:S(2)}) collective-permute-start(bf16[2,256,128]{2,1,0:T(8,128)(2,1)S(1)} %shard_map.71.refs_0_), channel_id=1, source_target_pairs={{0,2},{4,6},{8,10},{12,14},{16,18},{20,22},{24,26},{28,30}} | collective-permute-start | bytes 393224 | tf_op jit(solution)/shard_map/ppermute | solution.py:382
  22.7 2.8 %collective-permute-done.1.refs_7_ = bf16[1152,128]{1,0:T(8,128)(2,1)S(1)} collective-permute-done((bf16[1152,128]{1,0:T(8,128)(2,1)S(1)}, bf16[1152,128]{1,0:T(8,128)(2,1)S(1)}, u32[]{:S(2)}, u32[]{:S(2)}) %collective-permute-start.1) | collective-permute-done | bytes 294944 | tf_op jit(solution)/shard_map/ppermute | solution.py:325
  25.4 0.1 maximum_convert_fusion.refs_3_.refs_2_
  25.5 1.3 %collective-permute-done.6.refs_5_.refs_1_ = bf16[2,256,128]{2,1,0:T(8,128)(2,1)S(1)} collective-permute-done((bf16[2,256,128]{2,1,0:T(8,128)(2,1)S(1)}, bf16[2,256,128]{2,1,0:T(8,128)(2,1)S(1)}, u32[]{:S(2)}, u32[]{:S(2)}) %collective-permute-start.6) | collective-permute-done | bytes 131104 | tf_op jit(solution)/shard_map/ppermute | solution.py:382
  26.8 1.8 %shard_map.72 = (f32[2,2,512,128]{3,2,1,0:T(8,128)S(1)}, f32[2,2,512,128]{3,2,1,0:T(8,128)S(1)}) custom-call(bf16[8,256,128]{2,1,0:T(8,128)(2,1)S(1)} %get-tuple-element.25.refs_0_, bf16[36,256,256]{2,1,0:T(8,128)(2,1)S(1)} %get-tuple-element.23.refs_1_.refs_0_, s32[185]{0:T(256)S(1)} %get-tuple-element.24.refs_2_.refs_1_, ...), custom_call_target="tpu_custom_call" | custom-call | bytes 7340836 | tf_op jit(solution)/shard_map/pallas_call | solution.py:31
  28.7 0.0 copy-start
  28.7 2.0 %collective-permute-done.7.refs_1_ = s16[4,272,128]{2,1,0:T(8,128)(2,1)S(1)} collective-permute-done((s16[4,272,128]{2,1,0:T(8,128)(2,1)S(1)}, s16[4,272,128]{2,1,0:T(8,128)(2,1)S(1)}, u32[]{:S(2)}, u32[]{:S(2)}) %collective-permute-start.7) | collective-permute-done | bytes 278560 | tf_op jit(solution)/shard_map/ppermute | solution.py:381
  30.6 0.3 shard_map.73
  31.0 0.1 collective-permute-start.10
  31.0 0.5 collective-permute-start.2
  31.5 0.1 collective-permute-start.3
  31.6 1.3 %collective-permute-start.9 = (s16[4,272,128]{2,1,0:T(8,128)(2,1)S(1)}, s16[4,272,128]{2,1,0:T(8,128)(2,1)S(1)}, u32[]{:S(2)}, u32[]{:S(2)}) collective-permute-start(s16[4,272,128]{2,1,0:T(8,128)(2,1)S(1)} %get-tuple-element.32.refs_2_), channel_id=1, source_target_pairs={{1,0},{9,8},{17,16},{25,24}} | collective-permute-start | bytes 835592 | tf_op jit(solution)/shard_map/ppermute | solution.py:381
  32.9 0.8 %collective-permute-done.10.refs_1_ = f32[2,2,512,128]{3,2,1,0:T(8,128)S(1)} collective-permute-done((f32[2,2,512,128]{3,2,1,0:T(8,128)S(1)}, f32[2,2,512,128]{3,2,1,0:T(8,128)S(1)}, u32[]{:S(2)}, u32[]{:S(2)}) %collective-permute-start.10) | collective-permute-done | bytes 1048608 | tf_op jit(solution)/shard_map/ppermute | solution.py:288
  33.7 0.3 shard_map.76
  33.9 2.3 %collective-permute-start.11 = (s16[2,528,128]{2,1,0:T(8,128)(2,1)S(1)}, s16[2,528,128]{2,1,0:T(8,128)(2,1)S(1)}, u32[]{:S(2)}, u32[]{:S(2)}) collective-permute-start(s16[2,528,128]{2,1,0:T(8,128)(2,1)S(1)} %get-tuple-element.36), channel_id=1, source_target_pairs={{0,16},{8,24},{16,0},{24,8},{1,17},{9,25},{17,1},{25,9},{2,18},{10... | collective-permute-start | bytes 811016 | tf_op jit(solution)/shard_map/ppermute | solution.py:288
  36.3 4.7 %collective-permute-start.8 = (bf16[2,256,128]{2,1,0:T(8,128)(2,1)S(1)}, bf16[2,256,128]{2,1,0:T(8,128)(2,1)S(1)}, u32[]{:S(2)}, u32[]{:S(2)}) collective-permute-start(bf16[2,256,128]{2,1,0:T(8,128)(2,1)S(1)} %shard_map.74.refs_0_), channel_id=1, source_target_pairs={{0,1},{2,3},{4,5},{6,7},{8,9},{10,11},{12,13},{14,15},{16,17},{18,... | collective-permute-start | bytes 393224 | tf_op jit(solution)/shard_map/ppermute | solution.py:382
  41.0 2.8 %collective-permute-done.8.refs_1_ = bf16[2,256,128]{2,1,0:T(8,128)(2,1)S(1)} collective-permute-done((bf16[2,256,128]{2,1,0:T(8,128)(2,1)S(1)}, bf16[2,256,128]{2,1,0:T(8,128)(2,1)S(1)}, u32[]{:S(2)}, u32[]{:S(2)}) %collective-permute-start.8) | collective-permute-done | bytes 131104 | tf_op jit(solution)/shard_map/ppermute | solution.py:382
  43.8 0.0 collective-permute-done.2.refs_6_
  43.8 0.0 collective-permute-done.9.refs_11_
  43.8 0.0 collective-permute-done.3.refs_8_
  43.8 0.0 collective-permute-done.11.refs_12_.refs_1_
  43.9 0.0 copy-done
  43.9 2.0 %shard_map.77 = (f32[2,2,512,128]{3,2,1,0:T(8,128)S(1)}, f32[2,2,512,128]{3,2,1,0:T(8,128)S(1)}) custom-call(bf16[36,256,256]{2,1,0:T(8,128)(2,1)S(1)} %get-tuple-element.23.refs_1_.refs_0_, s32[185]{0:T(256)S(1)} %get-tuple-element.24.refs_2_.refs_1_, s32[16]{0:T(128)S(1)} %maximum_convert_fusion.refs_3_.refs_2_, s32[8]{0:T(128)S(1)} %bitcast.9, ...), custom_call_target="tpu_custom_call" | custom-call | bytes 11027268 | tf_op jit(solution)/shard_map/pallas_call | solution.py:31
  45.8 0.1 collective-permute-start.12
  45.9 0.2 shard_map.78
  46.1 1.3 %collective-permute-start.14 = (s16[1,528,128]{2,1,0:T(8,128)(2,1)S(1)}, s16[1,528,128]{2,1,0:T(8,128)(2,1)S(1)}, u32[]{:S(2)}, u32[]{:S(2)}) collective-permute-start(s16[1,528,128]{2,1,0:T(8,128)(2,1)S(1)} %get-tuple-element.43), channel_id=1, source_target_pairs={{1,3},{2,0},{3,5},{4,2},{5,7},{6,4},{9,11},{10,8},{11,13},{12,10},... | collective-permute-start | bytes 405512 | tf_op jit(solution)/shard_map/ppermute | solution.py:416
  47.4 1.1 %collective-permute-done.12.refs_1_ = f32[2,2,512,128]{3,2,1,0:T(8,128)S(1)} collective-permute-done((f32[2,2,512,128]{3,2,1,0:T(8,128)S(1)}, f32[2,2,512,128]{3,2,1,0:T(8,128)S(1)}, u32[]{:S(2)}, u32[]{:S(2)}) %collective-permute-start.12) | collective-permute-done | bytes 1048608 | tf_op jit(solution)/shard_map/ppermute | solution.py:288
  48.6 0.2 shard_map.79
  48.8 0.9 %collective-permute-start.13 = (s16[2,528,128]{2,1,0:T(8,128)(2,1)S(1)}, s16[2,528,128]{2,1,0:T(8,128)(2,1)S(1)}, u32[]{:S(2)}, u32[]{:S(2)}) collective-permute-start(s16[2,528,128]{2,1,0:T(8,128)(2,1)S(1)} %get-tuple-element.42), channel_id=1, source_target_pairs={{0,16},{8,24},{16,0},{24,8},{1,17},{9,25},{17,1},{25,9},{2,18},{10... | collective-permute-start | bytes 811016 | tf_op jit(solution)/shard_map/ppermute | solution.py:288
  49.8 4.2 %collective-permute-done.14.refs_1_ = s16[1,528,128]{2,1,0:T(8,128)(2,1)S(1)} collective-permute-done((s16[1,528,128]{2,1,0:T(8,128)(2,1)S(1)}, s16[1,528,128]{2,1,0:T(8,128)(2,1)S(1)}, u32[]{:S(2)}, u32[]{:S(2)}) %collective-permute-start.14) | collective-permute-done | bytes 135200 | tf_op jit(solution)/shard_map/ppermute | solution.py:416
  54.0 0.1 shard_map.80
  54.1 0.5 collective-permute-start.15
  54.7 4.7 %collective-permute-done.15.refs_2_ = s16[1,528,128]{2,1,0:T(8,128)(2,1)S(1)} collective-permute-done((s16[1,528,128]{2,1,0:T(8,128)(2,1)S(1)}, s16[1,528,128]{2,1,0:T(8,128)(2,1)S(1)}, u32[]{:S(2)}, u32[]{:S(2)}) %collective-permute-start.15) | collective-permute-done | bytes 135200 | tf_op jit(solution)/shard_map/ppermute | solution.py:418
  59.4 0.0 collective-permute-done.13.refs_1_
  59.4 0.8 %shard_map.81 = (bf16[1,512,128]{2,1,0:T(8,128)(2,1)}, bf16[1,512,128]{2,1,0:T(8,128)(2,1)}) custom-call(f32[2,1,512,128]{3,2,1,0:T(8,128)S(1)} %get-tuple-element.41.refs_0_, s16[2,528,128]{2,1,0:T(8,128)(2,1)S(1)} %collective-permute-done.13.refs_1_, s16[1,528,128]{2,1,0:T(8,128)(2,1)S(1)} %collective-permute-done.15.refs_2_), custom_call_target="tpu_custom_call" | custom-call | bytes 1191936 | tf_op jit(solution)/shard_map/pallas_call | solution.py:31
  (6 shorter events, 0.1 us)
Async XLA Ops:
  2.3 13.0 %collective-permute-start = (bf16[1152,128]{1,0:T(8,128)(2,1)S(1)}, bf16[1152,128]{1,0:T(8,128)(2,1)S(1)}, u32[]{:S(2)}, u32[]{:S(2)}) collective-permute-start(bf16[1152,128]{1,0:T(8,128)(2,1)S(1)} %fusion.1), channel_id=1, source_target_pairs={{0,1},{1,0},{2,3},{3,2},{4,5},{5,4},{6,7},{7,6},{8,9},{9,8},{10,11... | collective-permute-start | bytes 884744 | tf_op jit(solution)/shard_map/ppermute | solution.py:324
  8.5 11.2 %collective-permute-start.5 = (s16[4,272,128]{2,1,0:T(8,128)(2,1)S(1)}, s16[4,272,128]{2,1,0:T(8,128)(2,1)S(1)}, u32[]{:S(2)}, u32[]{:S(2)}) collective-permute-start(s16[4,272,128]{2,1,0:T(8,128)(2,1)S(1)} %get-tuple-element.28), channel_id=1, source_target_pairs={{2,0},{3,1},{6,4},{7,5},{10,8},{11,9},{14,12},{15,13},{18,16},{19,... | collective-permute-start | bytes 835592 | tf_op jit(solution)/shard_map/ppermute | solution.py:381
  9.8 11.5 %collective-permute-start.4 = (bf16[2,256,128]{2,1,0:T(8,128)(2,1)S(1)}, bf16[2,256,128]{2,1,0:T(8,128)(2,1)S(1)}, u32[]{:S(2)}, u32[]{:S(2)}) collective-permute-start(bf16[2,256,128]{2,1,0:T(8,128)(2,1)S(1)} %get-tuple-element.26.refs_0_), channel_id=1, source_target_pairs={{0,4},{8,12},{16,20},{24,28}} | collective-permute-start | bytes 393224 | tf_op jit(solution)/shard_map/ppermute | solution.py:382
  15.3 10.2 %collective-permute-start.1 = (bf16[1152,128]{1,0:T(8,128)(2,1)S(1)}, bf16[1152,128]{1,0:T(8,128)(2,1)S(1)}, u32[]{:S(2)}, u32[]{:S(2)}) collective-permute-start(bf16[1152,128]{1,0:T(8,128)(2,1)S(1)} %collective-permute-done.refs_2_.refs_5_), channel_id=1, source_target_pairs={{3,1},{0,2},{5,3},{2,4},{7,5},{4,6},{11,9},{8,10},{13,11},{10,12},... | collective-permute-start | bytes 884744 | tf_op jit(solution)/shard_map/ppermute | solution.py:325
  20.0 10.6 %collective-permute-start.7 = (s16[4,272,128]{2,1,0:T(8,128)(2,1)S(1)}, s16[4,272,128]{2,1,0:T(8,128)(2,1)S(1)}, u32[]{:S(2)}, u32[]{:S(2)}) collective-permute-start(s16[4,272,128]{2,1,0:T(8,128)(2,1)S(1)} %get-tuple-element.29.refs_2_.refs_4_), channel_id=1, source_target_pairs={{4,0},{5,1},{12,8},{13,9},{20,16},{21,17},{28,24},{29,25}} | collective-permute-start | bytes 835592 | tf_op jit(solution)/shard_map/ppermute | solution.py:381
  21.4 5.5 %collective-permute-start.6 = (bf16[2,256,128]{2,1,0:T(8,128)(2,1)S(1)}, bf16[2,256,128]{2,1,0:T(8,128)(2,1)S(1)}, u32[]{:S(2)}, u32[]{:S(2)}) collective-permute-start(bf16[2,256,128]{2,1,0:T(8,128)(2,1)S(1)} %shard_map.71.refs_0_), channel_id=1, source_target_pairs={{0,2},{4,6},{8,10},{12,14},{16,18},{20,22},{24,26},{28,30}} | collective-permute-start | bytes 393224 | tf_op jit(solution)/shard_map/ppermute | solution.py:382
  28.7 15.2 %copy-start = (s32[1,1,8]{2,1,0:T(1,128)S(1)}, s32[1,1,8]{2,1,0:T(1,128)}, u32[]{:S(2)}) copy-start(s32[1,1,8]{2,1,0:T(1,128)} %refs_2_.1) | copy-start | bytes 100
  31.0 2.7 %collective-permute-start.10 = (f32[2,2,512,128]{3,2,1,0:T(8,128)S(1)}, f32[2,2,512,128]{3,2,1,0:T(8,128)S(1)}, u32[]{:S(2)}, u32[]{:S(2)}) collective-permute-start(f32[2,2,512,128]{3,2,1,0:T(8,128)S(1)} %get-tuple-element.35), channel_id=1, source_target_pairs={{0,8},{8,0},{16,24},{24,16},{1,9},{9,1},{17,25},{25,17},{2,10},{10... | collective-permute-start | bytes 3145736 | tf_op jit(solution)/shard_map/ppermute | solution.py:288
  31.0 12.8 %collective-permute-start.2 = (bf16[1152,128]{1,0:T(8,128)(2,1)S(1)}, bf16[1152,128]{1,0:T(8,128)(2,1)S(1)}, u32[]{:S(2)}, u32[]{:S(2)}) collective-permute-start(bf16[1152,128]{1,0:T(8,128)(2,1)S(1)} %collective-permute-done.refs_2_.refs_5_), channel_id=1, source_target_pairs={{0,8},{8,0},{16,24},{24,16},{1,9},{9,1},{17,25},{25,17},{2,10},{10... | collective-permute-start | bytes 884744 | tf_op jit(solution)/shard_map/ppermute | solution.py:326
  31.5 12.3 %collective-permute-start.3 = (bf16[1152,128]{1,0:T(8,128)(2,1)S(1)}, bf16[1152,128]{1,0:T(8,128)(2,1)S(1)}, u32[]{:S(2)}, u32[]{:S(2)}) collective-permute-start(bf16[1152,128]{1,0:T(8,128)(2,1)S(1)} %collective-permute-done.1.refs_7_), channel_id=1, source_target_pairs={{0,8},{8,0},{16,24},{24,16},{1,9},{9,1},{17,25},{25,17},{2,10},{10... | collective-permute-start | bytes 884744 | tf_op jit(solution)/shard_map/ppermute | solution.py:327
  31.6 12.2 %collective-permute-start.9 = (s16[4,272,128]{2,1,0:T(8,128)(2,1)S(1)}, s16[4,272,128]{2,1,0:T(8,128)(2,1)S(1)}, u32[]{:S(2)}, u32[]{:S(2)}) collective-permute-start(s16[4,272,128]{2,1,0:T(8,128)(2,1)S(1)} %get-tuple-element.32.refs_2_), channel_id=1, source_target_pairs={{1,0},{9,8},{17,16},{25,24}} | collective-permute-start | bytes 835592 | tf_op jit(solution)/shard_map/ppermute | solution.py:381
  33.9 9.9 %collective-permute-start.11 = (s16[2,528,128]{2,1,0:T(8,128)(2,1)S(1)}, s16[2,528,128]{2,1,0:T(8,128)(2,1)S(1)}, u32[]{:S(2)}, u32[]{:S(2)}) collective-permute-start(s16[2,528,128]{2,1,0:T(8,128)(2,1)S(1)} %get-tuple-element.36), channel_id=1, source_target_pairs={{0,16},{8,24},{16,0},{24,8},{1,17},{9,25},{17,1},{25,9},{2,18},{10... | collective-permute-start | bytes 811016 | tf_op jit(solution)/shard_map/ppermute | solution.py:288
  36.3 7.5 %collective-permute-start.8 = (bf16[2,256,128]{2,1,0:T(8,128)(2,1)S(1)}, bf16[2,256,128]{2,1,0:T(8,128)(2,1)S(1)}, u32[]{:S(2)}, u32[]{:S(2)}) collective-permute-start(bf16[2,256,128]{2,1,0:T(8,128)(2,1)S(1)} %shard_map.74.refs_0_), channel_id=1, source_target_pairs={{0,1},{2,3},{4,5},{6,7},{8,9},{10,11},{12,13},{14,15},{16,17},{18,... | collective-permute-start | bytes 393224 | tf_op jit(solution)/shard_map/ppermute | solution.py:382
  45.8 2.7 %collective-permute-start.12 = (f32[2,2,512,128]{3,2,1,0:T(8,128)S(1)}, f32[2,2,512,128]{3,2,1,0:T(8,128)S(1)}, u32[]{:S(2)}, u32[]{:S(2)}) collective-permute-start(f32[2,2,512,128]{3,2,1,0:T(8,128)S(1)} %get-tuple-element.38), channel_id=1, source_target_pairs={{0,8},{8,0},{16,24},{24,16},{1,9},{9,1},{17,25},{25,17},{2,10},{10... | collective-permute-start | bytes 3145736 | tf_op jit(solution)/shard_map/ppermute | solution.py:288
  46.1 7.9 %collective-permute-start.14 = (s16[1,528,128]{2,1,0:T(8,128)(2,1)S(1)}, s16[1,528,128]{2,1,0:T(8,128)(2,1)S(1)}, u32[]{:S(2)}, u32[]{:S(2)}) collective-permute-start(s16[1,528,128]{2,1,0:T(8,128)(2,1)S(1)} %get-tuple-element.43), channel_id=1, source_target_pairs={{1,3},{2,0},{3,5},{4,2},{5,7},{6,4},{9,11},{10,8},{11,13},{12,10},... | collective-permute-start | bytes 405512 | tf_op jit(solution)/shard_map/ppermute | solution.py:416
  48.8 10.6 %collective-permute-start.13 = (s16[2,528,128]{2,1,0:T(8,128)(2,1)S(1)}, s16[2,528,128]{2,1,0:T(8,128)(2,1)S(1)}, u32[]{:S(2)}, u32[]{:S(2)}) collective-permute-start(s16[2,528,128]{2,1,0:T(8,128)(2,1)S(1)} %get-tuple-element.42), channel_id=1, source_target_pairs={{0,16},{8,24},{16,0},{24,8},{1,17},{9,25},{17,1},{25,9},{2,18},{10... | collective-permute-start | bytes 811016 | tf_op jit(solution)/shard_map/ppermute | solution.py:288
  54.1 5.3 %collective-permute-start.15 = (s16[1,528,128]{2,1,0:T(8,128)(2,1)S(1)}, s16[1,528,128]{2,1,0:T(8,128)(2,1)S(1)}, u32[]{:S(2)}, u32[]{:S(2)}) collective-permute-start(s16[1,528,128]{2,1,0:T(8,128)(2,1)S(1)} %shard_map.80), channel_id=1, source_target_pairs={{0,1},{1,0},{2,3},{3,2},{4,5},{5,4},{6,7},{7,6},{8,9},{9,8},{10,11... | collective-permute-start | bytes 405512 | tf_op jit(solution)/shard_map/ppermute | solution.py:418

commit v6 on v5

--- a/solution.py
+++ b/solution.py
@@ -381,13 +381,13 @@
         came = lax.ppermute(coded, "band", [(i, i - bit) for i in senders])
         got = lax.ppermute(xh, "band", [(i, i + step) for i in range(0, bands, 2 * step)])
         if at == 1:
-            halo_send, halo_keep = halo_out(after=(coded, got))
+            halo_send, halo_keep = halo_out(after=(coded,))
         if bit != order[-1]:
             coded, heads, *passed = call(
                 heads_add_kernel,
                 (coded_heads, plain_heads),
                 (heads, came),
-                after=fences[at],
+                after=(*fences[at], got) if at == 1 else fences[at],
                 through=(halo_send,) if at == 1 else (),
             )
             halo_send = passed[0] if passed else halo_send

time: 60.3 us -> 60.3 us (level)
  waiting for transfers between devices: 19.7 us -> 18.9 us
  Pallas kernels: 12.4 us -> 13.2 us
    ppermute x3, waiting for transfers between devices: 1.96 us -> 4.53 us  [on_device(): came = lax.ppermute(coded, 'band', [(i, i - bit) for i in senders])]
    ppermute x3, waiting for transfers between devices: 4.06 us -> 2.76 us  [on_device(): lax.ppermute(xh, 'band', [(i, i + step) for i in range(0, bands, 2 * step)])]
    ppermute x1, waiting for transfers between devices: 2.76 us -> 1.5 us  [on_device(): other_x = lax.ppermute(pair_x, 'band', inward)]
    ppermute x4, starting transfers between devices: 3.39 us -> 2.35 us  [over_levels(): came = lax.ppermute(send, 'level', pairs)]
    ppermute x3, starting transfers between devices: 11.5 us -> 12.2 us  [on_device(): lax.ppermute(xh, 'band', [(i, i + step) for i in range(0, bands, 2 * step)])]
    pallas_call x14, Pallas kernels: 12.4 us -> 13.2 us  [call(): pl.pallas_call(body, out_shape=[*outs, *(array(a.shape, a.dtype) for a in...]
  transfers between devices with their start and end apart: 16 -> 16, of which waited for: 8 -> 7; matrix products, arithmetic and copies ran while one was open for 0% -> 0% of each run, Pallas kernels for 15% -> 17%
where the time goes in v6:
time: 60.3 us; the launch traced here: 60.2 us
  starting transfers between devices  25.5 us (42%)
  waiting for transfers between devices  18.9 us (31%)
  Pallas kernels  13.2 us (22%)
  local copies, waits for them, and re-layouts  0.98 us (2%)
  between operations  0.89 us (1%)
  other arithmetic  0.76 us (1%)
    pallas_call x14, Pallas kernels, call(): pl.pallas_call(body, out_shape=[*outs, *(array(a.shape, a.dtype) for a in...  13.2 us
    ppermute x3, starting transfers between devices, on_device(): lax.ppermute(xh, 'band', [(i, i + step) for i in range(0, bands, 2 * step)])  12.2 us
    ppermute x3, waiting for transfers between devices, on_device(): came = lax.ppermute(coded, 'band', [(i, i - bit) for i in senders])  4.53 us
    ppermute x1, waiting for transfers between devices, on_device(): from_near = lax.ppermute(to_pair, 'band', pairs)  4.39 us
    ppermute x3, starting transfers between devices, on_device(): came = lax.ppermute(coded, 'band', [(i, i - bit) for i in senders])  3.86 us
    ppermute x1, waiting for transfers between devices, on_device(): relayed = lax.ppermute(relayed, 'band', outward)  3.79 us
    ppermute x1, starting transfers between devices, on_device(): pair_x = lax.ppermute(mine, 'band', pairs)  3.03 us
    ppermute x3, waiting for transfers between devices, on_device(): lax.ppermute(xh, 'band', [(i, i + step) for i in range(0, bands, 2 * step)])  2.76 us
  transfers between devices with their start and end apart: 16, of which 7 were waited for; matrix products, arithmetic and copies ran while one was open for 0% of the time, Pallas kernels for 17%

profile of v6, /device:TPU:0, one launch (start us, length us, event | category | flops | bytes accessed | tf_op | source)
XLA Modules:
  0.0 60.2 jit_solution(7575133176984805731)
XLA Ops:
  0.6 0.7 %convert_bitcast_fusion = bf16[1,8]{1,0:T(2,128)(2,1)S(1)} fusion(s32[1,1,8]{2,1,0:T(1,128)} %refs_2_.1), kind=kLoop, calls=%fused_computation.6 | loop fusion | flops 8 | bytes 48 | tf_op jit(solution)/shard_map/convert_element_type | solution.py:322
  1.3 1.0 %constant_dynamic-slice_fusion = bf16[1024,128]{1,0:T(8,128)(2,1)S(1)} fusion(bf16[2048,128]{1,0:T(8,128)(2,1)} %param.5, s32[]{:T(128)S(6)} %select_n.3), kind=kLoop, calls=%fused_computation.7 | loop fusion | bytes 524292 | tf_op jit(solution)/shard_map/dynamic_slice | solution.py:321
  2.3 3.0 %collective-permute-start = (bf16[1152,128]{1,0:T(8,128)(2,1)S(1)}, bf16[1152,128]{1,0:T(8,128)(2,1)S(1)}, u32[]{:S(2)}, u32[]{:S(2)}) collective-permute-start(bf16[1152,128]{1,0:T(8,128)(2,1)S(1)} %fusion.1), channel_id=1, source_target_pairs={{0,1},{1,0},{2,3},{3,2},{4,5},{5,4},{6,7},{7,6},{8,9},{9,8},{10,11... | collective-permute-start | bytes 884744 | tf_op jit(solution)/shard_map/ppermute | solution.py:324
  5.3 3.2 %shard_map.68 = (s32[185]{0:T(256)S(1)}, s16[4,272,128]{2,1,0:T(8,128)(2,1)S(1)}, f32[4,256,128]{2,1,0:T(8,128)S(1)}, bf16[2,256,128]{2,1,0:T(8,128)(2,1)S(1)}, ...) custom-call(s32[1,36]{1,0:T(1,128)} %refs_0_.1, s32[1,36]{1,0:T(1,128)} %refs_1_.1, ...), custom_call_target="tpu_custom_call" | custom-call | bytes 11420708 | tf_op jit(solution)/shard_map/pallas_call | solution.py:31
  8.5 1.3 %collective-permute-start.5 = (s16[4,272,128]{2,1,0:T(8,128)(2,1)S(1)}, s16[4,272,128]{2,1,0:T(8,128)(2,1)S(1)}, u32[]{:S(2)}, u32[]{:S(2)}) collective-permute-start(s16[4,272,128]{2,1,0:T(8,128)(2,1)S(1)} %get-tuple-element.28), channel_id=1, source_target_pairs={{2,0},{3,1},{6,4},{7,5},{10,8},{11,9},{14,12},{15,13},{18,16},{19,... | collective-permute-start | bytes 835592 | tf_op jit(solution)/shard_map/ppermute | solution.py:381
  9.8 5.5 %collective-permute-start.4 = (bf16[2,256,128]{2,1,0:T(8,128)(2,1)S(1)}, bf16[2,256,128]{2,1,0:T(8,128)(2,1)S(1)}, u32[]{:S(2)}, u32[]{:S(2)}) collective-permute-start(bf16[2,256,128]{2,1,0:T(8,128)(2,1)S(1)} %get-tuple-element.26.refs_0_), channel_id=1, source_target_pairs={{0,4},{8,12},{16,20},{24,28}} | collective-permute-start | bytes 393224 | tf_op jit(solution)/shard_map/ppermute | solution.py:382
  15.3 0.0 collective-permute-done.refs_2_.refs_5_
  15.3 1.3 %collective-permute-start.1 = (bf16[1152,128]{1,0:T(8,128)(2,1)S(1)}, bf16[1152,128]{1,0:T(8,128)(2,1)S(1)}, u32[]{:S(2)}, u32[]{:S(2)}) collective-permute-start(bf16[1152,128]{1,0:T(8,128)(2,1)S(1)} %collective-permute-done.refs_2_.refs_5_), channel_id=1, source_target_pairs={{3,1},{0,2},{5,3},{2,4},{7,5},{4,6},{11,9},{8,10},{13,11},{10,12},... | collective-permute-start | bytes 884744 | tf_op jit(solution)/shard_map/ppermute | solution.py:325
  16.6 3.8 %shard_map.69.refs_2_.refs_4_ = f32[16,256,128]{2,1,0:T(8,128)S(1)} custom-call(bf16[8,256,128]{2,1,0:T(8,128)(2,1)S(1)} %get-tuple-element.25.refs_0_, bf16[36,256,256]{2,1,0:T(8,128)(2,1)S(1)} %get-tuple-element.23.refs_1_.refs_0_, s32[185]{0:T(256)S(1)} %get-tuple-element.24.refs_2_.refs_1_), custom_call_target="tpu_custom_call" | custom-call | bytes 7340772 | tf_op jit(solution)/shard_map/pallas_call | solution.py:31
  20.4 0.0 collective-permute-done.5.refs_1_
  20.4 0.3 shard_map.70
  20.7 1.3 %collective-permute-start.7 = (s16[4,272,128]{2,1,0:T(8,128)(2,1)S(1)}, s16[4,272,128]{2,1,0:T(8,128)(2,1)S(1)}, u32[]{:S(2)}, u32[]{:S(2)}) collective-permute-start(s16[4,272,128]{2,1,0:T(8,128)(2,1)S(1)} %get-tuple-element.29.refs_2_.refs_4_), channel_id=1, source_target_pairs={{4,0},{5,1},{12,8},{13,9},{20,16},{21,17},{28,24},{29,25}} | collective-permute-start | bytes 835592 | tf_op jit(solution)/shard_map/ppermute | solution.py:381
  22.0 0.0 collective-permute-done.4.refs_1_
  22.1 1.3 %collective-permute-start.6 = (bf16[2,256,128]{2,1,0:T(8,128)(2,1)S(1)}, bf16[2,256,128]{2,1,0:T(8,128)(2,1)S(1)}, u32[]{:S(2)}, u32[]{:S(2)}) collective-permute-start(bf16[2,256,128]{2,1,0:T(8,128)(2,1)S(1)} %shard_map.71.refs_0_), channel_id=1, source_target_pairs={{0,2},{4,6},{8,10},{12,14},{16,18},{20,22},{24,26},{28,30}} | collective-permute-start | bytes 393224 | tf_op jit(solution)/shard_map/ppermute | solution.py:382
  23.4 1.5 %collective-permute-done.1.refs_7_ = bf16[1152,128]{1,0:T(8,128)(2,1)S(1)} collective-permute-done((bf16[1152,128]{1,0:T(8,128)(2,1)S(1)}, bf16[1152,128]{1,0:T(8,128)(2,1)S(1)}, u32[]{:S(2)}, u32[]{:S(2)}) %collective-permute-start.1) | collective-permute-done | bytes 294944 | tf_op jit(solution)/shard_map/ppermute | solution.py:325
  24.9 0.1 maximum_convert_fusion.refs_3_.refs_2_
  25.0 1.8 %shard_map.72 = (f32[2,2,512,128]{3,2,1,0:T(8,128)S(1)}, f32[2,2,512,128]{3,2,1,0:T(8,128)S(1)}) custom-call(bf16[8,256,128]{2,1,0:T(8,128)(2,1)S(1)} %get-tuple-element.25.refs_0_, bf16[36,256,256]{2,1,0:T(8,128)(2,1)S(1)} %get-tuple-element.23.refs_1_.refs_0_, s32[185]{0:T(256)S(1)} %get-tuple-element.24.refs_2_.refs_1_, ...), custom_call_target="tpu_custom_call" | custom-call | bytes 7340836 | tf_op jit(solution)/shard_map/pallas_call | solution.py:31
  26.8 0.0 copy-start
  26.8 0.0 collective-permute-done.6.refs_3_.refs_1_
  26.9 4.5 %collective-permute-done.7.refs_1_ = s16[4,272,128]{2,1,0:T(8,128)(2,1)S(1)} collective-permute-done((s16[4,272,128]{2,1,0:T(8,128)(2,1)S(1)}, s16[4,272,128]{2,1,0:T(8,128)(2,1)S(1)}, u32[]{:S(2)}, u32[]{:S(2)}) %collective-permute-start.7) | collective-permute-done | bytes 278560 | tf_op jit(solution)/shard_map/ppermute | solution.py:381
  31.4 0.3 shard_map.73
  31.7 0.1 collective-permute-start.10
  31.8 0.5 collective-permute-start.2
  32.3 0.1 collective-permute-start.3
  32.4 1.3 %collective-permute-start.9 = (s16[4,272,128]{2,1,0:T(8,128)(2,1)S(1)}, s16[4,272,128]{2,1,0:T(8,128)(2,1)S(1)}, u32[]{:S(2)}, u32[]{:S(2)}) collective-permute-start(s16[4,272,128]{2,1,0:T(8,128)(2,1)S(1)} %get-tuple-element.32.refs_2_), channel_id=1, source_target_pairs={{1,0},{9,8},{17,16},{25,24}} | collective-permute-start | bytes 835592 | tf_op jit(solution)/shard_map/ppermute | solution.py:381
  33.6 0.8 %collective-permute-done.10.refs_1_ = f32[2,2,512,128]{3,2,1,0:T(8,128)S(1)} collective-permute-done((f32[2,2,512,128]{3,2,1,0:T(8,128)S(1)}, f32[2,2,512,128]{3,2,1,0:T(8,128)S(1)}, u32[]{:S(2)}, u32[]{:S(2)}) %collective-permute-start.10) | collective-permute-done | bytes 1048608 | tf_op jit(solution)/shard_map/ppermute | solution.py:288
  34.4 0.3 shard_map.76
  34.7 0.8 %collective-permute-start.11 = (s16[2,528,128]{2,1,0:T(8,128)(2,1)S(1)}, s16[2,528,128]{2,1,0:T(8,128)(2,1)S(1)}, u32[]{:S(2)}, u32[]{:S(2)}) collective-permute-start(s16[2,528,128]{2,1,0:T(8,128)(2,1)S(1)} %get-tuple-element.36), channel_id=1, source_target_pairs={{0,16},{8,24},{16,0},{24,8},{1,17},{9,25},{17,1},{25,9},{2,18},{10... | collective-permute-start | bytes 811016 | tf_op jit(solution)/shard_map/ppermute | solution.py:288
  35.5 5.5 %collective-permute-start.8 = (bf16[2,256,128]{2,1,0:T(8,128)(2,1)S(1)}, bf16[2,256,128]{2,1,0:T(8,128)(2,1)S(1)}, u32[]{:S(2)}, u32[]{:S(2)}) collective-permute-start(bf16[2,256,128]{2,1,0:T(8,128)(2,1)S(1)} %shard_map.74.refs_0_), channel_id=1, source_target_pairs={{0,1},{2,3},{4,5},{6,7},{8,9},{10,11},{12,13},{14,15},{16,17},{18,... | collective-permute-start | bytes 393224 | tf_op jit(solution)/shard_map/ppermute | solution.py:382
  41.0 2.8 %collective-permute-done.8.refs_1_ = bf16[2,256,128]{2,1,0:T(8,128)(2,1)S(1)} collective-permute-done((bf16[2,256,128]{2,1,0:T(8,128)(2,1)S(1)}, bf16[2,256,128]{2,1,0:T(8,128)(2,1)S(1)}, u32[]{:S(2)}, u32[]{:S(2)}) %collective-permute-start.8) | collective-permute-done | bytes 131104 | tf_op jit(solution)/shard_map/ppermute | solution.py:382
  43.8 0.0 collective-permute-done.2.refs_6_
  43.8 0.0 collective-permute-done.9.refs_11_
  43.8 0.0 collective-permute-done.3.refs_8_
  43.9 0.0 collective-permute-done.11.refs_12_.refs_1_
  43.9 0.0 copy-done
  43.9 2.0 %shard_map.77 = (f32[2,2,512,128]{3,2,1,0:T(8,128)S(1)}, f32[2,2,512,128]{3,2,1,0:T(8,128)S(1)}) custom-call(bf16[36,256,256]{2,1,0:T(8,128)(2,1)S(1)} %get-tuple-element.23.refs_1_.refs_0_, s32[185]{0:T(256)S(1)} %get-tuple-element.24.refs_2_.refs_1_, s32[16]{0:T(128)S(1)} %maximum_convert_fusion.refs_3_.refs_2_, s32[8]{0:T(128)S(1)} %bitcast.9, ...), custom_call_target="tpu_custom_call" | custom-call | bytes 11027268 | tf_op jit(solution)/shard_map/pallas_call | solution.py:31
  45.9 0.1 collective-permute-start.12
  45.9 0.2 shard_map.78
  46.1 1.3 %collective-permute-start.14 = (s16[1,528,128]{2,1,0:T(8,128)(2,1)S(1)}, s16[1,528,128]{2,1,0:T(8,128)(2,1)S(1)}, u32[]{:S(2)}, u32[]{:S(2)}) collective-permute-start(s16[1,528,128]{2,1,0:T(8,128)(2,1)S(1)} %get-tuple-element.43), channel_id=1, source_target_pairs={{1,3},{2,0},{3,5},{4,2},{5,7},{6,4},{9,11},{10,8},{11,13},{12,10},... | collective-permute-start | bytes 405512 | tf_op jit(solution)/shard_map/ppermute | solution.py:416
  47.4 1.1 %collective-permute-done.12.refs_1_ = f32[2,2,512,128]{3,2,1,0:T(8,128)S(1)} collective-permute-done((f32[2,2,512,128]{3,2,1,0:T(8,128)S(1)}, f32[2,2,512,128]{3,2,1,0:T(8,128)S(1)}, u32[]{:S(2)}, u32[]{:S(2)}) %collective-permute-start.12) | collective-permute-done | bytes 1048608 | tf_op jit(solution)/shard_map/ppermute | solution.py:288
  48.6 0.2 shard_map.79
  48.8 1.4 %collective-permute-start.13 = (s16[2,528,128]{2,1,0:T(8,128)(2,1)S(1)}, s16[2,528,128]{2,1,0:T(8,128)(2,1)S(1)}, u32[]{:S(2)}, u32[]{:S(2)}) collective-permute-start(s16[2,528,128]{2,1,0:T(8,128)(2,1)S(1)} %get-tuple-element.42), channel_id=1, source_target_pairs={{0,16},{8,24},{16,0},{24,8},{1,17},{9,25},{17,1},{25,9},{2,18},{10... | collective-permute-start | bytes 811016 | tf_op jit(solution)/shard_map/ppermute | solution.py:288
  50.2 3.8 %collective-permute-done.14.refs_1_ = s16[1,528,128]{2,1,0:T(8,128)(2,1)S(1)} collective-permute-done((s16[1,528,128]{2,1,0:T(8,128)(2,1)S(1)}, s16[1,528,128]{2,1,0:T(8,128)(2,1)S(1)}, u32[]{:S(2)}, u32[]{:S(2)}) %collective-permute-start.14) | collective-permute-done | bytes 135200 | tf_op jit(solution)/shard_map/ppermute | solution.py:416
  54.0 0.1 shard_map.80
  54.1 0.9 %collective-permute-start.15 = (s16[1,528,128]{2,1,0:T(8,128)(2,1)S(1)}, s16[1,528,128]{2,1,0:T(8,128)(2,1)S(1)}, u32[]{:S(2)}, u32[]{:S(2)}) collective-permute-start(s16[1,528,128]{2,1,0:T(8,128)(2,1)S(1)} %shard_map.80), channel_id=1, source_target_pairs={{0,1},{1,0},{2,3},{3,2},{4,5},{5,4},{6,7},{7,6},{8,9},{9,8},{10,11... | collective-permute-start | bytes 405512 | tf_op jit(solution)/shard_map/ppermute | solution.py:418
  55.0 4.4 %collective-permute-done.15.refs_2_ = s16[1,528,128]{2,1,0:T(8,128)(2,1)S(1)} collective-permute-done((s16[1,528,128]{2,1,0:T(8,128)(2,1)S(1)}, s16[1,528,128]{2,1,0:T(8,128)(2,1)S(1)}, u32[]{:S(2)}, u32[]{:S(2)}) %collective-permute-start.15) | collective-permute-done | bytes 135200 | tf_op jit(solution)/shard_map/ppermute | solution.py:418
  59.4 0.0 collective-permute-done.13.refs_1_
  59.4 0.8 %shard_map.81 = (bf16[1,512,128]{2,1,0:T(8,128)(2,1)}, bf16[1,512,128]{2,1,0:T(8,128)(2,1)}) custom-call(f32[2,1,512,128]{3,2,1,0:T(8,128)S(1)} %get-tuple-element.41.refs_0_, s16[2,528,128]{2,1,0:T(8,128)(2,1)S(1)} %collective-permute-done.13.refs_1_, s16[1,528,128]{2,1,0:T(8,128)(2,1)S(1)} %collective-permute-done.15.refs_2_), custom_call_target="tpu_custom_call" | custom-call | bytes 1191936 | tf_op jit(solution)/shard_map/pallas_call | solution.py:31
  (6 shorter events, 0.1 us)
Async XLA Ops:
  2.3 13.0 %collective-permute-start = (bf16[1152,128]{1,0:T(8,128)(2,1)S(1)}, bf16[1152,128]{1,0:T(8,128)(2,1)S(1)}, u32[]{:S(2)}, u32[]{:S(2)}) collective-permute-start(bf16[1152,128]{1,0:T(8,128)(2,1)S(1)} %fusion.1), channel_id=1, source_target_pairs={{0,1},{1,0},{2,3},{3,2},{4,5},{5,4},{6,7},{7,6},{8,9},{9,8},{10,11... | collective-permute-start | bytes 884744 | tf_op jit(solution)/shard_map/ppermute | solution.py:324
  8.5 11.9 %collective-permute-start.5 = (s16[4,272,128]{2,1,0:T(8,128)(2,1)S(1)}, s16[4,272,128]{2,1,0:T(8,128)(2,1)S(1)}, u32[]{:S(2)}, u32[]{:S(2)}) collective-permute-start(s16[4,272,128]{2,1,0:T(8,128)(2,1)S(1)} %get-tuple-element.28), channel_id=1, source_target_pairs={{2,0},{3,1},{6,4},{7,5},{10,8},{11,9},{14,12},{15,13},{18,16},{19,... | collective-permute-start | bytes 835592 | tf_op jit(solution)/shard_map/ppermute | solution.py:381
  9.8 12.3 %collective-permute-start.4 = (bf16[2,256,128]{2,1,0:T(8,128)(2,1)S(1)}, bf16[2,256,128]{2,1,0:T(8,128)(2,1)S(1)}, u32[]{:S(2)}, u32[]{:S(2)}) collective-permute-start(bf16[2,256,128]{2,1,0:T(8,128)(2,1)S(1)} %get-tuple-element.26.refs_0_), channel_id=1, source_target_pairs={{0,4},{8,12},{16,20},{24,28}} | collective-permute-start | bytes 393224 | tf_op jit(solution)/shard_map/ppermute | solution.py:382
  15.3 9.7 %collective-permute-start.1 = (bf16[1152,128]{1,0:T(8,128)(2,1)S(1)}, bf16[1152,128]{1,0:T(8,128)(2,1)S(1)}, u32[]{:S(2)}, u32[]{:S(2)}) collective-permute-start(bf16[1152,128]{1,0:T(8,128)(2,1)S(1)} %collective-permute-done.refs_2_.refs_5_), channel_id=1, source_target_pairs={{3,1},{0,2},{5,3},{2,4},{7,5},{4,6},{11,9},{8,10},{13,11},{10,12},... | collective-permute-start | bytes 884744 | tf_op jit(solution)/shard_map/ppermute | solution.py:325
  20.7 10.6 %collective-permute-start.7 = (s16[4,272,128]{2,1,0:T(8,128)(2,1)S(1)}, s16[4,272,128]{2,1,0:T(8,128)(2,1)S(1)}, u32[]{:S(2)}, u32[]{:S(2)}) collective-permute-start(s16[4,272,128]{2,1,0:T(8,128)(2,1)S(1)} %get-tuple-element.29.refs_2_.refs_4_), channel_id=1, source_target_pairs={{4,0},{5,1},{12,8},{13,9},{20,16},{21,17},{28,24},{29,25}} | collective-permute-start | bytes 835592 | tf_op jit(solution)/shard_map/ppermute | solution.py:381
  22.1 4.7 %collective-permute-start.6 = (bf16[2,256,128]{2,1,0:T(8,128)(2,1)S(1)}, bf16[2,256,128]{2,1,0:T(8,128)(2,1)S(1)}, u32[]{:S(2)}, u32[]{:S(2)}) collective-permute-start(bf16[2,256,128]{2,1,0:T(8,128)(2,1)S(1)} %shard_map.71.refs_0_), channel_id=1, source_target_pairs={{0,2},{4,6},{8,10},{12,14},{16,18},{20,22},{24,26},{28,30}} | collective-permute-start | bytes 393224 | tf_op jit(solution)/shard_map/ppermute | solution.py:382
  26.8 17.0 %copy-start = (s32[1,1,8]{2,1,0:T(1,128)S(1)}, s32[1,1,8]{2,1,0:T(1,128)}, u32[]{:S(2)}) copy-start(s32[1,1,8]{2,1,0:T(1,128)} %refs_2_.1) | copy-start | bytes 100
  31.7 2.7 %collective-permute-start.10 = (f32[2,2,512,128]{3,2,1,0:T(8,128)S(1)}, f32[2,2,512,128]{3,2,1,0:T(8,128)S(1)}, u32[]{:S(2)}, u32[]{:S(2)}) collective-permute-start(f32[2,2,512,128]{3,2,1,0:T(8,128)S(1)} %get-tuple-element.35), channel_id=1, source_target_pairs={{0,8},{8,0},{16,24},{24,16},{1,9},{9,1},{17,25},{25,17},{2,10},{10... | collective-permute-start | bytes 3145736 | tf_op jit(solution)/shard_map/ppermute | solution.py:288
  31.8 12.0 %collective-permute-start.2 = (bf16[1152,128]{1,0:T(8,128)(2,1)S(1)}, bf16[1152,128]{1,0:T(8,128)(2,1)S(1)}, u32[]{:S(2)}, u32[]{:S(2)}) collective-permute-start(bf16[1152,128]{1,0:T(8,128)(2,1)S(1)} %collective-permute-done.refs_2_.refs_5_), channel_id=1, source_target_pairs={{0,8},{8,0},{16,24},{24,16},{1,9},{9,1},{17,25},{25,17},{2,10},{10... | collective-permute-start | bytes 884744 | tf_op jit(solution)/shard_map/ppermute | solution.py:326
  32.3 11.6 %collective-permute-start.3 = (bf16[1152,128]{1,0:T(8,128)(2,1)S(1)}, bf16[1152,128]{1,0:T(8,128)(2,1)S(1)}, u32[]{:S(2)}, u32[]{:S(2)}) collective-permute-start(bf16[1152,128]{1,0:T(8,128)(2,1)S(1)} %collective-permute-done.1.refs_7_), channel_id=1, source_target_pairs={{0,8},{8,0},{16,24},{24,16},{1,9},{9,1},{17,25},{25,17},{2,10},{10... | collective-permute-start | bytes 884744 | tf_op jit(solution)/shard_map/ppermute | solution.py:327
  32.4 11.5 %collective-permute-start.9 = (s16[4,272,128]{2,1,0:T(8,128)(2,1)S(1)}, s16[4,272,128]{2,1,0:T(8,128)(2,1)S(1)}, u32[]{:S(2)}, u32[]{:S(2)}) collective-permute-start(s16[4,272,128]{2,1,0:T(8,128)(2,1)S(1)} %get-tuple-element.32.refs_2_), channel_id=1, source_target_pairs={{1,0},{9,8},{17,16},{25,24}} | collective-permute-start | bytes 835592 | tf_op jit(solution)/shard_map/ppermute | solution.py:381
  34.7 9.2 %collective-permute-start.11 = (s16[2,528,128]{2,1,0:T(8,128)(2,1)S(1)}, s16[2,528,128]{2,1,0:T(8,128)(2,1)S(1)}, u32[]{:S(2)}, u32[]{:S(2)}) collective-permute-start(s16[2,528,128]{2,1,0:T(8,128)(2,1)S(1)} %get-tuple-element.36), channel_id=1, source_target_pairs={{0,16},{8,24},{16,0},{24,8},{1,17},{9,25},{17,1},{25,9},{2,18},{10... | collective-permute-start | bytes 811016 | tf_op jit(solution)/shard_map/ppermute | solution.py:288
  35.5 8.2 %collective-permute-start.8 = (bf16[2,256,128]{2,1,0:T(8,128)(2,1)S(1)}, bf16[2,256,128]{2,1,0:T(8,128)(2,1)S(1)}, u32[]{:S(2)}, u32[]{:S(2)}) collective-permute-start(bf16[2,256,128]{2,1,0:T(8,128)(2,1)S(1)} %shard_map.74.refs_0_), channel_id=1, source_target_pairs={{0,1},{2,3},{4,5},{6,7},{8,9},{10,11},{12,13},{14,15},{16,17},{18,... | collective-permute-start | bytes 393224 | tf_op jit(solution)/shard_map/ppermute | solution.py:382
  45.9 2.7 %collective-permute-start.12 = (f32[2,2,512,128]{3,2,1,0:T(8,128)S(1)}, f32[2,2,512,128]{3,2,1,0:T(8,128)S(1)}, u32[]{:S(2)}, u32[]{:S(2)}) collective-permute-start(f32[2,2,512,128]{3,2,1,0:T(8,128)S(1)} %get-tuple-element.38), channel_id=1, source_target_pairs={{0,8},{8,0},{16,24},{24,16},{1,9},{9,1},{17,25},{25,17},{2,10},{10... | collective-permute-start | bytes 3145736 | tf_op jit(solution)/shard_map/ppermute | solution.py:288
  46.1 7.9 %collective-permute-start.14 = (s16[1,528,128]{2,1,0:T(8,128)(2,1)S(1)}, s16[1,528,128]{2,1,0:T(8,128)(2,1)S(1)}, u32[]{:S(2)}, u32[]{:S(2)}) collective-permute-start(s16[1,528,128]{2,1,0:T(8,128)(2,1)S(1)} %get-tuple-element.43), channel_id=1, source_target_pairs={{1,3},{2,0},{3,5},{4,2},{5,7},{6,4},{9,11},{10,8},{11,13},{12,10},... | collective-permute-start | bytes 405512 | tf_op jit(solution)/shard_map/ppermute | solution.py:416
  48.8 10.6 %collective-permute-start.13 = (s16[2,528,128]{2,1,0:T(8,128)(2,1)S(1)}, s16[2,528,128]{2,1,0:T(8,128)(2,1)S(1)}, u32[]{:S(2)}, u32[]{:S(2)}) collective-permute-start(s16[2,528,128]{2,1,0:T(8,128)(2,1)S(1)} %get-tuple-element.42), channel_id=1, source_target_pairs={{0,16},{8,24},{16,0},{24,8},{1,17},{9,25},{17,1},{25,9},{2,18},{10... | collective-permute-start | bytes 811016 | tf_op jit(solution)/shard_map/ppermute | solution.py:288
  54.1 5.3 %collective-permute-start.15 = (s16[1,528,128]{2,1,0:T(8,128)(2,1)S(1)}, s16[1,528,128]{2,1,0:T(8,128)(2,1)S(1)}, u32[]{:S(2)}, u32[]{:S(2)}) collective-permute-start(s16[1,528,128]{2,1,0:T(8,128)(2,1)S(1)} %shard_map.80), channel_id=1, source_target_pairs={{0,1},{1,0},{2,3},{3,2},{4,5},{5,4},{6,7},{7,6},{8,9},{9,8},{10,11... | collective-permute-start | bytes 405512 | tf_op jit(solution)/shard_map/ppermute | solution.py:418
